TPU v7x, 256 devices: a whole 4x4x8 slice. The times are simulated.
256 devices in a mesh: replica: 16 (over z_hi, x), fsdp: 16 (over y, z_lo, core).
Axes of the slice: x: 4, y: 4, z: 8 (z_hi: 4, z_lo: 2; z = z_hi * 2 + z_lo), core: 2. Of those that a mesh axis runs over, the one named last changes fastest.
Arguments:
- outer_params: float32 [384, 3072], P('fsdp'), may hold values from -4 to 4
- outer_momentum: float32 [384, 3072], P('fsdp'), may hold values from -1.5 to 1.5
- inner_mean: float32 [16, 384, 3072], P('replica', 'fsdp')
- inner_square: float32 [16, 384, 3072], P('replica', 'fsdp'), as said below
- latents: bfloat16 [2, 131072, 64], P(None, ('replica', 'fsdp')), may hold values from -6 to 6
- noise_draw: bfloat16 [2, 131072, 64], P(None, ('replica', 'fsdp')), may hold values from -6 to 6
- timesteps: int32 [2, 131072], P(None, ('replica', 'fsdp')), may hold values from 0 to 999
- fragment: int32 [1], replicated, may hold values from 0 to 14
- modulation: float32 [15, 2, 3072], replicated, may hold values from -3 to 3
Outputs:
- new_params: float32 [384, 3072], P('fsdp')
- new_momentum: float32 [384, 3072], P('fsdp')
- new_mean: float32 [16, 384, 3072], P('replica', 'fsdp')
- new_square: float32 [16, 384, 3072], P('replica', 'fsdp')
Inputs may be any that keep to these rules, and one draw needn't show every extreme that they name: `inner_square`: positive.
All inputs are finite; a program needn't handle non-finite values.
Results may differ from a plain program's by a relative error of at most 0.034.
Values may be sent and summed in bfloat16 or wider, within the bound.
No kernel may reach another device: no remote copies, remote signals or barrier semaphores. Data moves between devices by JAX's collectives and lax.ppermute only.
A program may use at most 64 MiB of HBM per device.

v0:
```python
import math

import jax
import jax.numpy as jnp
from jax import lax
from jax.sharding import PartitionSpec as P

STEPS = 2
LEVELS = 1000


BETA_ONE = 0.9
BETA_TWO = 0.95
INNER_RATE = 0.2
DECAY_RATE = 0.1
ADAM_EPS = 1e-08
NORM_EPS = 1e-06
OUTER_RATE = 0.7
NESTEROV = 0.9


def embed_levels(levels, time_width):
    half_width = time_width // 2
    noise_level = (levels.astype(jnp.float32) + 0.5) / LEVELS
    frequencies = jnp.exp(
        -math.log(10000.0) * jnp.arange(half_width, dtype=jnp.float32) / half_width
    )
    angles = (1000.0 * noise_level)[:, None] * frequencies[None, :]
    return (jnp.concatenate([jnp.cos(angles), jnp.sin(angles)], axis=-1), noise_level)


def local_grads(weights, latent_rows, noise_rows, levels, mod_shift, mod_scale, total_rows):
    channels = latent_rows.shape[1]
    model_width = weights.shape[1]
    time_width = weights.shape[0] - 2 * channels
    in_weight = weights[:channels]
    time_weight = weights[channels : channels + time_width]
    out_weight = weights[channels + time_width :]
    level_embed, noise_level = embed_levels(levels, time_width)
    latent_f = latent_rows.astype(jnp.float32)
    noise_f = noise_rows.astype(jnp.float32)
    noised = ((1.0 - noise_level)[:, None] * latent_f + noise_level[:, None] * noise_f).astype(
        jnp.bfloat16
    )
    target = noise_f - latent_f
    embed_b = level_embed.astype(jnp.bfloat16)
    time_pre = jnp.dot(embed_b, time_weight, preferred_element_type=jnp.float32) / math.sqrt(
        time_width
    )
    hidden = jnp.dot(noised, in_weight, preferred_element_type=jnp.float32) / math.sqrt(
        channels
    ) + jax.nn.silu(time_pre)
    inverse = lax.rsqrt(jnp.mean(hidden * hidden, axis=-1, keepdims=True) + NORM_EPS)
    normed = hidden * inverse
    factor = 1.0 + mod_scale
    modded = (normed * factor + mod_shift).astype(jnp.bfloat16)
    output = lax.dot_general(
        modded, out_weight, (((1,), (1,)), ((), ())), preferred_element_type=jnp.float32
    ) / math.sqrt(model_width)
    out_grad = (2.0 / (total_rows * channels) * (output - target)).astype(jnp.bfloat16)
    grad_out = lax.dot_general(
        out_grad, modded, (((0,), (0,)), ((), ())), preferred_element_type=jnp.float32
    ) / math.sqrt(model_width)
    mod_grad = jnp.dot(out_grad, out_weight, preferred_element_type=jnp.float32) / math.sqrt(
        model_width
    )
    norm_grad = mod_grad * factor
    hid_grad = inverse * (norm_grad - normed * jnp.mean(norm_grad * normed, axis=-1, keepdims=True))
    sigmoid_pre = jax.nn.sigmoid(time_pre)
    pre_grad = hid_grad * (sigmoid_pre * (1.0 + time_pre * (1.0 - sigmoid_pre)))
    grad_in = lax.dot_general(
        noised,
        hid_grad.astype(jnp.bfloat16),
        (((0,), (0,)), ((), ())),
        preferred_element_type=jnp.float32,
    ) / math.sqrt(channels)
    grad_time = lax.dot_general(
        embed_b,
        pre_grad.astype(jnp.bfloat16),
        (((0,), (0,)), ((), ())),
        preferred_element_type=jnp.float32,
    ) / math.sqrt(time_width)
    return jnp.concatenate([grad_in, grad_time, grad_out], axis=0)


def adam_update(params, moment_one, moment_two, gradient):
    moment_one = BETA_ONE * moment_one + (1.0 - BETA_ONE) * gradient
    moment_two = BETA_TWO * moment_two + (1.0 - BETA_TWO) * gradient * gradient
    params = params - INNER_RATE * (
        moment_one / (jnp.sqrt(moment_two) + ADAM_EPS) + DECAY_RATE * params
    )
    return (params, moment_one, moment_two)


def on_device(
    outer_params,
    outer_momentum,
    inner_mean,
    inner_square,
    latents,
    noise_draw,
    timesteps,
    fragment,
    modulation,
):
    mod_rows = lax.dynamic_index_in_dim(modulation, fragment[0], 0, keepdims=False)
    mod_shift = mod_rows[0]
    mod_scale = mod_rows[1]
    total_rows = latents.shape[1] * lax.axis_size("fsdp")
    params = outer_params
    moment_one = inner_mean[0]
    moment_two = inner_square[0]
    for inner_step in range(STEPS):
        gathered = lax.all_gather(params.astype(jnp.bfloat16), "fsdp", axis=0, tiled=True)
        grad_local = local_grads(
            gathered,
            latents[inner_step],
            noise_draw[inner_step],
            timesteps[inner_step],
            mod_shift,
            mod_scale,
            total_rows,
        )
        gradient = lax.psum_scatter(
            grad_local.astype(jnp.bfloat16), "fsdp", scatter_dimension=0, tiled=True
        ).astype(jnp.float32)
        params, moment_one, moment_two = adam_update(params, moment_one, moment_two, gradient)
    drift = outer_params - params
    replicas = lax.axis_size("replica")
    average = lax.psum(drift.astype(jnp.bfloat16), "replica").astype(jnp.float32) / replicas
    new_momentum = NESTEROV * outer_momentum + average
    new_params = outer_params - OUTER_RATE * (average + NESTEROV * new_momentum)
    return (new_params, new_momentum, moment_one[None], moment_two[None])


def solution(mesh):
    return jax.shard_map(
        on_device,
        mesh=mesh,
        in_specs=(
            P("fsdp", None),
            P("fsdp", None),
            P("replica", "fsdp", None),
            P("replica", "fsdp", None),
            P(None, ("replica", "fsdp"), None),
            P(None, ("replica", "fsdp"), None),
            P(None, ("replica", "fsdp")),
            P(),
            P(),
        ),
        out_specs=(
            P("fsdp", None),
            P("fsdp", None),
            P("replica", "fsdp", None),
            P("replica", "fsdp", None),
        ),
        check_vma=False,
    )
```

profile of v0, /device:TPU:1, one launch (start us, length us, event | category | flops | bytes accessed | tf_op | source)
XLA Modules:
  0.0 411.7 jit_solution(10766023376895626933)
XLA Ops:
  7.2 0.0 copy-start.5
  7.2 0.0 copy-start.6
  7.2 0.0 all-gather.3.cloned.1.call-start
  7.2 1.7 convert_element_type.110
  8.9 0.0 all-gather.3.cloned.1.call-update
  9.0 0.0 reduce-scatter.3.cloned.1.call-start
  9.7 0.8 convert_add_fusion
  10.4 0.8 dynamic-slice_add_fusion
  11.3 2.2 fusion.32
  13.5 38.2 %all-gather.3.cloned.1.call-done = bf16[384,3072]{1,0:T(8,128)(2,1)} async-done(((bf16[24,3072]{1,0:T(8,128)(2,1)}), bf16[384,3072]{1,0:T(8,128)(2,1)}) %all-gather.3.cloned.1.call-update) | async-done | bytes 2359312 | tf_op jit(solution)/shard_map/all_gather | solution.py:114
  51.7 0.0 copy-start.1
  51.7 2.5 fusion.10
  54.2 0.0 copy-done.5
  54.3 0.0 copy-done.6
  54.3 0.0 copy-done.1
  54.3 2.6 multiply_reduce_fusion.3
  56.9 1.1 add_convert_fusion.1
  58.0 1.1 fusion.16
  59.1 0.7 fusion.3
  59.7 1.3 multiply_reduce_fusion.2
  61.0 4.0 fusion
  65.0 1.7 fusion.2
  66.7 0.0 copy-start
  66.7 0.0 copy-start.3
  66.7 0.0 copy-start.4
  66.7 1.6 pad_maximum_fusion
  68.3 0.0 reduce-scatter.3.cloned.1.call-update
  68.3 0.0 all-gather.5.cloned.1.call-start
  68.4 64.4 %reduce-scatter.3.cloned.1.call-done = bf16[24,3072]{1,0:T(8,128)(2,1)} async-done(((bf16[384,3072]{1,0:T(8,128)(2,1)}), bf16[24,3072]{1,0:T(8,128)(2,1)}) %reduce-scatter.3.cloned.1.call-update) | async-done | bytes 147472 | tf_op jit(solution)/shard_map/reduce_scatter | solution.py:124
  132.7 0.0 copy-done
  132.7 0.0 copy-done.3
  132.7 0.0 copy-done.4
  132.8 1.8 fusion.36
  134.6 0.0 all-gather.5.cloned.1.call-update
  134.6 0.0 reduce-scatter.5.cloned.1.call-start
  134.6 39.0 %all-gather.5.cloned.1.call-done = bf16[384,3072]{1,0:T(8,128)(2,1)} async-done(((bf16[24,3072]{1,0:T(8,128)(2,1)}), bf16[384,3072]{1,0:T(8,128)(2,1)}) %all-gather.5.cloned.1.call-update) | async-done | bytes 2359312 | tf_op jit(solution)/shard_map/all_gather | solution.py:114
  173.6 0.0 copy-start.2
  173.6 2.6 fusion.8
  176.2 0.0 copy-done.2
  176.2 2.6 multiply_reduce_fusion.1
  178.8 1.1 add_convert_fusion
  179.9 1.1 fusion.17
  181.0 0.7 fusion.5
  181.7 1.3 multiply_reduce_fusion
  182.9 4.0 fusion.1
  187.0 1.5 fusion.4
  188.5 0.0 copy-start.7
  188.5 0.0 copy-start.8
  188.5 1.6 pad_maximum_fusion.1
  190.1 0.0 reduce-scatter.5.cloned.1.call-update
  190.1 0.0 all-reduce.2.cloned.1.call-start
  190.1 63.8 %reduce-scatter.5.cloned.1.call-done = bf16[24,3072]{1,0:T(8,128)(2,1)} async-done(((bf16[384,3072]{1,0:T(8,128)(2,1)}), bf16[24,3072]{1,0:T(8,128)(2,1)}) %reduce-scatter.5.cloned.1.call-update) | async-done | bytes 147472 | tf_op jit(solution)/shard_map/reduce_scatter | solution.py:124
  254.0 0.0 copy-done.7
  254.0 2.2 fusion.35
  256.2 0.0 all-reduce.2.cloned.1.call-update
  256.2 147.1 %all-reduce.2.cloned.1.call-done = bf16[24,3072]{1,0:T(8,128)(2,1)} async-done(((bf16[24,3072]{1,0:T(8,128)(2,1)}), bf16[24,3072]{1,0:T(8,128)(2,1)}) %all-reduce.2.cloned.1.call-update) | async-done | bytes 147472 | tf_op jit(solution)/shard_map/psum | solution.py:130
  403.3 0.0 copy-done.8
  403.3 1.8 multiply_subtract_fusion
  (8 shorter events, 0.1 us)
Async XLA Ops:
  7.2 47.1 %copy-start.5 = (bf16[2,512,64]{1,2,0:T(8,128)(2,1)S(1)}, bf16[2,512,64]{1,2,0:T(8,128)(2,1)}, u32[]{:S(2)}) copy-start(bf16[2,512,64]{1,2,0:T(8,128)(2,1)} %param.14) | copy-start | bytes 393220
  7.2 47.1 %copy-start.6 = (bf16[2,512,64]{1,2,0:T(8,128)(2,1)S(1)}, bf16[2,512,64]{1,2,0:T(8,128)(2,1)}, u32[]{:S(2)}) copy-start(bf16[2,512,64]{1,2,0:T(8,128)(2,1)} %param.13) | copy-start | bytes 393220
  7.2 44.5 %all-gather.3.cloned.1.call-start = ((), (), s32[]{:S(2)}) async-start(), calls=%async_computation.2 | async-start | bytes 2506752 | tf_op jit(solution)/shard_map/all_gather | solution.py:114
  9.0 123.8 %reduce-scatter.3.cloned.1.call-start = ((), (), s32[]{:S(2)}) async-start(), calls=%async_computation.3 | async-start | bytes 2506752 | tf_op jit(solution)/shard_map/reduce_scatter | solution.py:124
  51.7 2.6 copy-start.1
  66.7 66.0 %copy-start = (f32[24,3072]{1,0:T(8,128)S(1)}, f32[24,3072]{1,0:T(8,128)}, u32[]{:S(2)}) copy-start(f32[24,3072]{1,0:T(8,128)} %param.9) | copy-start | bytes 884740
  66.7 66.0 %copy-start.3 = (f32[1,24,3072]{2,1,0:T(8,128)S(1)}, f32[1,24,3072]{2,1,0:T(8,128)}, u32[]{:S(2)}) copy-start(f32[1,24,3072]{2,1,0:T(8,128)} %param.11) | copy-start | bytes 884740
  66.7 66.0 %copy-start.4 = (f32[1,24,3072]{2,1,0:T(8,128)S(1)}, f32[1,24,3072]{2,1,0:T(8,128)}, u32[]{:S(2)}) copy-start(f32[1,24,3072]{2,1,0:T(8,128)} %param.12) | copy-start | bytes 884740
  68.3 105.3 %all-gather.5.cloned.1.call-start = ((), (), s32[]{:S(2)}) async-start(), calls=%async_computation.4 | async-start | bytes 2506752 | tf_op jit(solution)/shard_map/all_gather | solution.py:114
  134.6 119.4 %reduce-scatter.5.cloned.1.call-start = ((), (), s32[]{:S(2)}) async-start(), calls=%async_computation.5 | async-start | bytes 2506752 | tf_op jit(solution)/shard_map/reduce_scatter | solution.py:124
  173.6 2.6 copy-start.2
  188.5 65.5 %copy-start.7 = (bf16[24,3072]{1,0:T(8,128)(2,1)S(1)}, bf16[24,3072]{1,0:T(8,128)(2,1)}, u32[]{:S(2)}) copy-start(bf16[24,3072]{1,0:T(8,128)(2,1)} %reduce-scatter.3.cloned.1.call-done) | copy-start | bytes 442372
  188.5 214.9 %copy-start.8 = (f32[24,3072]{1,0:T(8,128)S(1)}, f32[24,3072]{1,0:T(8,128)}, u32[]{:S(2)}) copy-start(f32[24,3072]{1,0:T(8,128)} %param.10) | copy-start | bytes 884740
  190.1 213.2 %all-reduce.2.cloned.1.call-start = ((), (), s32[]{:S(2)}) async-start(), calls=%async_computation.6 | async-start | bytes 294912 | tf_op jit(solution)/shard_map/psum | solution.py:130
Sparse Core Ops, SparseCore 0:
  10.4 41.2 all-gather.2
  68.5 64.2 reduce-scatter.2
  135.2 38.4 all-gather.4
  190.2 63.7 reduce-scatter.4
  257.0 146.2 all-reduce.1
where the time goes:
time: 419 us; the launch traced here: 412 us
  waiting for transfers between devices  353 us (84%)
  matrix products  27.5 us (7%)
  other arithmetic  16.8 us (4%)
  between operations  14.6 us (3%)
    psum x1, waiting for transfers between devices, on_device(): lax.psum(drift.astype(jnp.bfloat16), 'replica').astype(jnp.float32)  147 us
    reduce_scatter x2, waiting for transfers between devices, on_device(): lax.psum_scatter(grad_local.astype(jnp.bfloat16), 'fsdp', scatter_dimensi...  128 us
    all_gather x2, waiting for transfers between devices, on_device(): lax.all_gather(params.astype(jnp.bfloat16), 'fsdp', axis=0, tiled=True)  77.2 us
  transfers between devices with their start and end apart: 5, of which 5 were waited for; matrix products, arithmetic and copies ran while one was open for 1% of the time, Pallas kernels for 0%

commit v1 on v0

v1 whole, which is shorter than its diff:
```python
import math

import jax
import jax.numpy as jnp
from jax import lax
from jax.experimental import pallas as pl
from jax.experimental.pallas import tpu as pltpu
from jax.sharding import PartitionSpec as P

STEPS = 2
LEVELS = 1000


BETA_ONE = 0.9
BETA_TWO = 0.95
INNER_RATE = 0.2
DECAY_RATE = 0.1
ADAM_EPS = 1e-08
NORM_EPS = 1e-06
OUTER_RATE = 0.7
NESTEROV = 0.9

CORES = 2
LANES = 128
ROW_CHUNK = 16
FWD_COLUMNS = 256
STRIP_ROWS = 16
STRIP_PARTS = 4
KERNEL_VMEM = 24 * 2**20

BF16 = jnp.bfloat16
F32 = jnp.float32
VMEM = pl.BlockSpec(memory_space=pltpu.VMEM)
SMEM = pl.BlockSpec(memory_space=pltpu.SMEM)
TRANSPOSED = (((1,), (1,)), ((), ()))


def local_call(kernel, name, args, outs, scratch=(), core=None, flops=0, hbm_outs=False):
    place = pltpu.VMEM if not hbm_outs else jax.ShapeDtypeStruct
    specs = [VMEM] * len(args)
    values = [pltpu.with_memory_space_constraint(a, pltpu.VMEM) for a in args]
    if core is not None:
        specs = [SMEM] + specs
        values = [core] + values
    moved = sum(math.prod(o[0]) * 4 for o in outs) + sum(a.size * a.dtype.itemsize for a in args)
    return pl.pallas_call(
        kernel,
        in_specs=specs,
        out_specs=[VMEM] * len(outs),
        out_shape=[place(shape, dtype) for shape, dtype in outs],
        scratch_shapes=list(scratch),
        compiler_params=pltpu.CompilerParams(vmem_limit_bytes=KERNEL_VMEM),
        cost_estimate=pl.CostEstimate(flops=flops, bytes_accessed=moved, transcendentals=0),
        name=name,
    )(*values)


def core_swap(values, width):
    return lax.ppermute(values, "fsdp", [(i, i ^ 1) for i in range(width)])


def chip_exchange(blocks, width):
    groups = [list(range(core, width, CORES)) for core in range(CORES)]
    return lax.all_to_all(blocks, "fsdp", 0, 0, axis_index_groups=groups)


def pair_kernel(core, own, got, pair, *copies):
    rows = own.shape[0]
    half = own.shape[1] // CORES

    @pl.when(core[0] == 0)
    def _():
        pair[0:rows] = own[:, 0:half]
        pair[rows:] = got[:, 0:half]

    @pl.when(core[0] != 0)
    def _():
        pair[0:rows] = got[:, half:]
        pair[rows:] = own[:, half:]

    for copy in copies:
        block = pair[...].astype(BF16)
        for chip in range(copy.shape[0]):
            copy[chip] = block


def to_pair(values, core, width, copies=()):
    rows, columns = values.shape
    shape = (rows * CORES, columns // CORES)
    outs = [(shape, F32)] + [((n,) + shape, BF16) for n in copies]
    return local_call(pair_kernel, "pair", (values, core_swap(values, width)), outs, core=core)


def unpair_kernel(core, own, got, out):
    rows = out.shape[0]
    half = out.shape[1] // CORES

    @pl.when(core[0] == 0)
    def _():
        out[:, 0:half] = own[0:rows]
        out[:, half:] = got[0:rows]

    @pl.when(core[0] != 0)
    def _():
        out[:, 0:half] = got[rows:]
        out[:, half:] = own[rows:]


def from_pair(values, core, width):
    rows, columns = values.shape
    outs = [((rows // CORES, columns * CORES), F32)]
    args = (values, core_swap(values, width))
    return local_call(unpair_kernel, "unpair", args, outs, core=core, hbm_outs=True)[0]


def forward_kernel(tokens, embed, weights, factor, shift, hid, mod, slope, out, square, bias, pre_buf, in_buf):
    channels = tokens.shape[1]
    time_end = channels + embed.shape[1]
    square[...] = jnp.zeros_like(square)
    for index in range(weights.shape[1] // FWD_COLUMNS):
        slot = index % 2
        cols = pl.ds(index * FWD_COLUMNS, FWD_COLUMNS)
        pre_buf[slot] = jnp.dot(
            embed[...], weights[channels:time_end, cols], preferred_element_type=F32
        )
        in_buf[slot] = jnp.dot(tokens[...], weights[0:channels, cols], preferred_element_type=F32)
        scale = jnp.broadcast_to(factor[0:1, cols], (ROW_CHUNK, FWD_COLUMNS))
        for start in range(0, tokens.shape[0], ROW_CHUNK):
            rows = pl.ds(start, ROW_CHUNK)
            pre = pre_buf[slot, rows, :]
            sigma = 0.5 * jnp.tanh(0.5 * pre) + 0.5
            silu = pre * sigma
            hidden = in_buf[slot, rows, :] + silu
            mod[rows, cols] = (hidden * scale).astype(BF16)
            hid[rows, cols] = hidden.astype(BF16)
            slope[rows, cols] = (sigma + (silu - silu * sigma)).astype(BF16)
            power = hidden * hidden
            partial = power[:, 0:LANES]
            for lane in range(LANES, FWD_COLUMNS, LANES):
                partial = partial + power[:, lane : lane + LANES]
            square[rows, :] += partial
    out_weight = weights[time_end:, :]
    out[...] = lax.dot_general(mod[...], out_weight, TRANSPOSED, preferred_element_type=F32)
    bias[...] = lax.dot_general(shift[...], out_weight, TRANSPOSED, preferred_element_type=F32)


def forward(tokens, embed, weights, factor, shift):
    rows, columns = tokens.shape[0], weights.shape[1]
    channels = tokens.shape[1]
    outs = [((rows, columns), BF16)] * 3 + [
        ((rows, channels), F32),
        ((rows, LANES), F32),
        ((shift.shape[0], channels), F32),
    ]
    scratch = [pltpu.VMEM((2, rows, FWD_COLUMNS), F32)] * 2
    flops = 2 * rows * columns * weights.shape[0]
    args = (tokens, embed, weights, factor, shift)
    return local_call(forward_kernel, "forward", args, outs, scratch, flops=flops)


def make_head_kernel(model_width, total_rows):
    def head_kernel(out_a, out_b, square_a, square_b, bias_a, bias_b, target, grad, grad_t, pull, grad_sum):
        root = 1.0 / math.sqrt(model_width)
        raw = out_a[...] + out_b[...]
        power = jnp.sum(square_a[...] + square_b[...], axis=1, keepdims=True)
        inverse = lax.rsqrt(power * (1.0 / model_width) + NORM_EPS)
        bias = jnp.sum(bias_a[...] + bias_b[...], axis=0, keepdims=True)
        output = (inverse * raw + bias) * root
        out_grad = (2.0 / (total_rows * raw.shape[1])) * (output - target[...])
        scaled = (out_grad * inverse).astype(BF16)
        wide = scaled.astype(F32)
        grad[...] = scaled
        grad_t[...] = wide.T.astype(BF16)
        pulled = inverse * inverse * (root / model_width) * jnp.sum(wide * raw, axis=1, keepdims=True)
        pull[...] = jnp.broadcast_to(pulled, pull.shape)
        summed = jnp.sum(out_grad.T, axis=1, keepdims=True)
        grad_sum[...] = jnp.broadcast_to(summed, grad_sum.shape)

    return head_kernel


def make_backward_kernel(model_width):
    def backward_kernel(
        hid, mod, slope, weights, factor, shift, tokens_t, embed_t, grad, grad_t, pull, grad_sum,
        out, mod_buf, hid_buf, pre_buf,
    ):
        root = 1.0 / math.sqrt(model_width)
        channels = tokens_t.shape[0]
        time_end = channels + embed_t.shape[0]
        columns = out.shape[1]
        mod_buf[...] = jnp.dot(grad[...], weights[time_end:, :], preferred_element_type=F32)
        scale = jnp.broadcast_to(factor[0:1, :] * root, (ROW_CHUNK, columns))
        for start in range(0, grad.shape[0], ROW_CHUNK):
            rows = pl.ds(start, ROW_CHUNK)
            pulled = jnp.concatenate([pull[rows, :]] * (columns // LANES), axis=1)
            hid_grad = mod_buf[rows, :] * scale - hid[rows, :].astype(F32) * pulled
            hid_buf[rows, :] = hid_grad.astype(BF16)
            pre_buf[rows, :] = (hid_grad * slope[rows, :].astype(F32)).astype(BF16)
        out[0:channels, :] = jnp.dot(
            tokens_t[...], hid_buf[...], preferred_element_type=F32
        ).astype(BF16)
        out[channels:time_end, :] = jnp.dot(
            embed_t[...], pre_buf[...], preferred_element_type=F32
        ).astype(BF16)
        grad_out = jnp.dot(grad_t[...], mod[...], preferred_element_type=F32)
        summed = jnp.concatenate([grad_sum[...]] * (columns // LANES), axis=1)
        out[time_end:, :] = ((grad_out + summed * shift[0:1, :]) * root).astype(BF16)

    return backward_kernel


def backward(state, weights, factor, shift, tokens_t, embed_t, head, model_width):
    rows, columns = state[0].shape
    scratch = [
        pltpu.VMEM((rows, columns), F32),
        pltpu.VMEM((rows, columns), BF16),
        pltpu.VMEM((rows, columns), BF16),
    ]
    flops = 2 * rows * columns * (weights.shape[0] + tokens_t.shape[0])
    args = (*state, weights, factor, shift, tokens_t, embed_t, *head)
    outs = [(weights.shape, BF16)]
    return local_call(make_backward_kernel(model_width), "backward", args, outs, scratch, flops=flops)[0]


def prepare_tokens(latent_rows, noise_rows, levels, channels, time_width):
    half_width = time_width // 2
    noise_level = (levels.astype(F32) + 0.5) / LEVELS
    frequencies = jnp.exp(-math.log(10000.0) * jnp.arange(half_width, dtype=F32) / half_width)
    angles = (1000.0 * noise_level)[:, None] * frequencies[None, :]
    embed = jnp.concatenate([jnp.cos(angles), jnp.sin(angles)], axis=-1).astype(BF16)
    latent_f = latent_rows.astype(F32)
    noise_f = noise_rows.astype(F32)
    noised = ((1.0 - noise_level)[:, None] * latent_f + noise_level[:, None] * noise_f).astype(BF16)
    noised = noised * BF16(1.0 / math.sqrt(channels))
    embed = embed * BF16(1.0 / math.sqrt(time_width))
    return noised, embed, noised.T, embed.T, noise_f - latent_f


def step_kernel(blocks, params, mean, square, new_mean, new_square, new_params, copies):
    first, second, new = adam(blocks, params, mean, square)
    new_mean[...] = first
    new_square[...] = second
    new_params[...] = new
    block = new.astype(BF16)
    for chip in range(copies.shape[0]):
        copies[chip] = block


def last_kernel(blocks, params, mean, square, start, new_mean, new_square, strips):
    first, second, new = adam(blocks, params, mean, square)
    new_mean[...] = first
    new_square[...] = second
    drift = (start[...] - new).astype(BF16)
    rows, columns = strips.shape[1:]
    used = 0
    for top in range(0, drift.shape[0], rows):
        for left in range(0, drift.shape[1], columns):
            strips[used] = drift[top : top + rows, left : left + columns]
            used += 1
    for index in range(used, strips.shape[0]):
        strips[index] = jnp.zeros((rows, columns), BF16)


def adam(blocks, params, mean, square):
    gradient = blocks[0].astype(F32)
    for chip in range(1, blocks.shape[0]):
        gradient = gradient + blocks[chip].astype(F32)
    old = params[...]
    first = BETA_ONE * mean[...] + (1.0 - BETA_ONE) * gradient
    second = BETA_TWO * square[...] + (1.0 - BETA_TWO) * gradient * gradient
    new = old - INNER_RATE * (first / (jnp.sqrt(second) + ADAM_EPS) + DECAY_RATE * old)
    return first, second, new


def strip_sum_kernel(strips, copies):
    total = strips[0].astype(F32)
    for index in range(1, strips.shape[0]):
        total = total + strips[index].astype(F32)
    block = total.astype(BF16)
    for index in range(copies.shape[0]):
        copies[index] = block


def make_outer_kernel(replicas):
    def outer_kernel(core, own, got, params, momentum, new_params, new_momentum, own_buf, got_buf):
        strip_rows, strip_columns = own.shape[1:]
        rows = params.shape[0]
        half = params.shape[1] // CORES
        index = 0
        for top in range(0, rows * CORES, strip_rows):
            for left in range(0, half, strip_columns):
                place = (slice(top, top + strip_rows), slice(left, left + strip_columns))
                own_buf[place] = own[index].astype(F32)
                got_buf[place] = got[index].astype(F32)
                index += 1

        def finish(cols, values):
            average = values * (1.0 / replicas)
            moved = NESTEROV * momentum[:, cols] + average
            new_momentum[:, cols] = moved
            new_params[:, cols] = params[:, cols] - OUTER_RATE * (average + NESTEROV * moved)

        @pl.when(core[0] == 0)
        def _():
            finish(slice(0, half), own_buf[0:rows])
            finish(slice(half, 2 * half), got_buf[0:rows])

        @pl.when(core[0] != 0)
        def _():
            finish(slice(0, half), got_buf[rows:])
            finish(slice(half, 2 * half), own_buf[rows:])

    return outer_kernel


def on_device(
    outer_params,
    outer_momentum,
    inner_mean,
    inner_square,
    latents,
    noise_draw,
    timesteps,
    fragment,
    modulation,
):
    width = lax.axis_size("fsdp")
    replicas = lax.axis_size("replica")
    chips = width // CORES
    core = (lax.axis_index("fsdp") % CORES).astype(jnp.int32)
    core_arg = core.reshape(1)
    rows, model_width = outer_params.shape
    half = model_width // CORES
    channels = latents.shape[2]
    time_width = rows * width - 2 * channels
    total_rows = latents.shape[1] * width

    start, copies = to_pair(outer_params, core_arg, width, (chips,))
    gathered = chip_exchange(copies, width)

    mod_rows = lax.dynamic_index_in_dim(modulation, fragment[0], 0, keepdims=False)
    mods = []
    for side in (core, 1 - core):
        rows_here = lax.dynamic_slice_in_dim(mod_rows, side * half, half, 1)
        shift = rows_here[0:1]
        high = shift.astype(BF16)
        low = (shift - high.astype(F32)).astype(BF16)
        terms = jnp.concatenate([high, low, jnp.zeros((14, half), BF16)], axis=0)
        mods.append((1.0 + rows_here[1:2], shift, terms))
    prepared = [
        prepare_tokens(latents[s], noise_draw[s], timesteps[s], channels, time_width)
        for s in range(STEPS)
    ]
    params = start
    mean = to_pair(inner_mean[0], core_arg, width)[0]
    square = to_pair(inner_square[0], core_arg, width)[0]
    pair_shape = start.shape

    for step in range(STEPS):
        tokens, embed, tokens_t, embed_t, target = prepared[step]
        weights = gathered.reshape(chips * pair_shape[0], half)
        other = core_swap(weights, width)
        state = forward(tokens, embed, weights, mods[0][0], mods[0][2])
        state_other = forward(tokens, embed, other, mods[1][0], mods[1][2])
        shapes = [
            ((target.shape[0], channels), BF16),
            ((channels, target.shape[0]), BF16),
            ((target.shape[0], LANES), F32),
            ((channels, LANES), F32),
        ]
        head = local_call(
            make_head_kernel(model_width, total_rows),
            "head",
            (state[3], state_other[3], state[4], state_other[4], state[5], state_other[5], target),
            shapes,
        )
        grad_other = backward(
            state_other[:3], other, mods[1][0], mods[1][1], tokens_t, embed_t, head, model_width
        )
        received = core_swap(grad_other, width)
        head, grad_other = lax.optimization_barrier((head, grad_other))
        grad_mine = backward(
            state[:3], weights, mods[0][0], mods[0][1], tokens_t, embed_t, head, model_width
        )
        pair_sum = (grad_mine.astype(F32) + received.astype(F32)).astype(BF16)
        blocks = chip_exchange(pair_sum.reshape((chips,) + pair_shape), width)
        moments = [(pair_shape, F32)] * 2
        if step + 1 < STEPS:
            outs = moments + [(pair_shape, F32), ((chips,) + pair_shape, BF16)]
            mean, square, params, copies = local_call(
                step_kernel, "update", (blocks, params, mean, square), outs
            )
            gathered = chip_exchange(copies, width)
        else:
            strip = (STRIP_ROWS, half // STRIP_PARTS)
            outs = moments + [((replicas,) + strip, BF16)]
            mean, square, strips = local_call(
                last_kernel, "update_last", (blocks, params, mean, square, start), outs
            )
    strips = lax.all_to_all(strips, "replica", 0, 0)
    strips = local_call(strip_sum_kernel, "strip_sum", (strips,), [(strips.shape, BF16)])[0]
    strips = lax.all_to_all(strips, "replica", 0, 0)
    new_mean = from_pair(mean, core_arg, width)
    new_square = from_pair(square, core_arg, width)
    new_params, new_momentum = local_call(
        make_outer_kernel(replicas),
        "outer",
        (strips, core_swap(strips, width), outer_params, outer_momentum),
        [(outer_params.shape, F32)] * 2,
        [pltpu.VMEM(pair_shape, F32)] * 2,
        core=core_arg,
        hbm_outs=True,
    )
    return (new_params, new_momentum, new_mean[None], new_square[None])


def solution(mesh):
    return jax.shard_map(
        on_device,
        mesh=mesh,
        in_specs=(
            P("fsdp", None),
            P("fsdp", None),
            P("replica", "fsdp", None),
            P("replica", "fsdp", None),
            P(None, ("replica", "fsdp"), None),
            P(None, ("replica", "fsdp"), None),
            P(None, ("replica", "fsdp")),
            P(),
            P(),
        ),
        out_specs=(
            P("fsdp", None),
            P("fsdp", None),
            P("replica", "fsdp", None),
            P("replica", "fsdp", None),
        ),
        check_vma=False,
    )
```

time: 419 us -> 160 us (0.38); the launches traced: 412 us -> 159 us
  waiting for transfers between devices: 353 us -> 38.3 us
  blocking collectives: 0 us -> 57.8 us
  matrix products: 27.5 us -> 0 us
  starting transfers between devices: 0.21 us -> 26 us
  Pallas kernels: 0 us -> 20.6 us
  between operations: 14.6 us -> 1.72 us
  other arithmetic: 16.8 us -> 7.44 us
  local copies, waits for them, and re-layouts: 0.04 us -> 7.46 us
    psum x1 -> x0, waiting for transfers between devices: 147 us -> none  [on_device(): lax.psum(drift.astype(jnp.bfloat16), 'replica').astype(jnp.float32)]
    reduce_scatter x2 -> x0, waiting for transfers between devices: 128 us -> none  [on_device(): lax.psum_scatter(grad_local.astype(jnp.bfloat16), 'fsdp', scatter_dimensi...]
    all_gather x2 -> x0, waiting for transfers between devices: 77.2 us -> none  [on_device(): lax.all_gather(params.astype(jnp.bfloat16), 'fsdp', axis=0, tiled=True)]
    all_to_all x0 -> x3, blocking collectives: none -> 57.8 us  [the longest x2 38.5 us: chip_exchange(): return lax.all_to_all(blocks, 'fsdp', 0, 0, axis_index_groups=groups)]
    all_to_all x0 -> x3, waiting for transfers between devices: none -> 33.1 us  [the longest x2 26.4 us: chip_exchange(): return lax.all_to_all(blocks, 'fsdp', 0, 0, axis_index_groups=groups)]
    dot_general x14 -> x0, matrix products: 27.5 us -> none  [the longest x2 8.05 us: local_grads(): lax.dot_general(embed_b, pre_grad.astype(jnp.bfloat16), (((0,), (0,)), ((...]
    pallas_call x0 -> x19, Pallas kernels: none -> 20.6 us  [local_call(): pl.pallas_call(kernel, in_specs=specs, out_specs=[VMEM] * len(outs), out_...]
    ppermute x0 -> x10, starting transfers between devices: none -> 14.4 us  [core_swap(): return lax.ppermute(values, 'fsdp', [(i, i ^ 1) for i in range(width)])]
  transfers between devices with their start and end apart: 5 -> 13, of which waited for: 5 -> 8; matrix products, arithmetic and copies ran while one was open for 1% -> 6% of each run, Pallas kernels for 0% -> 6%
where the time goes in v1:
time: 160 us; the launch traced here: 159 us
  blocking collectives  57.8 us (36%)
  waiting for transfers between devices  38.3 us (24%)
  starting transfers between devices  26 us (16%)
  Pallas kernels  20.6 us (13%)
  local copies, waits for them, and re-layouts  7.46 us (5%)
  other arithmetic  7.44 us (5%)
  between operations  1.72 us (1%)
    all_to_all x2, blocking collectives, chip_exchange(): return lax.all_to_all(blocks, 'fsdp', 0, 0, axis_index_groups=groups)  38.5 us
    all_to_all x2, waiting for transfers between devices, chip_exchange(): return lax.all_to_all(blocks, 'fsdp', 0, 0, axis_index_groups=groups)  26.4 us
    pallas_call x19, Pallas kernels, local_call(): pl.pallas_call(kernel, in_specs=specs, out_specs=[VMEM] * len(outs), out_...  20.6 us
    all_to_all x1, blocking collectives, on_device(): strips = lax.all_to_all(strips, 'replica', 0, 0)  19.2 us
    ppermute x10, starting transfers between devices, core_swap(): return lax.ppermute(values, 'fsdp', [(i, i ^ 1) for i in range(width)])  14.4 us
    all_to_all x2, starting transfers between devices, chip_exchange(): return lax.all_to_all(blocks, 'fsdp', 0, 0, axis_index_groups=groups)  7.63 us
    all_to_all x1, waiting for transfers between devices, on_device(): strips = lax.all_to_all(strips, 'replica', 0, 0)  6.66 us
    ppermute x10, waiting for transfers between devices, core_swap(): return lax.ppermute(values, 'fsdp', [(i, i ^ 1) for i in range(width)])  5.23 us
  transfers between devices with their start and end apart: 13, of which 8 were waited for; matrix products, arithmetic and copies ran while one was open for 6% of the time, Pallas kernels for 6%

profile of v1, /device:TPU:1, one launch (start us, length us, event | category | flops | bytes accessed | tf_op | source)
XLA Modules:
  0.0 159.3 jit_solution(17849832349253894069)
XLA Ops:
  0.6 3.3 %collective-permute-start = (f32[24,3072]{1,0:T(8,128)}, f32[24,3072]{1,0:T(8,128)S(1)}, u32[]{:S(2)}, u32[]{:S(2)}) collective-permute-start(f32[24,3072]{1,0:T(8,128)} %params.1), channel_id=1, source_target_pairs={{0,1},{1,0},{2,3},{3,2},{4,5},{5,4},{6,7},{7,6},{8,9},{9,8},{10,11... | collective-permute-start | bytes 884744 | tf_op jit(solution)/shard_map/ppermute | solution.py:59
  4.0 1.4 collective-permute-done.got
  5.4 1.0 copy-done
  6.3 1.2 pair.3
  7.5 3.9 %all-to-all-start = ((bf16[8,48,1536]{2,1,0:T(8,128)(2,1)}), bf16[8,48,1536]{2,1,0:T(8,128)(2,1)S(1)}, u32[]{:S(2)}, u32[]{:S(2)}) async-start(bf16[8,48,1536]{2,1,0:T(8,128)(2,1)} %get-tuple-element.55), calls=%async_computation | async-start | bytes 2359296 | tf_op jit(solution)/shard_map/all_to_all | solution.py:64
  12.2 0.1 fusion.9
  12.2 0.1 copy.13.tokens
  12.4 2.9 %fusion.2 = (bf16[512,128]{0,1:T(8,128)(2,1)S(1)}, bf16[512,128]{0,1:T(8,128)(2,1)S(1)}, bf16[512,128]{0,1:T(8,128)(2,1)}, bf16[512,128]{0,1:T(8,128)(2,1)}) fusion(f32[512]{0:T(512)S(1)} %bitcast.65, f32[128]{0:T(128)S(1)} %multiply_exponential_fusion, f32[512]{0:T(512)S(1)} %bitcast.67), kind=kLoop, calls=%fused_computation.8 | loop fusion | flops 393216 | bytes 528896 | tf_op jit(solution)/shard_map/convert.4
  15.3 0.1 copy.14.embed
  15.5 0.7 convert_subtract_fusion
  16.2 0.1 copy.17.target
  16.3 0.1 pad.5.clone
  16.4 11.6 %all-to-all-done = bf16[8,48,1536]{2,1,0:T(8,128)(2,1)S(1)} async-done(((bf16[8,48,1536]{2,1,0:T(8,128)(2,1)}), bf16[8,48,1536]{2,1,0:T(8,128)(2,1)S(1)}, u32[]{:S(2)}, u32[]{:S(2)}) %all-to-all-start) | async-done | bytes 1179680 | tf_op jit(solution)/shard_map/all_to_all | solution.py:64
  28.0 1.5 collective-permute-start.1
  29.6 1.0 fusion.14
  30.6 0.1 maximum_maximum_fusion
  30.7 1.9 %forward.4 = (bf16[512,1536]{1,0:T(8,128)(2,1)S(1)}, bf16[512,1536]{1,0:T(8,128)(2,1)S(1)}, bf16[512,1536]{1,0:T(8,128)(2,1)S(1)}, f32[512,64]{1,0:T(8,128)S(1)}...) custom-call(bf16[512,64]{1,0:T(8,128)(2,1)S(1)} %copy.13.tokens, bf16[512,256]{1,0:T(8,128)(2,1)S(1)} %copy.14.embed, ...), custom_call_target="tpu_custom_call" | custom-call | flops 603979776 | bytes 11397120 | tf_op jit(solution)/shard_map/forward/pallas_call | solution.py:46
  32.6 1.9 %forward.5 = (bf16[512,1536]{1,0:T(8,128)(2,1)S(1)}, bf16[512,1536]{1,0:T(8,128)(2,1)S(1)}, bf16[512,1536]{1,0:T(8,128)(2,1)S(1)}, f32[512,64]{1,0:T(8,128)S(1)}...) custom-call(bf16[512,64]{1,0:T(8,128)(2,1)S(1)} %copy.13.tokens, bf16[512,256]{1,0:T(8,128)(2,1)S(1)} %copy.14.embed, ...), custom_call_target="tpu_custom_call" | custom-call | flops 603979776 | bytes 11397120 | tf_op jit(solution)/shard_map/forward/pallas_call | solution.py:46
  34.5 0.5 head.2
  35.0 1.6 %backward.4 = bf16[384,1536]{1,0:T(8,128)(2,1)S(1)} custom-call(bf16[512,1536]{1,0:T(8,128)(2,1)S(1)} %get-tuple-element.69.hid, bf16[512,1536]{1,0:T(8,128)(2,1)S(1)} %get-tuple-element.70.mod, bf16[512,1536]{1,0:T(8,128)(2,1)S(1)} %get-tuple-element.71.slope, bf16[384,1536]{1,0:T(8,128)(2,1)S(1)} %collective-permute-done.1.weights, ...), custom_call_target="tpu_custom_call" | custom-call | flops 704643072 | bytes 9023488 | tf_op jit(solution)/shard_map/backward/pallas_call | solution.py:46
  36.6 0.1 collective-permute-start.2
  36.7 1.6 %backward.5 = bf16[384,1536]{1,0:T(8,128)(2,1)S(1)} custom-call(bf16[512,1536]{1,0:T(8,128)(2,1)S(1)} %get-tuple-element.56.hid, bf16[512,1536]{1,0:T(8,128)(2,1)S(1)} %get-tuple-element.57.mod, bf16[512,1536]{1,0:T(8,128)(2,1)S(1)} %get-tuple-element.58.slope, bf16[384,1536]{1,0:T(8,128)(2,1)S(1)} %bitcast.49, f32[1,1536]{1,0:T(1,128)S(1)} %get-tuple-element.111.factor, ...), custom_call_target="tpu_custom_call" | custom-call | flops 704643072 | bytes 9023488 | tf_op jit(solution)/shard_map/backward/pallas_call | solution.py:46
  38.3 1.2 collective-permute-done.2
  39.5 1.4 add_convert_fusion.1
  40.9 3.7 %all-to-all-start.1 = ((bf16[8,48,1536]{2,1,0:T(8,128)(2,1)}), bf16[8,48,1536]{2,1,0:T(8,128)(2,1)S(1)}, u32[]{:S(2)}, u32[]{:S(2)}) async-start(bf16[8,48,1536]{2,1,0:T(8,128)(2,1)} %bitcast.17), calls=%async_computation.1 | async-start | bytes 2359296 | tf_op jit(solution)/shard_map/all_to_all | solution.py:64
  44.6 0.2 collective-permute-start.3
  44.8 0.4 collective-permute-start.4
  45.2 1.1 collective-permute-done.3.got
  46.3 0.4 collective-permute-done.4.got
  46.7 0.2 pair.5.square
  46.9 14.8 %all-to-all-done.1.blocks = bf16[8,48,1536]{2,1,0:T(8,128)(2,1)S(1)} async-done(((bf16[8,48,1536]{2,1,0:T(8,128)(2,1)}), bf16[8,48,1536]{2,1,0:T(8,128)(2,1)S(1)}, u32[]{:S(2)}, u32[]{:S(2)}) %all-to-all-start.1) | async-done | bytes 1179680 | tf_op jit(solution)/shard_map/all_to_all | solution.py:64
  61.7 0.4 update.1
  62.1 0.0 copy-start.2
  62.1 0.0 copy-start.4
  62.2 19.1 %all_to_all.30 = bf16[8,48,1536]{2,1,0:T(8,128)(2,1)S(1)} all-to-all(bf16[8,48,1536]{2,1,0:T(8,128)(2,1)S(1)} %get-tuple-element.77), channel_id=1, replica_groups={{0,2,4,6,8,10,12,14},{1,3,5,7,9,11,13,15},{16,18,20,22,24,26,28,30},{17..., dimensions={0} | all-to-all | bytes 2359296 | tf_op jit(solution)/shard_map/all_to_all | solution.py:64
  81.3 1.7 %collective-permute-start.5 = (bf16[384,1536]{1,0:T(8,128)(2,1)S(1)}, bf16[384,1536]{1,0:T(8,128)(2,1)S(1)}, u32[]{:S(2)}, u32[]{:S(2)}) collective-permute-start(bf16[384,1536]{1,0:T(8,128)(2,1)S(1)} %bitcast.50), channel_id=1, source_target_pairs={{0,1},{1,0},{2,3},{3,2},{4,5},{5,4},{6,7},{7,6},{8,9},{9,8},{10,11... | collective-permute-start | bytes 3538952 | tf_op jit(solution)/shard_map/ppermute | solution.py:59
  83.0 0.8 copy.18.tokens
  83.8 1.0 fusion.13
  84.8 0.8 copy.19.embed
  85.7 1.0 copy.22.target
  86.7 0.9 copy-done.9
  87.6 0.9 copy-done.10
  88.5 0.7 copy-done.12
  89.2 0.8 copy-done.19
  90.0 1.9 %forward.6 = (bf16[512,1536]{1,0:T(8,128)(2,1)S(1)}, bf16[512,1536]{1,0:T(8,128)(2,1)S(1)}, bf16[512,1536]{1,0:T(8,128)(2,1)S(1)}, f32[512,64]{1,0:T(8,128)S(1)}...) custom-call(bf16[512,64]{1,0:T(8,128)(2,1)S(1)} %copy-done.10, bf16[512,256]{1,0:T(8,128)(2,1)S(1)} %copy-done.9, ...), custom_call_target="tpu_custom_call" | custom-call | flops 603979776 | bytes 11397120 | tf_op jit(solution)/shard_map/forward/pallas_call | solution.py:46
  92.0 1.9 %forward.7 = (bf16[512,1536]{1,0:T(8,128)(2,1)S(1)}, bf16[512,1536]{1,0:T(8,128)(2,1)S(1)}, bf16[512,1536]{1,0:T(8,128)(2,1)S(1)}, f32[512,64]{1,0:T(8,128)S(1)}...) custom-call(bf16[512,64]{1,0:T(8,128)(2,1)S(1)} %copy-done.10, bf16[512,256]{1,0:T(8,128)(2,1)S(1)} %copy-done.9, ...), custom_call_target="tpu_custom_call" | custom-call | flops 603979776 | bytes 11397120 | tf_op jit(solution)/shard_map/forward/pallas_call | solution.py:46
  93.9 0.5 head.3
  94.4 1.8 %backward.6 = bf16[384,1536]{1,0:T(8,128)(2,1)S(1)} custom-call(bf16[512,1536]{1,0:T(8,128)(2,1)S(1)} %get-tuple-element.91.hid, bf16[512,1536]{1,0:T(8,128)(2,1)S(1)} %get-tuple-element.92.mod, bf16[512,1536]{1,0:T(8,128)(2,1)S(1)} %get-tuple-element.93.slope, bf16[384,1536]{1,0:T(8,128)(2,1)S(1)} %collective-permute-done.5.weights, ...), custom_call_target="tpu_custom_call" | custom-call | flops 704643072 | bytes 9023488 | tf_op jit(solution)/shard_map/backward/pallas_call | solution.py:46
  96.2 0.1 collective-permute-start.6
  96.3 1.7 %backward.7 = bf16[384,1536]{1,0:T(8,128)(2,1)S(1)} custom-call(bf16[512,1536]{1,0:T(8,128)(2,1)S(1)} %get-tuple-element.78.hid, bf16[512,1536]{1,0:T(8,128)(2,1)S(1)} %get-tuple-element.79.mod, bf16[512,1536]{1,0:T(8,128)(2,1)S(1)} %get-tuple-element.80.slope, bf16[384,1536]{1,0:T(8,128)(2,1)S(1)} %bitcast.52, f32[1,1536]{1,0:T(1,128)S(1)} %copy-done.13, ...), custom_call_target="tpu_custom_call" | custom-call | flops 704643072 | bytes 9023488 | tf_op jit(solution)/shard_map/backward/pallas_call | solution.py:46
  98.0 1.1 collective-permute-done.6
  99.1 0.3 add_convert_fusion
  99.4 19.4 %all_to_all.31.blocks = bf16[8,48,1536]{2,1,0:T(8,128)(2,1)S(1)} all-to-all(bf16[8,48,1536]{2,1,0:T(8,128)(2,1)S(1)} %bitcast.61), channel_id=1, replica_groups={{0,2,4,6,8,10,12,14},{1,3,5,7,9,11,13,15},{16,18,20,22,24,26,28,30},{17..., dimensions={0} | all-to-all | bytes 2359296 | tf_op jit(solution)/shard_map/all_to_all | solution.py:64
  118.8 0.4 update_last.1
  119.2 19.2 %all_to_all.32.strips = bf16[16,16,384]{2,1,0:T(8,128)(2,1)S(1)} all-to-all(bf16[16,16,384]{2,1,0:T(8,128)(2,1)S(1)} %get-tuple-element.101), channel_id=1, replica_groups=mesh['replica'=16,'fsdp'=16] {'replica'}, dimensions={0} | all-to-all | bytes 393216 | tf_op jit(solution)/shard_map/all_to_all | solution.py:400
  138.5 0.7 strip_sum.1
  139.2 4.0 %all-to-all-start.5 = ((bf16[16,16,384]{2,1,0:T(8,128)(2,1)}), bf16[16,16,384]{2,1,0:T(8,128)(2,1)S(1)}, u32[]{:S(2)}, u32[]{:S(2)}) async-start(bf16[16,16,384]{2,1,0:T(8,128)(2,1)} %strip_sum.1), calls=%async_computation.5 | async-start | bytes 393216 | tf_op jit(solution)/shard_map/all_to_all | solution.py:402
  143.2 2.9 %collective-permute-start.9 = (f32[48,1536]{1,0:T(8,128)S(1)}, f32[48,1536]{1,0:T(8,128)S(1)}, u32[]{:S(2)}, u32[]{:S(2)}) collective-permute-start(f32[48,1536]{1,0:T(8,128)S(1)} %get-tuple-element.105.own), channel_id=1, source_target_pairs={{0,1},{1,0},{2,3},{3,2},{4,5},{5,4},{6,7},{7,6},{8,9},{9,8},{10,11... | collective-permute-start | bytes 884744 | tf_op jit(solution)/shard_map/ppermute | solution.py:59
  146.1 0.1 collective-permute-start.8
  146.2 6.7 %all-to-all-done.5.own = bf16[16,16,384]{2,1,0:T(8,128)(2,1)S(1)} async-done(((bf16[16,16,384]{2,1,0:T(8,128)(2,1)}), bf16[16,16,384]{2,1,0:T(8,128)(2,1)S(1)}, u32[]{:S(2)}, u32[]{:S(2)}) %all-to-all-start.5) | async-done | bytes 196640 | tf_op jit(solution)/shard_map/all_to_all | solution.py:402
  152.9 4.0 %collective-permute-start.7 = (bf16[16,16,384]{2,1,0:T(8,128)(2,1)S(1)}, bf16[16,16,384]{2,1,0:T(8,128)(2,1)S(1)}, u32[]{:S(2)}, u32[]{:S(2)}) collective-permute-start(bf16[16,16,384]{2,1,0:T(8,128)(2,1)S(1)} %all-to-all-done.5.own), channel_id=1, source_target_pairs={{0,1},{1,0},{2,3},{3,2},{4,5},{5,4},{6,7},{7,6},{8,9},{9,8},{10,11... | collective-permute-start | bytes 589832 | tf_op jit(solution)/shard_map/ppermute | solution.py:59
  156.9 0.7 unpair.3
  157.6 0.7 unpair.2
  158.4 0.9 outer.1
  (51 shorter events, 0.2 us)
Async XLA Ops:
  0.6 4.7 %collective-permute-start = (f32[24,3072]{1,0:T(8,128)}, f32[24,3072]{1,0:T(8,128)S(1)}, u32[]{:S(2)}, u32[]{:S(2)}) collective-permute-start(f32[24,3072]{1,0:T(8,128)} %params.1), channel_id=1, source_target_pairs={{0,1},{1,0},{2,3},{3,2},{4,5},{5,4},{6,7},{7,6},{8,9},{9,8},{10,11... | collective-permute-start | bytes 884744 | tf_op jit(solution)/shard_map/ppermute | solution.py:59
  5.4 1.0 copy-start
  7.5 4.6 %copy-start.22 = (s32[2,512]{1,0:T(2,128)S(1)}, s32[2,512]{1,0:T(2,128)}, u32[]{:S(2)}) copy-start(s32[2,512]{1,0:T(2,128)} %param.15) | copy-start | bytes 12292
  7.5 4.6 %copy-start.20 = (bf16[2,512,64]{1,2,0:T(8,128)(2,1)S(1)}, bf16[2,512,64]{1,2,0:T(8,128)(2,1)}, u32[]{:S(2)}) copy-start(bf16[2,512,64]{1,2,0:T(8,128)(2,1)} %param.14) | copy-start | bytes 393220
  7.5 4.6 %copy-start.21 = (bf16[2,512,64]{1,2,0:T(8,128)(2,1)S(1)}, bf16[2,512,64]{1,2,0:T(8,128)(2,1)}, u32[]{:S(2)}) copy-start(bf16[2,512,64]{1,2,0:T(8,128)(2,1)} %param.13) | copy-start | bytes 393220
  7.5 20.5 %all-to-all-start = ((bf16[8,48,1536]{2,1,0:T(8,128)(2,1)}), bf16[8,48,1536]{2,1,0:T(8,128)(2,1)S(1)}, u32[]{:S(2)}, u32[]{:S(2)}) async-start(bf16[8,48,1536]{2,1,0:T(8,128)(2,1)} %get-tuple-element.55), calls=%async_computation | async-start | bytes 2359296 | tf_op jit(solution)/shard_map/all_to_all | solution.py:64
  28.0 4.5 %collective-permute-start.1 = (bf16[384,1536]{1,0:T(8,128)(2,1)S(1)}, bf16[384,1536]{1,0:T(8,128)(2,1)S(1)}, u32[]{:S(2)}, u32[]{:S(2)}) collective-permute-start(bf16[384,1536]{1,0:T(8,128)(2,1)S(1)} %bitcast.47), channel_id=1, source_target_pairs={{0,1},{1,0},{2,3},{3,2},{4,5},{5,4},{6,7},{7,6},{8,9},{9,8},{10,11... | collective-permute-start | bytes 3538952 | tf_op jit(solution)/shard_map/ppermute | solution.py:59
  30.5 4.4 %copy-start.14 = (f32[1,1536]{1,0:T(1,128)}, f32[1,1536]{1,0:T(1,128)S(1)}, u32[]{:S(2)}) copy-start(f32[1,1536]{1,0:T(1,128)S(1)} %get-tuple-element.110.factor) | copy-start | bytes 18436
  30.5 6.2 %copy-start.11 = (f32[1,1536]{1,0:T(1,128)}, f32[1,1536]{1,0:T(1,128)S(1)}, u32[]{:S(2)}) copy-start(f32[1,1536]{1,0:T(1,128)S(1)} %get-tuple-element.111.factor) | copy-start | bytes 18436
  30.7 3.8 %copy-start.16 = (bf16[16,1536]{1,0:T(8,128)(2,1)}, bf16[16,1536]{1,0:T(8,128)(2,1)S(1)}, u32[]{:S(2)}) copy-start(bf16[16,1536]{1,0:T(8,128)(2,1)S(1)} %get-tuple-element.133.shift) | copy-start | bytes 147460
  30.7 3.8 %copy-start.18 = (bf16[16,1536]{1,0:T(8,128)(2,1)}, bf16[16,1536]{1,0:T(8,128)(2,1)S(1)}, u32[]{:S(2)}) copy-start(bf16[16,1536]{1,0:T(8,128)(2,1)S(1)} %get-tuple-element.132.shift) | copy-start | bytes 147460
  36.6 2.9 %collective-permute-start.2 = (bf16[384,1536]{1,0:T(8,128)(2,1)S(1)}, bf16[384,1536]{1,0:T(8,128)(2,1)S(1)}, u32[]{:S(2)}, u32[]{:S(2)}) collective-permute-start(bf16[384,1536]{1,0:T(8,128)(2,1)S(1)} %backward.4), channel_id=1, source_target_pairs={{0,1},{1,0},{2,3},{3,2},{4,5},{5,4},{6,7},{7,6},{8,9},{9,8},{10,11... | collective-permute-start | bytes 3538952 | tf_op jit(solution)/shard_map/ppermute | solution.py:59
  40.9 3.7 %copy-start.6 = (f32[1,24,3072]{2,1,0:T(8,128)S(1)}, f32[1,24,3072]{2,1,0:T(8,128)}, u32[]{:S(2)}) copy-start(f32[1,24,3072]{2,1,0:T(8,128)} %param.11) | copy-start | bytes 884740
  40.9 3.9 %copy-start.7 = (f32[1,24,3072]{2,1,0:T(8,128)S(1)}, f32[1,24,3072]{2,1,0:T(8,128)}, u32[]{:S(2)}) copy-start(f32[1,24,3072]{2,1,0:T(8,128)} %param.12) | copy-start | bytes 884740
  40.9 20.8 %all-to-all-start.1 = ((bf16[8,48,1536]{2,1,0:T(8,128)(2,1)}), bf16[8,48,1536]{2,1,0:T(8,128)(2,1)S(1)}, u32[]{:S(2)}, u32[]{:S(2)}) async-start(bf16[8,48,1536]{2,1,0:T(8,128)(2,1)} %bitcast.17), calls=%async_computation.1 | async-start | bytes 2359296 | tf_op jit(solution)/shard_map/all_to_all | solution.py:64
  44.6 1.7 %collective-permute-start.3 = (f32[24,3072]{1,0:T(8,128)S(1)}, f32[24,3072]{1,0:T(8,128)S(1)}, u32[]{:S(2)}, u32[]{:S(2)}) collective-permute-start(f32[24,3072]{1,0:T(8,128)S(1)} %bitcast.57), channel_id=1, source_target_pairs={{0,1},{1,0},{2,3},{3,2},{4,5},{5,4},{6,7},{7,6},{8,9},{9,8},{10,11... | collective-permute-start | bytes 884744 | tf_op jit(solution)/shard_map/ppermute | solution.py:59
  44.8 1.9 %collective-permute-start.4 = (f32[24,3072]{1,0:T(8,128)S(1)}, f32[24,3072]{1,0:T(8,128)S(1)}, u32[]{:S(2)}, u32[]{:S(2)}) collective-permute-start(f32[24,3072]{1,0:T(8,128)S(1)} %bitcast.59), channel_id=1, source_target_pairs={{0,1},{1,0},{2,3},{3,2},{4,5},{5,4},{6,7},{7,6},{8,9},{9,8},{10,11... | collective-permute-start | bytes 884744 | tf_op jit(solution)/shard_map/ppermute | solution.py:59
  62.1 19.2 %copy-start.2 = (f32[48,1536]{1,0:T(8,128)}, f32[48,1536]{1,0:T(8,128)S(1)}, u32[]{:S(2)}) copy-start(f32[48,1536]{1,0:T(8,128)S(1)} %get-tuple-element.100.square) | copy-start | bytes 884740
  62.1 19.2 %copy-start.4 = (f32[48,1536]{1,0:T(8,128)}, f32[48,1536]{1,0:T(8,128)S(1)}, u32[]{:S(2)}) copy-start(f32[48,1536]{1,0:T(8,128)S(1)} %get-tuple-element.98.params) | copy-start | bytes 884740
  81.3 10.7 %collective-permute-start.5 = (bf16[384,1536]{1,0:T(8,128)(2,1)S(1)}, bf16[384,1536]{1,0:T(8,128)(2,1)S(1)}, u32[]{:S(2)}, u32[]{:S(2)}) collective-permute-start(bf16[384,1536]{1,0:T(8,128)(2,1)S(1)} %bitcast.50), channel_id=1, source_target_pairs={{0,1},{1,0},{2,3},{3,2},{4,5},{5,4},{6,7},{7,6},{8,9},{9,8},{10,11... | collective-permute-start | bytes 3538952 | tf_op jit(solution)/shard_map/ppermute | solution.py:59
  86.7 1.0 copy-start.9
  87.6 0.9 copy-start.10
  88.5 0.7 copy-start.12
  89.2 0.8 copy-start.19
  90.0 2.0 %copy-start.15 = (f32[1,1536]{1,0:T(1,128)S(1)}, f32[1,1536]{1,0:T(1,128)}, u32[]{:S(2)}) copy-start(f32[1,1536]{1,0:T(1,128)} %copy-done.14) | copy-start | bytes 18436
  90.0 2.0 %copy-start.17 = (bf16[16,1536]{1,0:T(8,128)(2,1)S(1)}, bf16[16,1536]{1,0:T(8,128)(2,1)}, u32[]{:S(2)}) copy-start(bf16[16,1536]{1,0:T(8,128)(2,1)} %copy-done.16) | copy-start | bytes 147460
  94.4 1.9 %copy-start.13 = (f32[1,1536]{1,0:T(1,128)S(1)}, f32[1,1536]{1,0:T(1,128)}, u32[]{:S(2)}) copy-start(f32[1,1536]{1,0:T(1,128)} %copy-done.11) | copy-start | bytes 18436
  96.2 2.9 %collective-permute-start.6 = (bf16[384,1536]{1,0:T(8,128)(2,1)S(1)}, bf16[384,1536]{1,0:T(8,128)(2,1)S(1)}, u32[]{:S(2)}, u32[]{:S(2)}) collective-permute-start(bf16[384,1536]{1,0:T(8,128)(2,1)S(1)} %backward.6), channel_id=1, source_target_pairs={{0,1},{1,0},{2,3},{3,2},{4,5},{5,4},{6,7},{7,6},{8,9},{9,8},{10,11... | collective-permute-start | bytes 3538952 | tf_op jit(solution)/shard_map/ppermute | solution.py:59
  99.4 19.4 %copy-start.3 = (f32[48,1536]{1,0:T(8,128)S(1)}, f32[48,1536]{1,0:T(8,128)}, u32[]{:S(2)}) copy-start(f32[48,1536]{1,0:T(8,128)} %copy-done.2) | copy-start | bytes 884740
  99.4 19.4 %copy-start.5 = (f32[48,1536]{1,0:T(8,128)S(1)}, f32[48,1536]{1,0:T(8,128)}, u32[]{:S(2)}) copy-start(f32[48,1536]{1,0:T(8,128)} %copy-done.4) | copy-start | bytes 884740
  139.2 19.2 %copy-start.1 = (f32[24,3072]{1,0:T(8,128)S(1)}, f32[24,3072]{1,0:T(8,128)}, u32[]{:S(2)}) copy-start(f32[24,3072]{1,0:T(8,128)} %params.1) | copy-start | bytes 884740
  139.2 19.2 %copy-start.8 = (f32[24,3072]{1,0:T(8,128)S(1)}, f32[24,3072]{1,0:T(8,128)}, u32[]{:S(2)}) copy-start(f32[24,3072]{1,0:T(8,128)} %momentum.1) | copy-start | bytes 884740
  139.2 13.7 %all-to-all-start.5 = ((bf16[16,16,384]{2,1,0:T(8,128)(2,1)}), bf16[16,16,384]{2,1,0:T(8,128)(2,1)S(1)}, u32[]{:S(2)}, u32[]{:S(2)}) async-start(bf16[16,16,384]{2,1,0:T(8,128)(2,1)} %strip_sum.1), calls=%async_computation.5 | async-start | bytes 393216 | tf_op jit(solution)/shard_map/all_to_all | solution.py:402
  143.2 13.7 %collective-permute-start.9 = (f32[48,1536]{1,0:T(8,128)S(1)}, f32[48,1536]{1,0:T(8,128)S(1)}, u32[]{:S(2)}, u32[]{:S(2)}) collective-permute-start(f32[48,1536]{1,0:T(8,128)S(1)} %get-tuple-element.105.own), channel_id=1, source_target_pairs={{0,1},{1,0},{2,3},{3,2},{4,5},{5,4},{6,7},{7,6},{8,9},{9,8},{10,11... | collective-permute-start | bytes 884744 | tf_op jit(solution)/shard_map/ppermute | solution.py:59
  146.1 11.5 %collective-permute-start.8 = (f32[48,1536]{1,0:T(8,128)S(1)}, f32[48,1536]{1,0:T(8,128)S(1)}, u32[]{:S(2)}, u32[]{:S(2)}) collective-permute-start(f32[48,1536]{1,0:T(8,128)S(1)} %get-tuple-element.104.own), channel_id=1, source_target_pairs={{0,1},{1,0},{2,3},{3,2},{4,5},{5,4},{6,7},{7,6},{8,9},{9,8},{10,11... | collective-permute-start | bytes 884744 | tf_op jit(solution)/shard_map/ppermute | solution.py:59
  152.9 5.5 %collective-permute-start.7 = (bf16[16,16,384]{2,1,0:T(8,128)(2,1)S(1)}, bf16[16,16,384]{2,1,0:T(8,128)(2,1)S(1)}, u32[]{:S(2)}, u32[]{:S(2)}) collective-permute-start(bf16[16,16,384]{2,1,0:T(8,128)(2,1)S(1)} %all-to-all-done.5.own), channel_id=1, source_target_pairs={{0,1},{1,0},{2,3},{3,2},{4,5},{5,4},{6,7},{7,6},{8,9},{9,8},{10,11... | collective-permute-start | bytes 589832 | tf_op jit(solution)/shard_map/ppermute | solution.py:59

commit v2 on v1

--- a/solution.py
+++ b/solution.py
@@ -35,13 +35,10 @@
 TRANSPOSED = (((1,), (1,)), ((), ()))
 
 
-def local_call(kernel, name, args, outs, scratch=(), core=None, flops=0, hbm_outs=False):
+def local_call(kernel, name, args, outs, scratch=(), scalars=(), flops=0, hbm_outs=False):
     place = pltpu.VMEM if not hbm_outs else jax.ShapeDtypeStruct
-    specs = [VMEM] * len(args)
-    values = [pltpu.with_memory_space_constraint(a, pltpu.VMEM) for a in args]
-    if core is not None:
-        specs = [SMEM] + specs
-        values = [core] + values
+    specs = [SMEM] * len(scalars) + [VMEM] * len(args)
+    values = [*scalars, *(pltpu.with_memory_space_constraint(a, pltpu.VMEM) for a in args)]
     moved = sum(math.prod(o[0]) * 4 for o in outs) + sum(a.size * a.dtype.itemsize for a in args)
     return pl.pallas_call(
         kernel,
@@ -64,7 +61,15 @@
     return lax.all_to_all(blocks, "fsdp", 0, 0, axis_index_groups=groups)
 
 
-def pair_kernel(core, own, got, pair, *copies):
+def hold_kernel(values, held):
+    held[...] = values[...]
+
+
+def hold(values):
+    return local_call(hold_kernel, "hold", (values,), [(values.shape, values.dtype)])[0]
+
+
+def pair_halves(core, own, got, pair):
     rows = own.shape[0]
     half = own.shape[1] // CORES
 
@@ -78,20 +83,20 @@
         pair[0:rows] = got[:, half:]
         pair[rows:] = own[:, half:]
 
-    for copy in copies:
-        block = pair[...].astype(BF16)
-        for chip in range(copy.shape[0]):
-            copy[chip] = block
-
-
-def to_pair(values, core, width, copies=()):
-    rows, columns = values.shape
-    shape = (rows * CORES, columns // CORES)
-    outs = [(shape, F32)] + [((n,) + shape, BF16) for n in copies]
-    return local_call(pair_kernel, "pair", (values, core_swap(values, width)), outs, core=core)
-
-
-def unpair_kernel(core, own, got, out):
+
+def start_kernel(core, own, got, pair, copies):
+    pair_halves(core, own, got, pair)
+    block = pair[...].astype(BF16)
+    for chip in range(copies.shape[0]):
+        copies[chip] = block
+
+
+def moments_kernel(core, mean, mean_got, square, square_got, mean_pair, square_pair):
+    pair_halves(core, mean, mean_got, mean_pair)
+    pair_halves(core, square, square_got, square_pair)
+
+
+def unpair_halves(core, own, got, out):
     rows = out.shape[0]
     half = out.shape[1] // CORES
 
@@ -106,11 +111,9 @@
         out[:, half:] = own[rows:]
 
 
-def from_pair(values, core, width):
-    rows, columns = values.shape
-    outs = [((rows // CORES, columns * CORES), F32)]
-    args = (values, core_swap(values, width))
-    return local_call(unpair_kernel, "unpair", args, outs, core=core, hbm_outs=True)[0]
+def unpair_kernel(core, mean, mean_got, square, square_got, new_mean, new_square):
+    unpair_halves(core, mean, mean_got, new_mean)
+    unpair_halves(core, square, square_got, new_square)
 
 
 def forward_kernel(tokens, embed, weights, factor, shift, hid, mod, slope, out, square, bias, pre_buf, in_buf):
@@ -222,18 +225,73 @@
     return local_call(make_backward_kernel(model_width), "backward", args, outs, scratch, flops=flops)[0]
 
 
-def prepare_tokens(latent_rows, noise_rows, levels, channels, time_width):
-    half_width = time_width // 2
-    noise_level = (levels.astype(F32) + 0.5) / LEVELS
-    frequencies = jnp.exp(-math.log(10000.0) * jnp.arange(half_width, dtype=F32) / half_width)
-    angles = (1000.0 * noise_level)[:, None] * frequencies[None, :]
-    embed = jnp.concatenate([jnp.cos(angles), jnp.sin(angles)], axis=-1).astype(BF16)
-    latent_f = latent_rows.astype(F32)
-    noise_f = noise_rows.astype(F32)
-    noised = ((1.0 - noise_level)[:, None] * latent_f + noise_level[:, None] * noise_f).astype(BF16)
-    noised = noised * BF16(1.0 / math.sqrt(channels))
-    embed = embed * BF16(1.0 / math.sqrt(time_width))
-    return noised, embed, noised.T, embed.T, noise_f - latent_f
+def prepare_kernel(core, fragment, latents, noise, levels, modulation, *outs):
+    steps, channels, tokens = latents.shape
+    half_width = outs[1].shape[1] // 2
+    per_step = 5
+    for step in range(steps):
+        token_rows, embed_rows, token_cols, embed_cols, target = outs[per_step * step : per_step * (step + 1)]
+        level = (levels[step : step + 1, :].astype(F32) + 0.5) / LEVELS
+        latent = latents[step].astype(F32)
+        draw = noise[step].astype(F32)
+        noised = ((1.0 - level) * latent + level * draw).astype(BF16).astype(F32)
+        noised = noised * (1.0 / math.sqrt(channels))
+        token_cols[...] = noised.astype(BF16)
+        token_rows[...] = noised.T.astype(BF16)
+        target[...] = (draw - latent).T
+        order = lax.broadcasted_iota(jnp.int32, (half_width, tokens), 0).astype(F32)
+        angles = (1000.0 * level) * jnp.exp(-math.log(10000.0) * order / half_width)
+        root = 1.0 / math.sqrt(2 * half_width)
+        for part, wave in enumerate((jnp.cos(angles), jnp.sin(angles))):
+            wave = wave.astype(BF16).astype(F32) * root
+            place = pl.ds(part * half_width, half_width)
+            embed_cols[place, :] = wave.astype(BF16)
+            embed_rows[:, place] = wave.T.astype(BF16)
+    rows = modulation[fragment[0]]
+    half = rows.shape[1] // CORES
+    for side in range(CORES):
+        factor, shift, terms = outs[per_step * steps + 3 * side : per_step * steps + 3 * (side + 1)]
+
+        def place_half(first):
+            here = rows[:, first : first + half]
+            factor[...] = 1.0 + here[1:2]
+            shift[...] = here[0:1]
+            wide = jnp.broadcast_to(here[0:1], terms.shape)
+            high = wide.astype(BF16).astype(F32)
+            index = lax.broadcasted_iota(jnp.int32, terms.shape, 0)
+            split = jnp.where(index == 0, high, jnp.where(index == 1, wide - high, 0.0))
+            terms[...] = split.astype(BF16)
+
+        @pl.when(core[0] == side)
+        def _():
+            place_half(0)
+
+        @pl.when(core[0] != side)
+        def _():
+            place_half(half)
+
+
+def prepare(core, fragment, latents, noise_draw, timesteps, modulation, time_width):
+    steps, tokens, channels = latents.shape
+    half = modulation.shape[2] // CORES
+    outs = [
+        ((tokens, channels), BF16),
+        ((tokens, time_width), BF16),
+        ((channels, tokens), BF16),
+        ((time_width, tokens), BF16),
+        ((tokens, channels), F32),
+    ] * steps + [((1, half), F32), ((1, half), F32), ((16, half), BF16)] * CORES
+    args = (latents.transpose(0, 2, 1), noise_draw.transpose(0, 2, 1), timesteps, modulation)
+    results = local_call(
+        prepare_kernel, "prepare", args, outs, scalars=(core, fragment), flops=2**32
+    )
+    return [results[5 * s : 5 * s + 5] for s in range(steps)], [
+        results[5 * steps + 3 * c : 5 * steps + 3 * c + 3] for c in range(CORES)
+    ]
+
+
+def pair_sum_kernel(mine, got, out):
+    out[...] = (mine[...].astype(F32) + got[...].astype(F32)).astype(BF16)
 
 
 def step_kernel(blocks, params, mean, square, new_mean, new_square, new_params, copies):
@@ -335,26 +393,35 @@
     time_width = rows * width - 2 * channels
     total_rows = latents.shape[1] * width
 
-    start, copies = to_pair(outer_params, core_arg, width, (chips,))
+    pair_shape = (rows * CORES, half)
+    start, copies = local_call(
+        start_kernel,
+        "start",
+        (hold(outer_params), core_swap(outer_params, width)),
+        [(pair_shape, F32), ((chips,) + pair_shape, BF16)],
+        scalars=(core_arg,),
+    )
     gathered = chip_exchange(copies, width)
 
-    mod_rows = lax.dynamic_index_in_dim(modulation, fragment[0], 0, keepdims=False)
-    mods = []
-    for side in (core, 1 - core):
-        rows_here = lax.dynamic_slice_in_dim(mod_rows, side * half, half, 1)
-        shift = rows_here[0:1]
-        high = shift.astype(BF16)
-        low = (shift - high.astype(F32)).astype(BF16)
-        terms = jnp.concatenate([high, low, jnp.zeros((14, half), BF16)], axis=0)
-        mods.append((1.0 + rows_here[1:2], shift, terms))
-    prepared = [
-        prepare_tokens(latents[s], noise_draw[s], timesteps[s], channels, time_width)
-        for s in range(STEPS)
-    ]
+    prepared, mods = prepare(
+        core_arg, fragment, latents, noise_draw, timesteps, modulation, time_width
+    )
     params = start
-    mean = to_pair(inner_mean[0], core_arg, width)[0]
-    square = to_pair(inner_square[0], core_arg, width)[0]
-    pair_shape = start.shape
+    mean, square = local_call(
+        moments_kernel,
+        "moments",
+        (
+            inner_mean[0],
+            core_swap(inner_mean[0], width),
+            inner_square[0],
+            core_swap(inner_square[0], width),
+        ),
+        [(pair_shape, F32)] * 2,
+        scalars=(core_arg,),
+    )
+    gathered, prepared, mods, mean, square = lax.optimization_barrier(
+        (gathered, prepared, mods, mean, square)
+    )
 
     for step in range(STEPS):
         tokens, embed, tokens_t, embed_t, target = prepared[step]
@@ -382,7 +449,9 @@
         grad_mine = backward(
             state[:3], weights, mods[0][0], mods[0][1], tokens_t, embed_t, head, model_width
         )
-        pair_sum = (grad_mine.astype(F32) + received.astype(F32)).astype(BF16)
+        pair_sum = local_call(
+            pair_sum_kernel, "pair_sum", (grad_mine, received), [(weights.shape, BF16)]
+        )[0]
         blocks = chip_exchange(pair_sum.reshape((chips,) + pair_shape), width)
         moments = [(pair_shape, F32)] * 2
         if step + 1 < STEPS:
@@ -398,17 +467,24 @@
                 last_kernel, "update_last", (blocks, params, mean, square, start), outs
             )
     strips = lax.all_to_all(strips, "replica", 0, 0)
+    new_mean, new_square = local_call(
+        unpair_kernel,
+        "unpair",
+        (mean, core_swap(mean, width), square, core_swap(square, width)),
+        [(outer_params.shape, F32)] * 2,
+        scalars=(core_arg,),
+        hbm_outs=True,
+    )
+    strips, new_mean, new_square = lax.optimization_barrier((strips, new_mean, new_square))
     strips = local_call(strip_sum_kernel, "strip_sum", (strips,), [(strips.shape, BF16)])[0]
     strips = lax.all_to_all(strips, "replica", 0, 0)
-    new_mean = from_pair(mean, core_arg, width)
-    new_square = from_pair(square, core_arg, width)
     new_params, new_momentum = local_call(
         make_outer_kernel(replicas),
         "outer",
         (strips, core_swap(strips, width), outer_params, outer_momentum),
         [(outer_params.shape, F32)] * 2,
         [pltpu.VMEM(pair_shape, F32)] * 2,
-        core=core_arg,
+        scalars=(core_arg,),
         hbm_outs=True,
     )
     return (new_params, new_momentum, new_mean[None], new_square[None])

time: 160 us -> 150 us (0.938)
  waiting for transfers between devices: 38.3 us -> 18.9 us
  blocking collectives: 57.8 us -> 70.4 us
  other arithmetic: 7.44 us -> 0 us
  starting transfers between devices: 26 us -> 28.5 us
  Pallas kernels: 20.6 us -> 22.5 us
    all_to_all x2 -> x1, waiting for transfers between devices: 26.4 us -> 7.83 us  [chip_exchange(): return lax.all_to_all(blocks, 'fsdp', 0, 0, axis_index_groups=groups)]
    all_to_all x2 -> x3, blocking collectives: 38.5 us -> 57 us  [chip_exchange(): return lax.all_to_all(blocks, 'fsdp', 0, 0, axis_index_groups=groups)]
    all_to_all x1, starting transfers between devices: 3.99 us -> 10 us  [on_device(): strips = lax.all_to_all(strips, 'replica', 0, 0)]
    all_to_all x1, blocking collectives: 19.2 us -> 13.4 us  [on_device(): strips = lax.all_to_all(strips, 'replica', 0, 0)]
    all_to_all x2 -> x1, starting transfers between devices: 7.63 us -> 3.95 us  [chip_exchange(): return lax.all_to_all(blocks, 'fsdp', 0, 0, axis_index_groups=groups)]
    unnamed x46 -> x48, local copies, waits for them, and re-layouts: 4.38 us -> 7.51 us
    another operation x1 -> x0, other arithmetic: 2.9 us -> none
    convert_element_type x4 -> x0, other arithmetic: 2.61 us -> none  [the longest x2 1.63 us: on_device(): pair_sum = (grad_mine.astype(F32) + received.astype(F32)).astype(BF16)]
  transfers between devices with their start and end apart: 13 -> 12, of which waited for: 8 -> 9; matrix products, arithmetic and copies ran while one was open for 6% -> 0% of each run, Pallas kernels for 6% -> 7%
where the time goes in v2:
time: 150 us; the launch traced here: 149 us
  blocking collectives  70.4 us (47%)
  starting transfers between devices  28.5 us (19%)
  Pallas kernels  22.5 us (15%)
  waiting for transfers between devices  18.9 us (13%)
  local copies, waits for them, and re-layouts  7.51 us (5%)
  between operations  1.56 us (1%)
    all_to_all x3, blocking collectives, chip_exchange(): return lax.all_to_all(blocks, 'fsdp', 0, 0, axis_index_groups=groups)  57 us
    pallas_call x21, Pallas kernels, local_call(): pl.pallas_call(kernel, in_specs=specs, out_specs=[VMEM] * len(outs), out_...  22.5 us
    ppermute x10, starting transfers between devices, core_swap(): return lax.ppermute(values, 'fsdp', [(i, i ^ 1) for i in range(width)])  14.6 us
    all_to_all x1, blocking collectives, on_device(): strips = lax.all_to_all(strips, 'replica', 0, 0)  13.4 us
    all_to_all x1, starting transfers between devices, on_device(): strips = lax.all_to_all(strips, 'replica', 0, 0)  10 us
    all_to_all x1, waiting for transfers between devices, chip_exchange(): return lax.all_to_all(blocks, 'fsdp', 0, 0, axis_index_groups=groups)  7.83 us
    unnamed x48, local copies, waits for them, and re-layouts  7.51 us
    ppermute x10, waiting for transfers between devices, core_swap(): return lax.ppermute(values, 'fsdp', [(i, i ^ 1) for i in range(width)])  5.6 us
  transfers between devices with their start and end apart: 12, of which 9 were waited for; matrix products, arithmetic and copies ran while one was open for 0% of the time, Pallas kernels for 7%

profile of v2, /device:TPU:1, one launch (start us, length us, event | category | flops | bytes accessed | tf_op | source)
XLA Modules:
  0.0 149.4 jit_solution(5667642194905275466)
XLA Ops:
  0.6 3.3 %collective-permute-start = (f32[24,3072]{1,0:T(8,128)}, f32[24,3072]{1,0:T(8,128)S(1)}, u32[]{:S(2)}, u32[]{:S(2)}) collective-permute-start(f32[24,3072]{1,0:T(8,128)} %params.1), channel_id=1, source_target_pairs={{0,1},{1,0},{2,3},{3,2},{4,5},{5,4},{6,7},{7,6},{8,9},{9,8},{10,11... | collective-permute-start | bytes 884744 | tf_op jit(solution)/shard_map/ppermute | solution.py:56
  4.0 1.0 copy-done
  5.0 0.4 collective-permute-done.got
  5.4 1.2 start.1
  6.6 0.0 copy-start.11
  6.6 0.0 copy-start.12
  6.6 4.0 %all-to-all-start = ((bf16[8,48,1536]{2,1,0:T(8,128)(2,1)}), bf16[8,48,1536]{2,1,0:T(8,128)(2,1)S(1)}, u32[]{:S(2)}, u32[]{:S(2)}) async-start(bf16[8,48,1536]{2,1,0:T(8,128)(2,1)} %get-tuple-element.97), calls=%async_computation | async-start | bytes 2359296 | tf_op jit(solution)/shard_map/all_to_all | solution.py:61
  10.5 0.7 collective-permute-start.1
  11.3 0.1 collective-permute-start.2
  12.1 2.3 %prepare.1 = (bf16[512,64]{1,0:T(8,128)(2,1)S(1)}, bf16[512,256]{1,0:T(8,128)(2,1)S(1)}, bf16[64,512]{1,0:T(8,128)(2,1)S(1)}, bf16[256,512]{1,0:T(8,128)(2,1)S(1...) custom-call(s32[1]{0:T(128)} %bitcast.core, ...), custom_call_target="tpu_custom_call" | custom-call | flops 4294967296 | bytes 3739648 | tf_op jit(solution)/shard_map/prepare/pallas_call | solution.py:43
  14.4 0.0 copy-start.5
  14.4 0.7 copy-done.5
  15.1 0.7 copy-done.7
  15.8 0.7 copy-done.13
  16.5 0.7 copy-done.15
  17.3 0.6 copy-done.17
  17.9 0.7 copy-done.19
  18.6 0.6 copy-done.21
  19.2 0.0 collective-permute-done.1.mean_got
  19.2 0.0 collective-permute-done.2.square_got
  19.2 0.1 moments.1
  19.3 7.8 %all-to-all-done = bf16[8,48,1536]{2,1,0:T(8,128)(2,1)S(1)} async-done(((bf16[8,48,1536]{2,1,0:T(8,128)(2,1)}), bf16[8,48,1536]{2,1,0:T(8,128)(2,1)S(1)}, u32[]{:S(2)}, u32[]{:S(2)}) %all-to-all-start) | async-done | bytes 1179680 | tf_op jit(solution)/shard_map/all_to_all | solution.py:61
  27.1 1.5 %collective-permute-start.3 = (bf16[384,1536]{1,0:T(8,128)(2,1)S(1)}, bf16[384,1536]{1,0:T(8,128)(2,1)S(1)}, u32[]{:S(2)}, u32[]{:S(2)}) collective-permute-start(bf16[384,1536]{1,0:T(8,128)(2,1)S(1)} %bitcast.13), channel_id=1, source_target_pairs={{0,1},{1,0},{2,3},{3,2},{4,5},{5,4},{6,7},{7,6},{8,9},{9,8},{10,11... | collective-permute-start | bytes 3538952 | tf_op jit(solution)/shard_map/ppermute | solution.py:56
  28.6 0.0 copy-done.20
  28.6 0.9 copy-done.16
  29.6 0.8 copy-done.22
  30.4 1.9 %forward.4 = (bf16[512,1536]{1,0:T(8,128)(2,1)S(1)}, bf16[512,1536]{1,0:T(8,128)(2,1)S(1)}, bf16[512,1536]{1,0:T(8,128)(2,1)S(1)}, f32[512,64]{1,0:T(8,128)S(1)}...) custom-call(bf16[512,64]{1,0:T(8,128)(2,1)S(1)} %copy-done.20, bf16[512,256]{1,0:T(8,128)(2,1)S(1)} %copy-done.16, ...), custom_call_target="tpu_custom_call" | custom-call | flops 603979776 | bytes 11397120 | tf_op jit(solution)/shard_map/forward/pallas_call | solution.py:43
  32.3 0.0 copy-start.8
  32.3 0.0 collective-permute-done.3.weights
  32.3 1.9 %forward.5 = (bf16[512,1536]{1,0:T(8,128)(2,1)S(1)}, bf16[512,1536]{1,0:T(8,128)(2,1)S(1)}, bf16[512,1536]{1,0:T(8,128)(2,1)S(1)}, f32[512,64]{1,0:T(8,128)S(1)}...) custom-call(bf16[512,64]{1,0:T(8,128)(2,1)S(1)} %copy-done.20, bf16[512,256]{1,0:T(8,128)(2,1)S(1)} %copy-done.16, ...), custom_call_target="tpu_custom_call" | custom-call | flops 603979776 | bytes 11397120 | tf_op jit(solution)/shard_map/forward/pallas_call | solution.py:43
  34.2 0.4 head.2
  34.7 1.6 %backward.4 = bf16[384,1536]{1,0:T(8,128)(2,1)S(1)} custom-call(bf16[512,1536]{1,0:T(8,128)(2,1)S(1)} %get-tuple-element.142.hid, bf16[512,1536]{1,0:T(8,128)(2,1)S(1)} %get-tuple-element.143.mod, bf16[512,1536]{1,0:T(8,128)(2,1)S(1)} %get-tuple-element.144.slope, bf16[384,1536]{1,0:T(8,128)(2,1)S(1)} %collective-permute-done.3.weights, ...), custom_call_target="tpu_custom_call" | custom-call | flops 704643072 | bytes 9023488 | tf_op jit(solution)/shard_map/backward/pallas_call | solution.py:43
  36.3 0.3 collective-permute-start.4
  36.6 1.6 %backward.5.mine = bf16[384,1536]{1,0:T(8,128)(2,1)S(1)} custom-call(bf16[512,1536]{1,0:T(8,128)(2,1)S(1)} %get-tuple-element.123.hid, bf16[512,1536]{1,0:T(8,128)(2,1)S(1)} %get-tuple-element.124.mod, bf16[512,1536]{1,0:T(8,128)(2,1)S(1)} %get-tuple-element.125.slope, bf16[384,1536]{1,0:T(8,128)(2,1)S(1)} %bitcast.15, ...), custom_call_target="tpu_custom_call" | custom-call | flops 704643072 | bytes 9023488 | tf_op jit(solution)/shard_map/backward/pallas_call | solution.py:43
  38.2 1.2 collective-permute-done.4.got
  39.4 0.3 pair_sum.2
  39.7 19.3 %all_to_all.30.blocks = bf16[8,48,1536]{2,1,0:T(8,128)(2,1)S(1)} all-to-all(bf16[8,48,1536]{2,1,0:T(8,128)(2,1)S(1)} %bitcast.11), channel_id=1, replica_groups={{0,2,4,6,8,10,12,14},{1,3,5,7,9,11,13,15},{16,18,20,22,24,26,28,30},{17..., dimensions={0} | all-to-all | bytes 2359296 | tf_op jit(solution)/shard_map/all_to_all | solution.py:61
  59.0 0.4 update.1
  59.5 0.0 copy-start.14
  59.5 18.5 %all_to_all.31 = bf16[8,48,1536]{2,1,0:T(8,128)(2,1)S(1)} all-to-all(bf16[8,48,1536]{2,1,0:T(8,128)(2,1)S(1)} %get-tuple-element.153), channel_id=1, replica_groups={{0,2,4,6,8,10,12,14},{1,3,5,7,9,11,13,15},{16,18,20,22,24,26,28,30},{17..., dimensions={0} | all-to-all | bytes 2359296 | tf_op jit(solution)/shard_map/all_to_all | solution.py:61
  78.0 2.3 %collective-permute-start.5 = (bf16[384,1536]{1,0:T(8,128)(2,1)S(1)}, bf16[384,1536]{1,0:T(8,128)(2,1)S(1)}, u32[]{:S(2)}, u32[]{:S(2)}) collective-permute-start(bf16[384,1536]{1,0:T(8,128)(2,1)S(1)} %bitcast.16), channel_id=1, source_target_pairs={{0,1},{1,0},{2,3},{3,2},{4,5},{5,4},{6,7},{7,6},{8,9},{9,8},{10,11... | collective-permute-start | bytes 3538952 | tf_op jit(solution)/shard_map/ppermute | solution.py:56
  80.3 1.9 %forward.6 = (bf16[512,1536]{1,0:T(8,128)(2,1)S(1)}, bf16[512,1536]{1,0:T(8,128)(2,1)S(1)}, bf16[512,1536]{1,0:T(8,128)(2,1)S(1)}, f32[512,64]{1,0:T(8,128)S(1)}...) custom-call(bf16[512,64]{1,0:T(8,128)(2,1)S(1)} %copy-done.18, bf16[512,256]{1,0:T(8,128)(2,1)S(1)} %copy-done.14, ...), custom_call_target="tpu_custom_call" | custom-call | flops 603979776 | bytes 11397120 | tf_op jit(solution)/shard_map/forward/pallas_call | solution.py:43
  82.3 0.0 copy-start.6
  82.3 0.5 collective-permute-done.5.weights
  82.8 1.9 %forward.7 = (bf16[512,1536]{1,0:T(8,128)(2,1)S(1)}, bf16[512,1536]{1,0:T(8,128)(2,1)S(1)}, bf16[512,1536]{1,0:T(8,128)(2,1)S(1)}, f32[512,64]{1,0:T(8,128)S(1)}...) custom-call(bf16[512,64]{1,0:T(8,128)(2,1)S(1)} %copy-done.18, bf16[512,256]{1,0:T(8,128)(2,1)S(1)} %copy-done.14, ...), custom_call_target="tpu_custom_call" | custom-call | flops 603979776 | bytes 11397120 | tf_op jit(solution)/shard_map/forward/pallas_call | solution.py:43
  84.7 0.4 head.3
  85.2 1.6 %backward.6 = bf16[384,1536]{1,0:T(8,128)(2,1)S(1)} custom-call(bf16[512,1536]{1,0:T(8,128)(2,1)S(1)} %get-tuple-element.170.hid, bf16[512,1536]{1,0:T(8,128)(2,1)S(1)} %get-tuple-element.171.mod, bf16[512,1536]{1,0:T(8,128)(2,1)S(1)} %get-tuple-element.172.slope, bf16[384,1536]{1,0:T(8,128)(2,1)S(1)} %collective-permute-done.5.weights, ...), custom_call_target="tpu_custom_call" | custom-call | flops 704643072 | bytes 9023488 | tf_op jit(solution)/shard_map/backward/pallas_call | solution.py:43
  86.8 0.5 collective-permute-start.6
  87.3 1.6 %backward.7.mine = bf16[384,1536]{1,0:T(8,128)(2,1)S(1)} custom-call(bf16[512,1536]{1,0:T(8,128)(2,1)S(1)} %get-tuple-element.154.hid, bf16[512,1536]{1,0:T(8,128)(2,1)S(1)} %get-tuple-element.155.mod, bf16[512,1536]{1,0:T(8,128)(2,1)S(1)} %get-tuple-element.156.slope, bf16[384,1536]{1,0:T(8,128)(2,1)S(1)} %bitcast.18, ...), custom_call_target="tpu_custom_call" | custom-call | flops 704643072 | bytes 9023488 | tf_op jit(solution)/shard_map/backward/pallas_call | solution.py:43
  88.9 0.9 collective-permute-done.6.got
  89.7 0.3 pair_sum.3
  90.0 19.2 %all_to_all.32.blocks = bf16[8,48,1536]{2,1,0:T(8,128)(2,1)S(1)} all-to-all(bf16[8,48,1536]{2,1,0:T(8,128)(2,1)S(1)} %bitcast.12), channel_id=1, replica_groups={{0,2,4,6,8,10,12,14},{1,3,5,7,9,11,13,15},{16,18,20,22,24,26,28,30},{17..., dimensions={0} | all-to-all | bytes 2359296 | tf_op jit(solution)/shard_map/all_to_all | solution.py:61
  109.3 1.1 update_last.1
  110.3 10.0 %all-to-all-start.4 = ((bf16[16,16,384]{2,1,0:T(8,128)(2,1)}), bf16[16,16,384]{2,1,0:T(8,128)(2,1)S(1)}, u32[]{:S(2)}, u32[]{:S(2)}) async-start(bf16[16,16,384]{2,1,0:T(8,128)(2,1)} %get-tuple-element.180), calls=%async_computation.4 | async-start | bytes 393216 | tf_op jit(solution)/shard_map/all_to_all | solution.py:469
  120.3 1.7 %collective-permute-start.7 = (f32[48,1536]{1,0:T(8,128)S(1)}, f32[48,1536]{1,0:T(8,128)S(1)}, u32[]{:S(2)}, u32[]{:S(2)}) collective-permute-start(f32[48,1536]{1,0:T(8,128)S(1)} %get-tuple-element.181.mean), channel_id=1, source_target_pairs={{0,1},{1,0},{2,3},{3,2},{4,5},{5,4},{6,7},{7,6},{8,9},{9,8},{10,11... | collective-permute-start | bytes 884744 | tf_op jit(solution)/shard_map/ppermute | solution.py:56
  122.0 0.1 collective-permute-start.8
  122.1 1.1 collective-permute-done.7.mean_got
  123.2 0.4 collective-permute-done.8.square_got
  123.7 0.9 unpair.1
  124.5 5.4 %all-to-all-done.4.strips = bf16[16,16,384]{2,1,0:T(8,128)(2,1)S(1)} async-done(((bf16[16,16,384]{2,1,0:T(8,128)(2,1)}), bf16[16,16,384]{2,1,0:T(8,128)(2,1)S(1)}, u32[]{:S(2)}, u32[]{:S(2)}) %all-to-all-start.4) | async-done | bytes 196640 | tf_op jit(solution)/shard_map/all_to_all | solution.py:469
  130.0 13.4 %all_to_all.33.own = bf16[16,16,384]{2,1,0:T(8,128)(2,1)S(1)} all-to-all(bf16[16,16,384]{2,1,0:T(8,128)(2,1)S(1)} %strip_sum.1), channel_id=1, replica_groups=mesh['replica'=16,'fsdp'=16] {'replica'}, dimensions={0} | all-to-all | bytes 393216 | tf_op jit(solution)/shard_map/all_to_all | solution.py:480
  143.3 4.0 %collective-permute-start.9 = (bf16[16,16,384]{2,1,0:T(8,128)(2,1)S(1)}, bf16[16,16,384]{2,1,0:T(8,128)(2,1)S(1)}, u32[]{:S(2)}, u32[]{:S(2)}) collective-permute-start(bf16[16,16,384]{2,1,0:T(8,128)(2,1)S(1)} %all_to_all.33.own), channel_id=1, source_target_pairs={{0,1},{1,0},{2,3},{3,2},{4,5},{5,4},{6,7},{7,6},{8,9},{9,8},{10,11... | collective-permute-start | bytes 589832 | tf_op jit(solution)/shard_map/ppermute | solution.py:56
  147.3 1.1 collective-permute-done.9.got
  148.4 0.9 outer.1
  (33 shorter events, 0.1 us)
Async XLA Ops:
  0.6 4.7 %collective-permute-start = (f32[24,3072]{1,0:T(8,128)}, f32[24,3072]{1,0:T(8,128)S(1)}, u32[]{:S(2)}, u32[]{:S(2)}) collective-permute-start(f32[24,3072]{1,0:T(8,128)} %params.1), channel_id=1, source_target_pairs={{0,1},{1,0},{2,3},{3,2},{4,5},{5,4},{6,7},{7,6},{8,9},{9,8},{10,11... | collective-permute-start | bytes 884744 | tf_op jit(solution)/shard_map/ppermute | solution.py:56
  4.0 1.0 copy-start
  6.5 4.0 %copy-start.3 = (f32[1,24,3072]{2,1,0:T(8,128)S(1)}, f32[1,24,3072]{2,1,0:T(8,128)}, u32[]{:S(2)}) copy-start(f32[1,24,3072]{2,1,0:T(8,128)} %param.11) | copy-start | bytes 884740
  6.5 4.7 %copy-start.4 = (f32[1,24,3072]{2,1,0:T(8,128)S(1)}, f32[1,24,3072]{2,1,0:T(8,128)}, u32[]{:S(2)}) copy-start(f32[1,24,3072]{2,1,0:T(8,128)} %param.12) | copy-start | bytes 884740
  6.5 5.5 %copy-start.9 = (f32[15,2,3072]{2,1,0:T(2,128)S(1)}, f32[15,2,3072]{2,1,0:T(2,128)}, u32[]{:S(2)}) copy-start(f32[15,2,3072]{2,1,0:T(2,128)} %modulation.1) | copy-start | bytes 1105924
  6.5 5.5 %copy-start.10 = (bf16[2,512,64]{1,2,0:T(8,128)(2,1)S(1)}, bf16[2,512,64]{1,2,0:T(8,128)(2,1)}, u32[]{:S(2)}) copy-start(bf16[2,512,64]{1,2,0:T(8,128)(2,1)} %param.13) | copy-start | bytes 393220
  6.6 5.5 %copy-start.11 = (bf16[2,512,64]{1,2,0:T(8,128)(2,1)S(1)}, bf16[2,512,64]{1,2,0:T(8,128)(2,1)}, u32[]{:S(2)}) copy-start(bf16[2,512,64]{1,2,0:T(8,128)(2,1)} %param.14) | copy-start | bytes 393220
  6.6 5.5 %copy-start.12 = (s32[2,512]{1,0:T(2,128)S(1)}, s32[2,512]{1,0:T(2,128)}, u32[]{:S(2)}) copy-start(s32[2,512]{1,0:T(2,128)} %levels.1) | copy-start | bytes 12292
  6.6 20.5 %all-to-all-start = ((bf16[8,48,1536]{2,1,0:T(8,128)(2,1)}), bf16[8,48,1536]{2,1,0:T(8,128)(2,1)S(1)}, u32[]{:S(2)}, u32[]{:S(2)}) async-start(bf16[8,48,1536]{2,1,0:T(8,128)(2,1)} %get-tuple-element.97), calls=%async_computation | async-start | bytes 2359296 | tf_op jit(solution)/shard_map/all_to_all | solution.py:61
  10.5 8.7 %collective-permute-start.1 = (f32[24,3072]{1,0:T(8,128)S(1)}, f32[24,3072]{1,0:T(8,128)S(1)}, u32[]{:S(2)}, u32[]{:S(2)}) collective-permute-start(f32[24,3072]{1,0:T(8,128)S(1)} %bitcast.19), channel_id=1, source_target_pairs={{0,1},{1,0},{2,3},{3,2},{4,5},{5,4},{6,7},{7,6},{8,9},{9,8},{10,11... | collective-permute-start | bytes 884744 | tf_op jit(solution)/shard_map/ppermute | solution.py:56
  11.3 7.9 %collective-permute-start.2 = (f32[24,3072]{1,0:T(8,128)S(1)}, f32[24,3072]{1,0:T(8,128)S(1)}, u32[]{:S(2)}, u32[]{:S(2)}) collective-permute-start(f32[24,3072]{1,0:T(8,128)S(1)} %bitcast.21), channel_id=1, source_target_pairs={{0,1},{1,0},{2,3},{3,2},{4,5},{5,4},{6,7},{7,6},{8,9},{9,8},{10,11... | collective-permute-start | bytes 884744 | tf_op jit(solution)/shard_map/ppermute | solution.py:56
  14.4 0.7 copy-start.5
  15.1 0.7 copy-start.7
  15.8 0.7 copy-start.13
  16.5 0.7 copy-start.15
  17.2 0.6 copy-start.17
  17.9 0.7 copy-start.19
  18.6 0.6 copy-start.21
  19.2 9.4 %copy-start.20 = (bf16[512,64]{1,0:T(8,128)(2,1)S(1)}, bf16[512,64]{1,0:T(8,128)(2,1)}, u32[]{:S(2)}) copy-start(bf16[512,64]{1,0:T(8,128)(2,1)} %copy-done.19) | copy-start | bytes 196612
  27.1 5.2 %collective-permute-start.3 = (bf16[384,1536]{1,0:T(8,128)(2,1)S(1)}, bf16[384,1536]{1,0:T(8,128)(2,1)S(1)}, u32[]{:S(2)}, u32[]{:S(2)}) collective-permute-start(bf16[384,1536]{1,0:T(8,128)(2,1)S(1)} %bitcast.13), channel_id=1, source_target_pairs={{0,1},{1,0},{2,3},{3,2},{4,5},{5,4},{6,7},{7,6},{8,9},{9,8},{10,11... | collective-permute-start | bytes 3538952 | tf_op jit(solution)/shard_map/ppermute | solution.py:56
  28.6 1.0 copy-start.16
  29.6 0.8 copy-start.22
  32.3 1.9 %copy-start.8 = (f32[512,64]{1,0:T(8,128)S(1)}, f32[512,64]{1,0:T(8,128)}, u32[]{:S(2)}) copy-start(f32[512,64]{1,0:T(8,128)} %copy-done.7) | copy-start | bytes 393220
  36.3 3.1 %collective-permute-start.4 = (bf16[384,1536]{1,0:T(8,128)(2,1)S(1)}, bf16[384,1536]{1,0:T(8,128)(2,1)S(1)}, u32[]{:S(2)}, u32[]{:S(2)}) collective-permute-start(bf16[384,1536]{1,0:T(8,128)(2,1)S(1)} %backward.4), channel_id=1, source_target_pairs={{0,1},{1,0},{2,3},{3,2},{4,5},{5,4},{6,7},{7,6},{8,9},{9,8},{10,11... | collective-permute-start | bytes 3538952 | tf_op jit(solution)/shard_map/ppermute | solution.py:56
  59.5 20.9 %copy-start.14 = (bf16[512,256]{1,0:T(8,128)(2,1)S(1)}, bf16[512,256]{1,0:T(8,128)(2,1)}, u32[]{:S(2)}) copy-start(bf16[512,256]{1,0:T(8,128)(2,1)} %copy-done.13) | copy-start | bytes 786436
  59.5 20.8 %copy-start.18 = (bf16[512,64]{1,0:T(8,128)(2,1)S(1)}, bf16[512,64]{1,0:T(8,128)(2,1)}, u32[]{:S(2)}) copy-start(bf16[512,64]{1,0:T(8,128)(2,1)} %copy-done.17) | copy-start | bytes 196612
  59.5 20.8 %copy-start.23 = (bf16[16,1536]{1,0:T(8,128)(2,1)S(1)}, bf16[16,1536]{1,0:T(8,128)(2,1)}, u32[]{:S(2)}) copy-start(bf16[16,1536]{1,0:T(8,128)(2,1)} %copy-done.21) | copy-start | bytes 147460
  78.0 4.8 %collective-permute-start.5 = (bf16[384,1536]{1,0:T(8,128)(2,1)S(1)}, bf16[384,1536]{1,0:T(8,128)(2,1)S(1)}, u32[]{:S(2)}, u32[]{:S(2)}) collective-permute-start(bf16[384,1536]{1,0:T(8,128)(2,1)S(1)} %bitcast.16), channel_id=1, source_target_pairs={{0,1},{1,0},{2,3},{3,2},{4,5},{5,4},{6,7},{7,6},{8,9},{9,8},{10,11... | collective-permute-start | bytes 3538952 | tf_op jit(solution)/shard_map/ppermute | solution.py:56
  82.3 2.5 %copy-start.6 = (f32[512,64]{1,0:T(8,128)S(1)}, f32[512,64]{1,0:T(8,128)}, u32[]{:S(2)}) copy-start(f32[512,64]{1,0:T(8,128)} %copy-done.5) | copy-start | bytes 393220
  86.8 2.9 %collective-permute-start.6 = (bf16[384,1536]{1,0:T(8,128)(2,1)S(1)}, bf16[384,1536]{1,0:T(8,128)(2,1)S(1)}, u32[]{:S(2)}, u32[]{:S(2)}) collective-permute-start(bf16[384,1536]{1,0:T(8,128)(2,1)S(1)} %backward.6), channel_id=1, source_target_pairs={{0,1},{1,0},{2,3},{3,2},{4,5},{5,4},{6,7},{7,6},{8,9},{9,8},{10,11... | collective-permute-start | bytes 3538952 | tf_op jit(solution)/shard_map/ppermute | solution.py:56
  110.3 38.1 %copy-start.1 = (f32[24,3072]{1,0:T(8,128)S(1)}, f32[24,3072]{1,0:T(8,128)}, u32[]{:S(2)}) copy-start(f32[24,3072]{1,0:T(8,128)} %params.1) | copy-start | bytes 884740
  110.3 38.1 %copy-start.2 = (f32[24,3072]{1,0:T(8,128)S(1)}, f32[24,3072]{1,0:T(8,128)}, u32[]{:S(2)}) copy-start(f32[24,3072]{1,0:T(8,128)} %momentum.1) | copy-start | bytes 884740
  110.3 19.6 %all-to-all-start.4 = ((bf16[16,16,384]{2,1,0:T(8,128)(2,1)}), bf16[16,16,384]{2,1,0:T(8,128)(2,1)S(1)}, u32[]{:S(2)}, u32[]{:S(2)}) async-start(bf16[16,16,384]{2,1,0:T(8,128)(2,1)} %get-tuple-element.180), calls=%async_computation.4 | async-start | bytes 393216 | tf_op jit(solution)/shard_map/all_to_all | solution.py:469
  120.3 2.9 %collective-permute-start.7 = (f32[48,1536]{1,0:T(8,128)S(1)}, f32[48,1536]{1,0:T(8,128)S(1)}, u32[]{:S(2)}, u32[]{:S(2)}) collective-permute-start(f32[48,1536]{1,0:T(8,128)S(1)} %get-tuple-element.181.mean), channel_id=1, source_target_pairs={{0,1},{1,0},{2,3},{3,2},{4,5},{5,4},{6,7},{7,6},{8,9},{9,8},{10,11... | collective-permute-start | bytes 884744 | tf_op jit(solution)/shard_map/ppermute | solution.py:56
  122.0 1.6 %collective-permute-start.8 = (f32[48,1536]{1,0:T(8,128)S(1)}, f32[48,1536]{1,0:T(8,128)S(1)}, u32[]{:S(2)}, u32[]{:S(2)}) collective-permute-start(f32[48,1536]{1,0:T(8,128)S(1)} %get-tuple-element.182.square), channel_id=1, source_target_pairs={{0,1},{1,0},{2,3},{3,2},{4,5},{5,4},{6,7},{7,6},{8,9},{9,8},{10,11... | collective-permute-start | bytes 884744 | tf_op jit(solution)/shard_map/ppermute | solution.py:56
  143.3 5.1 %collective-permute-start.9 = (bf16[16,16,384]{2,1,0:T(8,128)(2,1)S(1)}, bf16[16,16,384]{2,1,0:T(8,128)(2,1)S(1)}, u32[]{:S(2)}, u32[]{:S(2)}) collective-permute-start(bf16[16,16,384]{2,1,0:T(8,128)(2,1)S(1)} %all_to_all.33.own), channel_id=1, source_target_pairs={{0,1},{1,0},{2,3},{3,2},{4,5},{5,4},{6,7},{7,6},{8,9},{9,8},{10,11... | collective-permute-start | bytes 589832 | tf_op jit(solution)/shard_map/ppermute | solution.py:56

commit v3 on v2

--- a/solution.py
+++ b/solution.py
@@ -116,8 +116,12 @@
     unpair_halves(core, square, square_got, new_square)
 
 
-def forward_kernel(tokens, embed, weights, factor, shift, hid, mod, slope, out, square, bias, pre_buf, in_buf):
-    channels = tokens.shape[1]
+def scaled_out_weight(weights, factor, time_end):
+    return (weights[time_end:, :].astype(F32) * factor[0:1, :]).astype(BF16)
+
+
+def forward_kernel(tokens, embed, weights, factor, shift, hid, slope, stats, pre_buf, in_buf, square):
+    rows_here, channels = tokens.shape
     time_end = channels + embed.shape[1]
     square[...] = jnp.zeros_like(square)
     for index in range(weights.shape[1] // FWD_COLUMNS):
@@ -127,133 +131,162 @@
             embed[...], weights[channels:time_end, cols], preferred_element_type=F32
         )
         in_buf[slot] = jnp.dot(tokens[...], weights[0:channels, cols], preferred_element_type=F32)
-        scale = jnp.broadcast_to(factor[0:1, cols], (ROW_CHUNK, FWD_COLUMNS))
-        for start in range(0, tokens.shape[0], ROW_CHUNK):
+        for start in range(0, rows_here, ROW_CHUNK):
             rows = pl.ds(start, ROW_CHUNK)
-            pre = pre_buf[slot, rows, :]
-            sigma = 0.5 * jnp.tanh(0.5 * pre) + 0.5
-            silu = pre * sigma
+            half_pre = pre_buf[slot, rows, :]
+            wave = jnp.tanh(half_pre)
+            above = wave + 1.0
+            silu = half_pre * above
             hidden = in_buf[slot, rows, :] + silu
-            mod[rows, cols] = (hidden * scale).astype(BF16)
             hid[rows, cols] = hidden.astype(BF16)
-            slope[rows, cols] = (sigma + (silu - silu * sigma)).astype(BF16)
+            slope[rows, cols] = (above + silu * (1.0 - wave)).astype(BF16)
             power = hidden * hidden
             partial = power[:, 0:LANES]
             for lane in range(LANES, FWD_COLUMNS, LANES):
                 partial = partial + power[:, lane : lane + LANES]
             square[rows, :] += partial
-    out_weight = weights[time_end:, :]
-    out[...] = lax.dot_general(mod[...], out_weight, TRANSPOSED, preferred_element_type=F32)
-    bias[...] = lax.dot_general(shift[...], out_weight, TRANSPOSED, preferred_element_type=F32)
+    scaled = scaled_out_weight(weights, factor, time_end)
+    out = lax.dot_general(hid[...], scaled, TRANSPOSED, preferred_element_type=F32)
+    bias = lax.dot_general(
+        shift[...], weights[time_end:, :], TRANSPOSED, preferred_element_type=F32
+    )
+    power = jnp.sum(square[...], axis=1, keepdims=True)
+    stats[0:rows_here, :] = jnp.concatenate(
+        [out, jnp.broadcast_to(power, (rows_here, LANES - channels))], axis=1
+    )
+    stats[rows_here:, :] = jnp.concatenate([bias, jnp.zeros_like(bias)], axis=1)
 
 
 def forward(tokens, embed, weights, factor, shift):
     rows, columns = tokens.shape[0], weights.shape[1]
-    channels = tokens.shape[1]
-    outs = [((rows, columns), BF16)] * 3 + [
-        ((rows, channels), F32),
-        ((rows, LANES), F32),
-        ((shift.shape[0], channels), F32),
-    ]
-    scratch = [pltpu.VMEM((2, rows, FWD_COLUMNS), F32)] * 2
+    outs = [((rows, columns), BF16)] * 2 + [((rows + shift.shape[0], LANES), F32)]
+    scratch = [pltpu.VMEM((2, rows, FWD_COLUMNS), F32)] * 2 + [pltpu.VMEM((rows, LANES), F32)]
     flops = 2 * rows * columns * weights.shape[0]
     args = (tokens, embed, weights, factor, shift)
     return local_call(forward_kernel, "forward", args, outs, scratch, flops=flops)
 
 
-def make_head_kernel(model_width, total_rows):
-    def head_kernel(out_a, out_b, square_a, square_b, bias_a, bias_b, target, grad, grad_t, pull, grad_sum):
+def make_backward_kernel(model_width, total_rows, added):
+    def backward_kernel(
+        own, got, target, hid, slope, weights, factor, shift, tokens_t, embed_t, *rest
+    ):
+        before = rest[0] if added else None
+        out, mod_buf, hid_buf, pre_buf, pull = rest[1:] if added else rest
         root = 1.0 / math.sqrt(model_width)
-        raw = out_a[...] + out_b[...]
-        power = jnp.sum(square_a[...] + square_b[...], axis=1, keepdims=True)
-        inverse = lax.rsqrt(power * (1.0 / model_width) + NORM_EPS)
-        bias = jnp.sum(bias_a[...] + bias_b[...], axis=0, keepdims=True)
-        output = (inverse * raw + bias) * root
-        out_grad = (2.0 / (total_rows * raw.shape[1])) * (output - target[...])
-        scaled = (out_grad * inverse).astype(BF16)
-        wide = scaled.astype(F32)
-        grad[...] = scaled
-        grad_t[...] = wide.T.astype(BF16)
-        pulled = inverse * inverse * (root / model_width) * jnp.sum(wide * raw, axis=1, keepdims=True)
-        pull[...] = jnp.broadcast_to(pulled, pull.shape)
-        summed = jnp.sum(out_grad.T, axis=1, keepdims=True)
-        grad_sum[...] = jnp.broadcast_to(summed, grad_sum.shape)
-
-    return head_kernel
-
-
-def make_backward_kernel(model_width):
-    def backward_kernel(
-        hid, mod, slope, weights, factor, shift, tokens_t, embed_t, grad, grad_t, pull, grad_sum,
-        out, mod_buf, hid_buf, pre_buf,
-    ):
-        root = 1.0 / math.sqrt(model_width)
-        channels = tokens_t.shape[0]
+        rows_here, channels = target.shape
         time_end = channels + embed_t.shape[0]
         columns = out.shape[1]
-        mod_buf[...] = jnp.dot(grad[...], weights[time_end:, :], preferred_element_type=F32)
-        scale = jnp.broadcast_to(factor[0:1, :] * root, (ROW_CHUNK, columns))
-        for start in range(0, grad.shape[0], ROW_CHUNK):
+
+        both = own[0:rows_here, :] + got[0:rows_here, :]
+        raw = both[:, 0:channels]
+        inverse = lax.rsqrt(both[:, channels : channels + 1] * (1.0 / model_width) + NORM_EPS)
+        terms = own[rows_here:, 0:channels] + got[rows_here:, 0:channels]
+        bias = jnp.sum(terms, axis=0, keepdims=True)
+        output = (inverse * raw + bias) * root
+        out_grad = (2.0 / (total_rows * channels)) * (output - target[...])
+        grad = (out_grad * (inverse * root)).astype(BF16)
+        wide = grad.astype(F32)
+        grad_t = wide.T.astype(BF16)
+        pulled = inverse * inverse * (1.0 / model_width)
+        pulled = pulled * jnp.sum(wide * raw, axis=1, keepdims=True)
+        pull[...] = jnp.broadcast_to(pulled, pull.shape)
+        grad_sum = jnp.sum(out_grad.T, axis=1, keepdims=True) * root
+
+        scaled = scaled_out_weight(weights, factor, time_end)
+        mod_buf[...] = jnp.dot(grad, scaled, preferred_element_type=F32)
+        for start in range(0, rows_here, ROW_CHUNK):
             rows = pl.ds(start, ROW_CHUNK)
-            pulled = jnp.concatenate([pull[rows, :]] * (columns // LANES), axis=1)
-            hid_grad = mod_buf[rows, :] * scale - hid[rows, :].astype(F32) * pulled
+            spread = jnp.concatenate([pull[rows, :]] * (columns // LANES), axis=1)
+            hid_grad = mod_buf[rows, :] - hid[rows, :].astype(F32) * spread
             hid_buf[rows, :] = hid_grad.astype(BF16)
             pre_buf[rows, :] = (hid_grad * slope[rows, :].astype(F32)).astype(BF16)
-        out[0:channels, :] = jnp.dot(
-            tokens_t[...], hid_buf[...], preferred_element_type=F32
-        ).astype(BF16)
-        out[channels:time_end, :] = jnp.dot(
-            embed_t[...], pre_buf[...], preferred_element_type=F32
-        ).astype(BF16)
-        grad_out = jnp.dot(grad_t[...], mod[...], preferred_element_type=F32)
-        summed = jnp.concatenate([grad_sum[...]] * (columns // LANES), axis=1)
-        out[time_end:, :] = ((grad_out + summed * shift[0:1, :]) * root).astype(BF16)
+
+        def put(rows, values):
+            if added:
+                values = values + before[rows, :]
+            out[rows, :] = values.astype(out.dtype)
+
+        put(
+            slice(0, channels),
+            jnp.dot(tokens_t[...], hid_buf[...], preferred_element_type=F32),
+        )
+        put(
+            slice(channels, time_end),
+            jnp.dot(embed_t[...], pre_buf[...], preferred_element_type=F32),
+        )
+        grad_out = jnp.dot(grad_t, hid[...], preferred_element_type=F32)
+        put(
+            slice(time_end, out.shape[0]),
+            grad_out * factor[0:1, :] + grad_sum * shift[0:1, :],
+        )
 
     return backward_kernel
 
 
-def backward(state, weights, factor, shift, tokens_t, embed_t, head, model_width):
+def backward(stats, target, state, weights, factor, shift, tokens_t, embed_t, before, sizes):
     rows, columns = state[0].shape
     scratch = [
         pltpu.VMEM((rows, columns), F32),
         pltpu.VMEM((rows, columns), BF16),
         pltpu.VMEM((rows, columns), BF16),
+        pltpu.VMEM((rows, LANES), F32),
     ]
     flops = 2 * rows * columns * (weights.shape[0] + tokens_t.shape[0])
-    args = (*state, weights, factor, shift, tokens_t, embed_t, *head)
-    outs = [(weights.shape, BF16)]
-    return local_call(make_backward_kernel(model_width), "backward", args, outs, scratch, flops=flops)[0]
-
-
-def prepare_kernel(core, fragment, latents, noise, levels, modulation, *outs):
+    args = (*stats, target, *state, weights, factor, shift, tokens_t, embed_t, *before)
+    outs = [(weights.shape, BF16 if before else F32)]
+    kernel = make_backward_kernel(*sizes, bool(before))
+    return local_call(kernel, "backward", args, outs, scratch, flops=flops)[0]
+
+
+def prepare_kernel(
+    core, fragment, latents, latents_got, noise, noise_got, levels, levels_got, modulation, *rest
+):
+    outs, (latent_buf, noise_buf, level_buf) = rest[:-3], rest[-3:]
     steps, channels, tokens = latents.shape
     half_width = outs[1].shape[1] // 2
-    per_step = 5
+    pairs = ((latents, latents_got), (noise, noise_got), (levels, levels_got))
+    for buffer, (own, got) in zip((latent_buf, noise_buf, level_buf), pairs):
+
+        @pl.when(core[0] == 0)
+        def _():
+            buffer[0] = own[...]
+            buffer[1] = got[...]
+
+        @pl.when(core[0] != 0)
+        def _():
+            buffer[0] = got[...]
+            buffer[1] = own[...]
+
+    place = 0
     for step in range(steps):
-        token_rows, embed_rows, token_cols, embed_cols, target = outs[per_step * step : per_step * (step + 1)]
-        level = (levels[step : step + 1, :].astype(F32) + 0.5) / LEVELS
-        latent = latents[step].astype(F32)
-        draw = noise[step].astype(F32)
-        noised = ((1.0 - level) * latent + level * draw).astype(BF16).astype(F32)
-        noised = noised * (1.0 / math.sqrt(channels))
-        token_cols[...] = noised.astype(BF16)
-        token_rows[...] = noised.T.astype(BF16)
-        target[...] = (draw - latent).T
-        order = lax.broadcasted_iota(jnp.int32, (half_width, tokens), 0).astype(F32)
-        angles = (1000.0 * level) * jnp.exp(-math.log(10000.0) * order / half_width)
-        root = 1.0 / math.sqrt(2 * half_width)
-        for part, wave in enumerate((jnp.cos(angles), jnp.sin(angles))):
-            wave = wave.astype(BF16).astype(F32) * root
-            place = pl.ds(part * half_width, half_width)
-            embed_cols[place, :] = wave.astype(BF16)
-            embed_rows[:, place] = wave.T.astype(BF16)
+        for owner in range(CORES):
+            token_rows, embed_rows, token_cols, embed_cols, target = outs[place : place + 5]
+            place += 5
+            level = (level_buf[owner, step : step + 1, :].astype(F32) + 0.5) / LEVELS
+            latent = latent_buf[owner, step].astype(F32)
+            draw = noise_buf[owner, step].astype(F32)
+            noised = ((1.0 - level) * latent + level * draw).astype(BF16).astype(F32)
+            noised = noised * (1.0 / math.sqrt(channels))
+            token_cols[...] = noised.astype(BF16)
+            token_rows[...] = noised.T.astype(BF16)
+            target[...] = (draw - latent).T
+            order = lax.broadcasted_iota(jnp.int32, (half_width, tokens), 0).astype(F32)
+            angles = (1000.0 * level) * jnp.exp(-math.log(10000.0) * order / half_width)
+            root = 0.5 / math.sqrt(2 * half_width)
+            for part, wave in enumerate((jnp.cos(angles), jnp.sin(angles))):
+                wave = wave.astype(BF16).astype(F32) * root
+                here = pl.ds(part * half_width, half_width)
+                embed_cols[here, :] = wave.astype(BF16)
+                embed_rows[:, here] = wave.T.astype(BF16)
     rows = modulation[fragment[0]]
     half = rows.shape[1] // CORES
+    factor, shift, terms = outs[place:]
+
     for side in range(CORES):
-        factor, shift, terms = outs[per_step * steps + 3 * side : per_step * steps + 3 * (side + 1)]
-
-        def place_half(first):
-            here = rows[:, first : first + half]
+
+        @pl.when(core[0] == side)
+        def _():
+            here = rows[:, side * half : (side + 1) * half]
             factor[...] = 1.0 + here[1:2]
             shift[...] = here[0:1]
             wide = jnp.broadcast_to(here[0:1], terms.shape)
@@ -262,16 +295,8 @@
             split = jnp.where(index == 0, high, jnp.where(index == 1, wide - high, 0.0))
             terms[...] = split.astype(BF16)
 
-        @pl.when(core[0] == side)
-        def _():
-            place_half(0)
-
-        @pl.when(core[0] != side)
-        def _():
-            place_half(half)
-
-
-def prepare(core, fragment, latents, noise_draw, timesteps, modulation, time_width):
+
+def prepare(core, fragment, latents, noise_draw, timesteps, modulation, time_width, width):
     steps, tokens, channels = latents.shape
     half = modulation.shape[2] // CORES
     outs = [
@@ -280,18 +305,23 @@
         ((channels, tokens), BF16),
         ((time_width, tokens), BF16),
         ((tokens, channels), F32),
-    ] * steps + [((1, half), F32), ((1, half), F32), ((16, half), BF16)] * CORES
-    args = (latents.transpose(0, 2, 1), noise_draw.transpose(0, 2, 1), timesteps, modulation)
+    ] * (steps * CORES) + [((1, half), F32), ((1, half), F32), ((16, half), BF16)]
+    args = []
+    scratch = []
+    for values in (latents.transpose(0, 2, 1), noise_draw.transpose(0, 2, 1), timesteps):
+        args += [values, core_swap(values, width)]
+        scratch.append(pltpu.VMEM((CORES,) + values.shape, values.dtype))
     results = local_call(
-        prepare_kernel, "prepare", args, outs, scalars=(core, fragment), flops=2**32
-    )
-    return [results[5 * s : 5 * s + 5] for s in range(steps)], [
-        results[5 * steps + 3 * c : 5 * steps + 3 * c + 3] for c in range(CORES)
-    ]
-
-
-def pair_sum_kernel(mine, got, out):
-    out[...] = (mine[...].astype(F32) + got[...].astype(F32)).astype(BF16)
+        prepare_kernel,
+        "prepare",
+        (*args, modulation),
+        outs,
+        scratch,
+        scalars=(core, fragment),
+        flops=2**32,
+    )
+    sets = [results[5 * i : 5 * i + 5] for i in range(steps * CORES)]
+    return [sets[CORES * s : CORES * (s + 1)] for s in range(steps)], results[-3:]
 
 
 def step_kernel(blocks, params, mean, square, new_mean, new_square, new_params, copies):
@@ -404,7 +434,7 @@
     gathered = chip_exchange(copies, width)
 
     prepared, mods = prepare(
-        core_arg, fragment, latents, noise_draw, timesteps, modulation, time_width
+        core_arg, fragment, latents, noise_draw, timesteps, modulation, time_width, width
     )
     params = start
     mean, square = local_call(
@@ -423,35 +453,22 @@
         (gathered, prepared, mods, mean, square)
     )
 
+    sizes = (model_width, total_rows)
+    factor, shift, terms = mods
     for step in range(STEPS):
-        tokens, embed, tokens_t, embed_t, target = prepared[step]
         weights = gathered.reshape(chips * pair_shape[0], half)
-        other = core_swap(weights, width)
-        state = forward(tokens, embed, weights, mods[0][0], mods[0][2])
-        state_other = forward(tokens, embed, other, mods[1][0], mods[1][2])
-        shapes = [
-            ((target.shape[0], channels), BF16),
-            ((channels, target.shape[0]), BF16),
-            ((target.shape[0], LANES), F32),
-            ((channels, LANES), F32),
-        ]
-        head = local_call(
-            make_head_kernel(model_width, total_rows),
-            "head",
-            (state[3], state_other[3], state[4], state_other[4], state[5], state_other[5], target),
-            shapes,
-        )
-        grad_other = backward(
-            state_other[:3], other, mods[1][0], mods[1][1], tokens_t, embed_t, head, model_width
-        )
-        received = core_swap(grad_other, width)
-        head, grad_other = lax.optimization_barrier((head, grad_other))
-        grad_mine = backward(
-            state[:3], weights, mods[0][0], mods[0][1], tokens_t, embed_t, head, model_width
-        )
-        pair_sum = local_call(
-            pair_sum_kernel, "pair_sum", (grad_mine, received), [(weights.shape, BF16)]
-        )[0]
+        states = []
+        for tokens, embed, _, _, _ in prepared[step]:
+            hid, slope, stats = forward(tokens, embed, weights, factor, terms)
+            states.append(((hid, slope), (stats, core_swap(stats, width))))
+        gradient = ()
+        for (state, stats), (_, _, tokens_t, embed_t, target) in zip(states, prepared[step]):
+            gradient = (
+                backward(
+                    stats, target, state, weights, factor, shift, tokens_t, embed_t, gradient, sizes
+                ),
+            )
+        pair_sum = gradient[0]
         blocks = chip_exchange(pair_sum.reshape((chips,) + pair_shape), width)
         moments = [(pair_shape, F32)] * 2
         if step + 1 < STEPS:

time: 150 us -> 150 us (level)
  waiting for transfers between devices: 18.9 us -> 8.43 us
  local copies, waits for them, and re-layouts: 7.51 us -> 16 us
  blocking collectives: 70.4 us -> 72.8 us
    unnamed x48 -> x88, local copies, waits for them, and re-layouts: 7.51 us -> 16 us
    all_to_all x1, waiting for transfers between devices: 7.83 us -> 0.01 us  [chip_exchange(): return lax.all_to_all(blocks, 'fsdp', 0, 0, axis_index_groups=groups)]
    ppermute x10 -> x13, waiting for transfers between devices: 5.6 us -> 2.97 us  [core_swap(): return lax.ppermute(values, 'fsdp', [(i, i ^ 1) for i in range(width)])]
    all_to_all x3, blocking collectives: 57 us -> 59.5 us  [chip_exchange(): return lax.all_to_all(blocks, 'fsdp', 0, 0, axis_index_groups=groups)]
    pallas_call x21 -> x17, Pallas kernels: 22.5 us -> 22.3 us  [local_call(): pl.pallas_call(kernel, in_specs=specs, out_specs=[VMEM] * len(outs), out_...]
    ppermute x10 -> x13, starting transfers between devices: 14.6 us -> 14.6 us  [core_swap(): return lax.ppermute(values, 'fsdp', [(i, i ^ 1) for i in range(width)])]
  transfers between devices with their start and end apart: 12 -> 15, of which waited for: 9 -> 5; matrix products, arithmetic and copies ran while one was open for 0% -> 0% of each run, Pallas kernels for 7% -> 8%
where the time goes in v3:
time: 150 us
  blocking collectives  72.8 us (49%)
  starting transfers between devices  28.4 us (19%)
  Pallas kernels  22.3 us (15%)
  local copies, waits for them, and re-layouts  16 us (11%)
  waiting for transfers between devices  8.43 us (6%)
  between operations  1.69 us (1%)
    all_to_all x3, blocking collectives, chip_exchange(): return lax.all_to_all(blocks, 'fsdp', 0, 0, axis_index_groups=groups)  59.5 us
    pallas_call x17, Pallas kernels, local_call(): pl.pallas_call(kernel, in_specs=specs, out_specs=[VMEM] * len(outs), out_...  22.3 us
    unnamed x88, local copies, waits for them, and re-layouts  16 us
    ppermute x13, starting transfers between devices, core_swap(): return lax.ppermute(values, 'fsdp', [(i, i ^ 1) for i in range(width)])  14.6 us
    all_to_all x1, blocking collectives, on_device(): strips = lax.all_to_all(strips, 'replica', 0, 0)  13.3 us
    all_to_all x1, starting transfers between devices, on_device(): strips = lax.all_to_all(strips, 'replica', 0, 0)  9.97 us
    all_to_all x1, waiting for transfers between devices, on_device(): strips = lax.all_to_all(strips, 'replica', 0, 0)  5.45 us
    all_to_all x1, starting transfers between devices, chip_exchange(): return lax.all_to_all(blocks, 'fsdp', 0, 0, axis_index_groups=groups)  3.81 us
  transfers between devices with their start and end apart: 15, of which 5 were waited for; matrix products, arithmetic and copies ran while one was open for 0% of the time, Pallas kernels for 8%

profile of v3, /device:TPU:1, one launch (start us, length us, event | category | flops | bytes accessed | tf_op | source)
XLA Modules:
  0.0 149.7 jit_solution(6668711320740440336)
XLA Ops:
  0.6 3.3 %collective-permute-start = (f32[24,3072]{1,0:T(8,128)}, f32[24,3072]{1,0:T(8,128)S(1)}, u32[]{:S(2)}, u32[]{:S(2)}) collective-permute-start(f32[24,3072]{1,0:T(8,128)} %params.1), channel_id=1, source_target_pairs={{0,1},{1,0},{2,3},{3,2},{4,5},{5,4},{6,7},{7,6},{8,9},{9,8},{10,11... | collective-permute-start | bytes 884744 | tf_op jit(solution)/shard_map/ppermute | solution.py:56
  4.0 1.0 copy-done
  5.0 0.0 copy-start.25
  5.0 0.0 copy-start.3
  5.0 0.4 collective-permute-done.got
  5.4 1.1 start.1
  6.5 3.8 %all-to-all-start = ((bf16[8,48,1536]{2,1,0:T(8,128)(2,1)}), bf16[8,48,1536]{2,1,0:T(8,128)(2,1)S(1)}, u32[]{:S(2)}, u32[]{:S(2)}) async-start(bf16[8,48,1536]{2,1,0:T(8,128)(2,1)} %get-tuple-element.83), calls=%async_computation | async-start | bytes 2359296 | tf_op jit(solution)/shard_map/all_to_all | solution.py:61
  10.3 0.7 collective-permute-start.1
  11.1 0.1 collective-permute-start.2
  11.2 0.4 collective-permute-start.3
  11.6 0.1 collective-permute-start.4
  11.7 0.4 collective-permute-start.5
  12.8 0.0 copy-start.24
  12.8 0.9 copy-done.24
  13.7 4.6 %prepare.1 = (bf16[512,64]{1,0:T(8,128)(2,1)S(1)}, bf16[512,256]{1,0:T(8,128)(2,1)S(1)}, bf16[64,512]{1,0:T(8,128)(2,1)S(1)}, bf16[256,512]{1,0:T(8,128)(2,1)S(1...) custom-call(s32[1]{0:T(128)} %bitcast.core, ...), custom_call_target="tpu_custom_call" | custom-call | flops 4294967296 | bytes 6778880 | tf_op jit(solution)/shard_map/prepare/pallas_call | solution.py:43
  18.3 0.7 copy-done.5
  19.0 0.7 copy-done.7
  19.7 0.7 copy-done.9
  20.4 0.7 copy-done.11
  21.1 0.7 copy-done.13
  21.8 0.6 copy-done.15
  22.5 0.6 copy-done.17
  23.1 0.6 copy-done.19
  23.7 0.7 copy-done.26
  24.4 0.7 copy-done.28
  25.1 0.7 copy-done.30
  25.8 0.7 copy-done.32
  26.5 0.6 copy-done.34
  27.2 0.6 copy-done.36
  27.8 0.6 copy-done.38
  28.5 0.7 copy-done.40
  29.1 0.6 copy-done.42
  29.8 1.0 copy-done.33
  30.8 0.9 copy-done.41
  31.7 0.8 copy-done.43
  32.5 1.5 forward.5
  34.0 0.4 collective-permute-start.7
  34.4 1.5 forward.4
  35.9 0.5 collective-permute-start.6
  36.4 0.0 copy-start.8
  36.4 1.8 %backward.4.rest_0_ = f32[384,1536]{1,0:T(8,128)S(1)} custom-call(f32[528,128]{1,0:T(8,128)S(1)} %get-tuple-element.125.own, f32[528,128]{1,0:T(8,128)S(1)} %collective-permute-done.7.got, f32[512,64]{1,0:T(8,128)S(1)} %copy-done.14, bf16[512,1536]{1,0:T(8,128)(2,1)S(1)} %get-tuple-element.127.hid, bf16[512,1536]{1,0:T(8,128)(2,1)S(1)} %get-tuple-element.128.slope, ...), custom_call_target="tpu_custom_call" | custom-call | flops 704643072 | bytes 7696384 | tf_op jit(solution)/shard_map/backward/pallas_call | solution.py:43
  38.3 1.8 %backward.5 = bf16[384,1536]{1,0:T(8,128)(2,1)S(1)} custom-call(f32[528,128]{1,0:T(8,128)S(1)} %get-tuple-element.116.own, f32[528,128]{1,0:T(8,128)S(1)} %collective-permute-done.6.got, f32[512,64]{1,0:T(8,128)S(1)} %copy-done.10, bf16[512,1536]{1,0:T(8,128)(2,1)S(1)} %get-tuple-element.118.hid, bf16[512,1536]{1,0:T(8,128)(2,1)S(1)} %get-tuple-element.119.slope, ...), custom_call_target="tpu_custom_call" | custom-call | flops 704643072 | bytes 10055680 | tf_op jit(solution)/shard_map/backward/pallas_call | solution.py:43
  40.1 22.0 %all_to_all.30.blocks = bf16[8,48,1536]{2,1,0:T(8,128)(2,1)S(1)} all-to-all(bf16[8,48,1536]{2,1,0:T(8,128)(2,1)S(1)} %bitcast.20), channel_id=1, replica_groups={{0,2,4,6,8,10,12,14},{1,3,5,7,9,11,13,15},{16,18,20,22,24,26,28,30},{17..., dimensions={0} | all-to-all | bytes 2359296 | tf_op jit(solution)/shard_map/all_to_all | solution.py:61
  62.1 0.4 update.1
  62.6 18.4 %all_to_all.31 = bf16[8,48,1536]{2,1,0:T(8,128)(2,1)S(1)} all-to-all(bf16[8,48,1536]{2,1,0:T(8,128)(2,1)S(1)} %get-tuple-element.134), channel_id=1, replica_groups={{0,2,4,6,8,10,12,14},{1,3,5,7,9,11,13,15},{16,18,20,22,24,26,28,30},{17..., dimensions={0} | all-to-all | bytes 2359296 | tf_op jit(solution)/shard_map/all_to_all | solution.py:61
  81.0 1.5 forward.7
  82.5 2.4 %collective-permute-start.9 = (f32[528,128]{1,0:T(8,128)S(1)}, f32[528,128]{1,0:T(8,128)S(1)}, u32[]{:S(2)}, u32[]{:S(2)}) collective-permute-start(f32[528,128]{1,0:T(8,128)S(1)} %get-tuple-element.143.own), channel_id=1, source_target_pairs={{0,1},{1,0},{2,3},{3,2},{4,5},{5,4},{6,7},{7,6},{8,9},{9,8},{10,11... | collective-permute-start | bytes 811016 | tf_op jit(solution)/shard_map/ppermute | solution.py:56
  84.9 1.5 %forward.6 = (bf16[512,1536]{1,0:T(8,128)(2,1)S(1)}, bf16[512,1536]{1,0:T(8,128)(2,1)S(1)}, f32[528,128]{1,0:T(8,128)S(1)}) custom-call(bf16[512,64]{1,0:T(8,128)(2,1)S(1)} %copy-done.35, bf16[512,256]{1,0:T(8,128)(2,1)S(1)} %copy-done.27, bf16[384,1536]{1,0:T(8,128)(2,1)S(1)} %bitcast.16, f32[1,1536]{1,0:T(1,128)S(1)} %get-tuple-element.114.factor, ...), custom_call_target="tpu_custom_call" | custom-call | flops 603979776 | bytes 8124416 | tf_op jit(solution)/shard_map/forward/pallas_call | solution.py:43
  86.4 0.3 collective-permute-start.8
  86.8 1.8 %backward.6.rest_0_ = f32[384,1536]{1,0:T(8,128)S(1)} custom-call(f32[528,128]{1,0:T(8,128)S(1)} %get-tuple-element.143.own, f32[528,128]{1,0:T(8,128)S(1)} %collective-permute-done.9.got, f32[512,64]{1,0:T(8,128)S(1)} %copy-done.6, bf16[512,1536]{1,0:T(8,128)(2,1)S(1)} %get-tuple-element.145.hid, bf16[512,1536]{1,0:T(8,128)(2,1)S(1)} %get-tuple-element.146.slope, ...), custom_call_target="tpu_custom_call" | custom-call | flops 704643072 | bytes 7696384 | tf_op jit(solution)/shard_map/backward/pallas_call | solution.py:43
  88.6 1.8 %backward.7 = bf16[384,1536]{1,0:T(8,128)(2,1)S(1)} custom-call(f32[528,128]{1,0:T(8,128)S(1)} %get-tuple-element.135.own, f32[528,128]{1,0:T(8,128)S(1)} %collective-permute-done.8.got, f32[512,64]{1,0:T(8,128)S(1)} %get-tuple-element.136.target, bf16[512,1536]{1,0:T(8,128)(2,1)S(1)} %get-tuple-element.137.hid, ...), custom_call_target="tpu_custom_call" | custom-call | flops 704643072 | bytes 10055680 | tf_op jit(solution)/shard_map/backward/pallas_call | solution.py:43
  90.4 19.1 %all_to_all.32.blocks = bf16[8,48,1536]{2,1,0:T(8,128)(2,1)S(1)} all-to-all(bf16[8,48,1536]{2,1,0:T(8,128)(2,1)S(1)} %bitcast.19), channel_id=1, replica_groups={{0,2,4,6,8,10,12,14},{1,3,5,7,9,11,13,15},{16,18,20,22,24,26,28,30},{17..., dimensions={0} | all-to-all | bytes 2359296 | tf_op jit(solution)/shard_map/all_to_all | solution.py:61
  109.6 1.1 update_last.1
  110.6 10.0 %all-to-all-start.4 = ((bf16[16,16,384]{2,1,0:T(8,128)(2,1)}), bf16[16,16,384]{2,1,0:T(8,128)(2,1)S(1)}, u32[]{:S(2)}, u32[]{:S(2)}) async-start(bf16[16,16,384]{2,1,0:T(8,128)(2,1)} %get-tuple-element.152), calls=%async_computation.4 | async-start | bytes 393216 | tf_op jit(solution)/shard_map/all_to_all | solution.py:486
  120.6 1.8 %collective-permute-start.10 = (f32[48,1536]{1,0:T(8,128)S(1)}, f32[48,1536]{1,0:T(8,128)S(1)}, u32[]{:S(2)}, u32[]{:S(2)}) collective-permute-start(f32[48,1536]{1,0:T(8,128)S(1)} %get-tuple-element.153.mean), channel_id=1, source_target_pairs={{0,1},{1,0},{2,3},{3,2},{4,5},{5,4},{6,7},{7,6},{8,9},{9,8},{10,11... | collective-permute-start | bytes 884744 | tf_op jit(solution)/shard_map/ppermute | solution.py:56
  122.4 0.1 collective-permute-start.11
  122.5 1.1 collective-permute-done.10.mean_got
  123.6 0.4 collective-permute-done.11.square_got
  124.0 0.9 unpair.1
  124.9 5.5 %all-to-all-done.4.strips = bf16[16,16,384]{2,1,0:T(8,128)(2,1)S(1)} async-done(((bf16[16,16,384]{2,1,0:T(8,128)(2,1)}), bf16[16,16,384]{2,1,0:T(8,128)(2,1)S(1)}, u32[]{:S(2)}, u32[]{:S(2)}) %all-to-all-start.4) | async-done | bytes 196640 | tf_op jit(solution)/shard_map/all_to_all | solution.py:486
  130.4 13.3 %all_to_all.33.own = bf16[16,16,384]{2,1,0:T(8,128)(2,1)S(1)} all-to-all(bf16[16,16,384]{2,1,0:T(8,128)(2,1)S(1)} %strip_sum.1), channel_id=1, replica_groups=mesh['replica'=16,'fsdp'=16] {'replica'}, dimensions={0} | all-to-all | bytes 393216 | tf_op jit(solution)/shard_map/all_to_all | solution.py:497
  143.7 4.0 %collective-permute-start.12 = (bf16[16,16,384]{2,1,0:T(8,128)(2,1)S(1)}, bf16[16,16,384]{2,1,0:T(8,128)(2,1)S(1)}, u32[]{:S(2)}, u32[]{:S(2)}) collective-permute-start(bf16[16,16,384]{2,1,0:T(8,128)(2,1)S(1)} %all_to_all.33.own), channel_id=1, source_target_pairs={{0,1},{1,0},{2,3},{3,2},{4,5},{5,4},{6,7},{7,6},{8,9},{9,8},{10,11... | collective-permute-start | bytes 589832 | tf_op jit(solution)/shard_map/ppermute | solution.py:56
  147.7 1.1 collective-permute-done.12.got
  148.8 0.9 outer.1
  (75 shorter events, 0.3 us)
Async XLA Ops:
  0.6 4.7 %collective-permute-start = (f32[24,3072]{1,0:T(8,128)}, f32[24,3072]{1,0:T(8,128)S(1)}, u32[]{:S(2)}, u32[]{:S(2)}) collective-permute-start(f32[24,3072]{1,0:T(8,128)} %params.1), channel_id=1, source_target_pairs={{0,1},{1,0},{2,3},{3,2},{4,5},{5,4},{6,7},{7,6},{8,9},{9,8},{10,11... | collective-permute-start | bytes 884744 | tf_op jit(solution)/shard_map/ppermute | solution.py:56
  4.0 1.0 copy-start
  4.9 5.4 %copy-start.22 = (bf16[2,512,64]{1,2,0:T(8,128)(2,1)S(1)}, bf16[2,512,64]{1,2,0:T(8,128)(2,1)}, u32[]{:S(2)}) copy-start(bf16[2,512,64]{1,2,0:T(8,128)(2,1)} %param.13) | copy-start | bytes 393220
  5.0 6.1 %copy-start.23 = (bf16[2,512,64]{1,2,0:T(8,128)(2,1)S(1)}, bf16[2,512,64]{1,2,0:T(8,128)(2,1)}, u32[]{:S(2)}) copy-start(bf16[2,512,64]{1,2,0:T(8,128)(2,1)} %param.14) | copy-start | bytes 393220
  5.0 6.2 %copy-start.25 = (s32[2,512]{1,0:T(2,128)S(1)}, s32[2,512]{1,0:T(2,128)}, u32[]{:S(2)}) copy-start(s32[2,512]{1,0:T(2,128)} %levels.1) | copy-start | bytes 12292
  5.0 6.6 %copy-start.3 = (f32[1,24,3072]{2,1,0:T(8,128)S(1)}, f32[1,24,3072]{2,1,0:T(8,128)}, u32[]{:S(2)}) copy-start(f32[1,24,3072]{2,1,0:T(8,128)} %param.11) | copy-start | bytes 884740
  5.0 6.7 %copy-start.4 = (f32[1,24,3072]{2,1,0:T(8,128)S(1)}, f32[1,24,3072]{2,1,0:T(8,128)}, u32[]{:S(2)}) copy-start(f32[1,24,3072]{2,1,0:T(8,128)} %param.12) | copy-start | bytes 884740
  5.0 7.8 %copy-start.21 = (f32[15,2,3072]{2,1,0:T(2,128)S(1)}, f32[15,2,3072]{2,1,0:T(2,128)}, u32[]{:S(2)}) copy-start(f32[15,2,3072]{2,1,0:T(2,128)} %modulation.1) | copy-start | bytes 1105924
  6.5 23.3 %all-to-all-start = ((bf16[8,48,1536]{2,1,0:T(8,128)(2,1)}), bf16[8,48,1536]{2,1,0:T(8,128)(2,1)S(1)}, u32[]{:S(2)}, u32[]{:S(2)}) async-start(bf16[8,48,1536]{2,1,0:T(8,128)(2,1)} %get-tuple-element.83), calls=%async_computation | async-start | bytes 2359296 | tf_op jit(solution)/shard_map/all_to_all | solution.py:61
  10.3 2.4 %collective-permute-start.1 = (bf16[2,64,512]{2,1,0:T(8,128)(2,1)S(1)}, bf16[2,64,512]{2,1,0:T(8,128)(2,1)S(1)}, u32[]{:S(2)}, u32[]{:S(2)}) collective-permute-start(bf16[2,64,512]{2,1,0:T(8,128)(2,1)S(1)} %bitcast.25), channel_id=1, source_target_pairs={{0,1},{1,0},{2,3},{3,2},{4,5},{5,4},{6,7},{7,6},{8,9},{9,8},{10,11... | collective-permute-start | bytes 393224 | tf_op jit(solution)/shard_map/ppermute | solution.py:56
  11.1 1.7 %collective-permute-start.2 = (bf16[2,64,512]{2,1,0:T(8,128)(2,1)S(1)}, bf16[2,64,512]{2,1,0:T(8,128)(2,1)S(1)}, u32[]{:S(2)}, u32[]{:S(2)}) collective-permute-start(bf16[2,64,512]{2,1,0:T(8,128)(2,1)S(1)} %bitcast.27), channel_id=1, source_target_pairs={{0,1},{1,0},{2,3},{3,2},{4,5},{5,4},{6,7},{7,6},{8,9},{9,8},{10,11... | collective-permute-start | bytes 393224 | tf_op jit(solution)/shard_map/ppermute | solution.py:56
  11.2 1.6 %collective-permute-start.3 = (s32[2,512]{1,0:T(2,128)S(1)}, s32[2,512]{1,0:T(2,128)S(1)}, u32[]{:S(2)}, u32[]{:S(2)}) collective-permute-start(s32[2,512]{1,0:T(2,128)S(1)} %copy-done.25), channel_id=1, source_target_pairs={{0,1},{1,0},{2,3},{3,2},{4,5},{5,4},{6,7},{7,6},{8,9},{9,8},{10,11... | collective-permute-start | bytes 12296 | tf_op jit(solution)/shard_map/ppermute | solution.py:56
  11.6 18.1 %collective-permute-start.4 = (f32[24,3072]{1,0:T(8,128)S(1)}, f32[24,3072]{1,0:T(8,128)S(1)}, u32[]{:S(2)}, u32[]{:S(2)}) collective-permute-start(f32[24,3072]{1,0:T(8,128)S(1)} %bitcast.21), channel_id=1, source_target_pairs={{0,1},{1,0},{2,3},{3,2},{4,5},{5,4},{6,7},{7,6},{8,9},{9,8},{10,11... | collective-permute-start | bytes 884744 | tf_op jit(solution)/shard_map/ppermute | solution.py:56
  11.7 18.0 %collective-permute-start.5 = (f32[24,3072]{1,0:T(8,128)S(1)}, f32[24,3072]{1,0:T(8,128)S(1)}, u32[]{:S(2)}, u32[]{:S(2)}) collective-permute-start(f32[24,3072]{1,0:T(8,128)S(1)} %bitcast.23), channel_id=1, source_target_pairs={{0,1},{1,0},{2,3},{3,2},{4,5},{5,4},{6,7},{7,6},{8,9},{9,8},{10,11... | collective-permute-start | bytes 884744 | tf_op jit(solution)/shard_map/ppermute | solution.py:56
  12.8 0.9 copy-start.24
  18.3 0.7 copy-start.5
  19.0 0.7 copy-start.7
  19.7 0.7 copy-start.9
  20.4 0.7 copy-start.11
  21.1 0.7 copy-start.13
  21.8 0.6 copy-start.15
  22.5 0.6 copy-start.17
  23.1 0.6 copy-start.19
  23.7 0.7 copy-start.26
  24.4 0.7 copy-start.28
  25.1 0.7 copy-start.30
  25.8 0.7 copy-start.32
  26.5 0.6 copy-start.34
  27.2 0.6 copy-start.36
  27.8 0.6 copy-start.38
  28.4 0.7 copy-start.40
  29.1 0.6 copy-start.42
  29.8 4.6 %copy-start.31 = (bf16[512,256]{1,0:T(8,128)(2,1)S(1)}, bf16[512,256]{1,0:T(8,128)(2,1)}, u32[]{:S(2)}) copy-start(bf16[512,256]{1,0:T(8,128)(2,1)} %copy-done.30) | copy-start | bytes 786436
  29.8 1.0 copy-start.33
  30.8 0.9 copy-start.41
  31.7 0.8 copy-start.43
  32.5 1.9 %copy-start.39 = (bf16[512,64]{1,0:T(8,128)(2,1)S(1)}, bf16[512,64]{1,0:T(8,128)(2,1)}, u32[]{:S(2)}) copy-start(bf16[512,64]{1,0:T(8,128)(2,1)} %copy-done.38) | copy-start | bytes 196612
  34.0 2.4 %copy-start.12 = (bf16[256,512]{1,0:T(8,128)(2,1)S(1)}, bf16[256,512]{1,0:T(8,128)(2,1)}, u32[]{:S(2)}) copy-start(bf16[256,512]{1,0:T(8,128)(2,1)} %copy-done.11) | copy-start | bytes 786436
  34.0 2.4 %copy-start.14 = (f32[512,64]{1,0:T(8,128)S(1)}, f32[512,64]{1,0:T(8,128)}, u32[]{:S(2)}) copy-start(f32[512,64]{1,0:T(8,128)} %copy-done.13) | copy-start | bytes 393220
  34.0 2.4 %copy-start.20 = (bf16[64,512]{1,0:T(8,128)(2,1)S(1)}, bf16[64,512]{1,0:T(8,128)(2,1)}, u32[]{:S(2)}) copy-start(bf16[64,512]{1,0:T(8,128)(2,1)} %copy-done.19) | copy-start | bytes 196612
  34.0 2.4 %collective-permute-start.7 = (f32[528,128]{1,0:T(8,128)S(1)}, f32[528,128]{1,0:T(8,128)S(1)}, u32[]{:S(2)}, u32[]{:S(2)}) collective-permute-start(f32[528,128]{1,0:T(8,128)S(1)} %get-tuple-element.125.own), channel_id=1, source_target_pairs={{0,1},{1,0},{2,3},{3,2},{4,5},{5,4},{6,7},{7,6},{8,9},{9,8},{10,11... | collective-permute-start | bytes 811016 | tf_op jit(solution)/shard_map/ppermute | solution.py:56
  35.9 2.3 %collective-permute-start.6 = (f32[528,128]{1,0:T(8,128)S(1)}, f32[528,128]{1,0:T(8,128)S(1)}, u32[]{:S(2)}, u32[]{:S(2)}) collective-permute-start(f32[528,128]{1,0:T(8,128)S(1)} %get-tuple-element.116.own), channel_id=1, source_target_pairs={{0,1},{1,0},{2,3},{3,2},{4,5},{5,4},{6,7},{7,6},{8,9},{9,8},{10,11... | collective-permute-start | bytes 811016 | tf_op jit(solution)/shard_map/ppermute | solution.py:56
  36.4 1.8 %copy-start.8 = (bf16[256,512]{1,0:T(8,128)(2,1)S(1)}, bf16[256,512]{1,0:T(8,128)(2,1)}, u32[]{:S(2)}) copy-start(bf16[256,512]{1,0:T(8,128)(2,1)} %copy-done.7) | copy-start | bytes 786436
  36.4 1.8 %copy-start.10 = (f32[512,64]{1,0:T(8,128)S(1)}, f32[512,64]{1,0:T(8,128)}, u32[]{:S(2)}) copy-start(f32[512,64]{1,0:T(8,128)} %copy-done.9) | copy-start | bytes 393220
  36.4 1.8 %copy-start.18 = (bf16[64,512]{1,0:T(8,128)(2,1)S(1)}, bf16[64,512]{1,0:T(8,128)(2,1)}, u32[]{:S(2)}) copy-start(bf16[64,512]{1,0:T(8,128)(2,1)} %copy-done.17) | copy-start | bytes 196612
  62.6 18.4 %copy-start.29 = (bf16[512,256]{1,0:T(8,128)(2,1)S(1)}, bf16[512,256]{1,0:T(8,128)(2,1)}, u32[]{:S(2)}) copy-start(bf16[512,256]{1,0:T(8,128)(2,1)} %copy-done.28) | copy-start | bytes 786436
  62.6 18.4 %copy-start.37 = (bf16[512,64]{1,0:T(8,128)(2,1)S(1)}, bf16[512,64]{1,0:T(8,128)(2,1)}, u32[]{:S(2)}) copy-start(bf16[512,64]{1,0:T(8,128)(2,1)} %copy-done.36) | copy-start | bytes 196612
  81.0 4.0 %copy-start.27 = (bf16[512,256]{1,0:T(8,128)(2,1)S(1)}, bf16[512,256]{1,0:T(8,128)(2,1)}, u32[]{:S(2)}) copy-start(bf16[512,256]{1,0:T(8,128)(2,1)} %copy-done.26) | copy-start | bytes 786436
  81.0 4.0 %copy-start.35 = (bf16[512,64]{1,0:T(8,128)(2,1)S(1)}, bf16[512,64]{1,0:T(8,128)(2,1)}, u32[]{:S(2)}) copy-start(bf16[512,64]{1,0:T(8,128)(2,1)} %copy-done.34) | copy-start | bytes 196612
  82.5 4.3 %copy-start.6 = (f32[512,64]{1,0:T(8,128)S(1)}, f32[512,64]{1,0:T(8,128)}, u32[]{:S(2)}) copy-start(f32[512,64]{1,0:T(8,128)} %copy-done.5) | copy-start | bytes 393220
  82.5 4.3 %copy-start.16 = (bf16[64,512]{1,0:T(8,128)(2,1)S(1)}, bf16[64,512]{1,0:T(8,128)(2,1)}, u32[]{:S(2)}) copy-start(bf16[64,512]{1,0:T(8,128)(2,1)} %copy-done.15) | copy-start | bytes 196612
  82.5 4.3 %collective-permute-start.9 = (f32[528,128]{1,0:T(8,128)S(1)}, f32[528,128]{1,0:T(8,128)S(1)}, u32[]{:S(2)}, u32[]{:S(2)}) collective-permute-start(f32[528,128]{1,0:T(8,128)S(1)} %get-tuple-element.143.own), channel_id=1, source_target_pairs={{0,1},{1,0},{2,3},{3,2},{4,5},{5,4},{6,7},{7,6},{8,9},{9,8},{10,11... | collective-permute-start | bytes 811016 | tf_op jit(solution)/shard_map/ppermute | solution.py:56
  86.4 2.1 %collective-permute-start.8 = (f32[528,128]{1,0:T(8,128)S(1)}, f32[528,128]{1,0:T(8,128)S(1)}, u32[]{:S(2)}, u32[]{:S(2)}) collective-permute-start(f32[528,128]{1,0:T(8,128)S(1)} %get-tuple-element.135.own), channel_id=1, source_target_pairs={{0,1},{1,0},{2,3},{3,2},{4,5},{5,4},{6,7},{7,6},{8,9},{9,8},{10,11... | collective-permute-start | bytes 811016 | tf_op jit(solution)/shard_map/ppermute | solution.py:56
  110.6 38.2 %copy-start.1 = (f32[24,3072]{1,0:T(8,128)S(1)}, f32[24,3072]{1,0:T(8,128)}, u32[]{:S(2)}) copy-start(f32[24,3072]{1,0:T(8,128)} %params.1) | copy-start | bytes 884740
  110.6 38.2 %copy-start.2 = (f32[24,3072]{1,0:T(8,128)S(1)}, f32[24,3072]{1,0:T(8,128)}, u32[]{:S(2)}) copy-start(f32[24,3072]{1,0:T(8,128)} %momentum.1) | copy-start | bytes 884740
  110.6 19.7 %all-to-all-start.4 = ((bf16[16,16,384]{2,1,0:T(8,128)(2,1)}), bf16[16,16,384]{2,1,0:T(8,128)(2,1)S(1)}, u32[]{:S(2)}, u32[]{:S(2)}) async-start(bf16[16,16,384]{2,1,0:T(8,128)(2,1)} %get-tuple-element.152), calls=%async_computation.4 | async-start | bytes 393216 | tf_op jit(solution)/shard_map/all_to_all | solution.py:486
  120.6 3.0 %collective-permute-start.10 = (f32[48,1536]{1,0:T(8,128)S(1)}, f32[48,1536]{1,0:T(8,128)S(1)}, u32[]{:S(2)}, u32[]{:S(2)}) collective-permute-start(f32[48,1536]{1,0:T(8,128)S(1)} %get-tuple-element.153.mean), channel_id=1, source_target_pairs={{0,1},{1,0},{2,3},{3,2},{4,5},{5,4},{6,7},{7,6},{8,9},{9,8},{10,11... | collective-permute-start | bytes 884744 | tf_op jit(solution)/shard_map/ppermute | solution.py:56
  122.4 1.6 %collective-permute-start.11 = (f32[48,1536]{1,0:T(8,128)S(1)}, f32[48,1536]{1,0:T(8,128)S(1)}, u32[]{:S(2)}, u32[]{:S(2)}) collective-permute-start(f32[48,1536]{1,0:T(8,128)S(1)} %get-tuple-element.154.square), channel_id=1, source_target_pairs={{0,1},{1,0},{2,3},{3,2},{4,5},{5,4},{6,7},{7,6},{8,9},{9,8},{10,11... | collective-permute-start | bytes 884744 | tf_op jit(solution)/shard_map/ppermute | solution.py:56
  143.7 5.1 %collective-permute-start.12 = (bf16[16,16,384]{2,1,0:T(8,128)(2,1)S(1)}, bf16[16,16,384]{2,1,0:T(8,128)(2,1)S(1)}, u32[]{:S(2)}, u32[]{:S(2)}) collective-permute-start(bf16[16,16,384]{2,1,0:T(8,128)(2,1)S(1)} %all_to_all.33.own), channel_id=1, source_target_pairs={{0,1},{1,0},{2,3},{3,2},{4,5},{5,4},{6,7},{7,6},{8,9},{9,8},{10,11... | collective-permute-start | bytes 589832 | tf_op jit(solution)/shard_map/ppermute | solution.py:56

commit v4 on v3

--- a/solution.py
+++ b/solution.py
@@ -33,6 +33,7 @@
 VMEM = pl.BlockSpec(memory_space=pltpu.VMEM)
 SMEM = pl.BlockSpec(memory_space=pltpu.SMEM)
 TRANSPOSED = (((1,), (1,)), ((), ()))
+BOTH_TRANSPOSED = (((0,), (0,)), ((), ()))
 
 
 def local_call(kernel, name, args, outs, scratch=(), scalars=(), flops=0, hbm_outs=False):
@@ -120,17 +121,25 @@
     return (weights[time_end:, :].astype(F32) * factor[0:1, :]).astype(BF16)
 
 
-def forward_kernel(tokens, embed, weights, factor, shift, hid, slope, stats, pre_buf, in_buf, square):
-    rows_here, channels = tokens.shape
-    time_end = channels + embed.shape[1]
+def forward_kernel(inputs_t, weights, factor, shift, hid, slope, stats, pre_buf, in_buf, square):
+    time_end, rows_here = inputs_t.shape
+    channels = weights.shape[0] - time_end
     square[...] = jnp.zeros_like(square)
     for index in range(weights.shape[1] // FWD_COLUMNS):
         slot = index % 2
         cols = pl.ds(index * FWD_COLUMNS, FWD_COLUMNS)
-        pre_buf[slot] = jnp.dot(
-            embed[...], weights[channels:time_end, cols], preferred_element_type=F32
+        pre_buf[slot] = lax.dot_general(
+            inputs_t[channels:, :],
+            weights[channels:time_end, cols],
+            BOTH_TRANSPOSED,
+            preferred_element_type=F32,
         )
-        in_buf[slot] = jnp.dot(tokens[...], weights[0:channels, cols], preferred_element_type=F32)
+        in_buf[slot] = lax.dot_general(
+            inputs_t[0:channels, :],
+            weights[0:channels, cols],
+            BOTH_TRANSPOSED,
+            preferred_element_type=F32,
+        )
         for start in range(0, rows_here, ROW_CHUNK):
             rows = pl.ds(start, ROW_CHUNK)
             half_pre = pre_buf[slot, rows, :]
@@ -157,24 +166,24 @@
     stats[rows_here:, :] = jnp.concatenate([bias, jnp.zeros_like(bias)], axis=1)
 
 
-def forward(tokens, embed, weights, factor, shift):
-    rows, columns = tokens.shape[0], weights.shape[1]
+def forward(inputs_t, weights, factor, shift):
+    rows, columns = inputs_t.shape[1], weights.shape[1]
     outs = [((rows, columns), BF16)] * 2 + [((rows + shift.shape[0], LANES), F32)]
     scratch = [pltpu.VMEM((2, rows, FWD_COLUMNS), F32)] * 2 + [pltpu.VMEM((rows, LANES), F32)]
     flops = 2 * rows * columns * weights.shape[0]
-    args = (tokens, embed, weights, factor, shift)
+    args = (inputs_t, weights, factor, shift)
     return local_call(forward_kernel, "forward", args, outs, scratch, flops=flops)
 
 
 def make_backward_kernel(model_width, total_rows, added):
     def backward_kernel(
-        own, got, target, hid, slope, weights, factor, shift, tokens_t, embed_t, *rest
+        own, got, target_t, hid, slope, weights, factor, shift, inputs_t, *rest
     ):
         before = rest[0] if added else None
         out, mod_buf, hid_buf, pre_buf, pull = rest[1:] if added else rest
         root = 1.0 / math.sqrt(model_width)
-        rows_here, channels = target.shape
-        time_end = channels + embed_t.shape[0]
+        channels, rows_here = target_t.shape
+        time_end = inputs_t.shape[0]
         columns = out.shape[1]
 
         both = own[0:rows_here, :] + got[0:rows_here, :]
@@ -183,7 +192,7 @@
         terms = own[rows_here:, 0:channels] + got[rows_here:, 0:channels]
         bias = jnp.sum(terms, axis=0, keepdims=True)
         output = (inverse * raw + bias) * root
-        out_grad = (2.0 / (total_rows * channels)) * (output - target[...])
+        out_grad = (2.0 / (total_rows * channels)) * (output - target_t[...].T)
         grad = (out_grad * (inverse * root)).astype(BF16)
         wide = grad.astype(F32)
         grad_t = wide.T.astype(BF16)
@@ -208,11 +217,11 @@
 
         put(
             slice(0, channels),
-            jnp.dot(tokens_t[...], hid_buf[...], preferred_element_type=F32),
+            jnp.dot(inputs_t[0:channels, :], hid_buf[...], preferred_element_type=F32),
         )
         put(
             slice(channels, time_end),
-            jnp.dot(embed_t[...], pre_buf[...], preferred_element_type=F32),
+            jnp.dot(inputs_t[channels:, :], pre_buf[...], preferred_element_type=F32),
         )
         grad_out = jnp.dot(grad_t, hid[...], preferred_element_type=F32)
         put(
@@ -223,7 +232,7 @@
     return backward_kernel
 
 
-def backward(stats, target, state, weights, factor, shift, tokens_t, embed_t, before, sizes):
+def backward(stats, target_t, state, weights, factor, shift, inputs_t, before, sizes):
     rows, columns = state[0].shape
     scratch = [
         pltpu.VMEM((rows, columns), F32),
@@ -231,19 +240,19 @@
         pltpu.VMEM((rows, columns), BF16),
         pltpu.VMEM((rows, LANES), F32),
     ]
-    flops = 2 * rows * columns * (weights.shape[0] + tokens_t.shape[0])
-    args = (*stats, target, *state, weights, factor, shift, tokens_t, embed_t, *before)
+    flops = 2 * rows * columns * (weights.shape[0] + target_t.shape[0])
+    args = (*stats, target_t, *state, weights, factor, shift, inputs_t, *before)
     outs = [(weights.shape, BF16 if before else F32)]
     kernel = make_backward_kernel(*sizes, bool(before))
     return local_call(kernel, "backward", args, outs, scratch, flops=flops)[0]
 
 
 def prepare_kernel(
-    core, fragment, latents, latents_got, noise, noise_got, levels, levels_got, modulation, *rest
+    core, latents, latents_got, noise, noise_got, levels, levels_got, modulation, *rest
 ):
     outs, (latent_buf, noise_buf, level_buf) = rest[:-3], rest[-3:]
     steps, channels, tokens = latents.shape
-    half_width = outs[1].shape[1] // 2
+    half_width = (outs[0].shape[0] - channels) // 2
     pairs = ((latents, latents_got), (noise, noise_got), (levels, levels_got))
     for buffer, (own, got) in zip((latent_buf, noise_buf, level_buf), pairs):
 
@@ -260,25 +269,22 @@
     place = 0
     for step in range(steps):
         for owner in range(CORES):
-            token_rows, embed_rows, token_cols, embed_cols, target = outs[place : place + 5]
-            place += 5
+            inputs_t, target_t = outs[place : place + 2]
+            place += 2
             level = (level_buf[owner, step : step + 1, :].astype(F32) + 0.5) / LEVELS
             latent = latent_buf[owner, step].astype(F32)
             draw = noise_buf[owner, step].astype(F32)
             noised = ((1.0 - level) * latent + level * draw).astype(BF16).astype(F32)
             noised = noised * (1.0 / math.sqrt(channels))
-            token_cols[...] = noised.astype(BF16)
-            token_rows[...] = noised.T.astype(BF16)
-            target[...] = (draw - latent).T
+            inputs_t[0:channels, :] = noised.astype(BF16)
+            target_t[...] = draw - latent
             order = lax.broadcasted_iota(jnp.int32, (half_width, tokens), 0).astype(F32)
             angles = (1000.0 * level) * jnp.exp(-math.log(10000.0) * order / half_width)
             root = 0.5 / math.sqrt(2 * half_width)
             for part, wave in enumerate((jnp.cos(angles), jnp.sin(angles))):
                 wave = wave.astype(BF16).astype(F32) * root
-                here = pl.ds(part * half_width, half_width)
-                embed_cols[here, :] = wave.astype(BF16)
-                embed_rows[:, here] = wave.T.astype(BF16)
-    rows = modulation[fragment[0]]
+                inputs_t[pl.ds(channels + part * half_width, half_width), :] = wave.astype(BF16)
+    rows = modulation[...]
     half = rows.shape[1] // CORES
     factor, shift, terms = outs[place:]
 
@@ -296,15 +302,12 @@
             terms[...] = split.astype(BF16)
 
 
-def prepare(core, fragment, latents, noise_draw, timesteps, modulation, time_width, width):
+def prepare(core, latents, noise_draw, timesteps, mod_rows, time_width, width):
     steps, tokens, channels = latents.shape
-    half = modulation.shape[2] // CORES
+    half = mod_rows.shape[1] // CORES
     outs = [
-        ((tokens, channels), BF16),
-        ((tokens, time_width), BF16),
-        ((channels, tokens), BF16),
-        ((time_width, tokens), BF16),
-        ((tokens, channels), F32),
+        ((channels + time_width, tokens), BF16),
+        ((channels, tokens), F32),
     ] * (steps * CORES) + [((1, half), F32), ((1, half), F32), ((16, half), BF16)]
     args = []
     scratch = []
@@ -314,13 +317,13 @@
     results = local_call(
         prepare_kernel,
         "prepare",
-        (*args, modulation),
+        (*args, mod_rows),
         outs,
         scratch,
-        scalars=(core, fragment),
+        scalars=(core,),
         flops=2**32,
     )
-    sets = [results[5 * i : 5 * i + 5] for i in range(steps * CORES)]
+    sets = [results[2 * i : 2 * i + 2] for i in range(steps * CORES)]
     return [sets[CORES * s : CORES * (s + 1)] for s in range(steps)], results[-3:]
 
 
@@ -433,8 +436,9 @@
     )
     gathered = chip_exchange(copies, width)
 
+    mod_rows = lax.dynamic_index_in_dim(modulation, fragment[0], 0, keepdims=False)
     prepared, mods = prepare(
-        core_arg, fragment, latents, noise_draw, timesteps, modulation, time_width, width
+        core_arg, latents, noise_draw, timesteps, mod_rows, time_width, width
     )
     params = start
     mean, square = local_call(
@@ -458,14 +462,14 @@
     for step in range(STEPS):
         weights = gathered.reshape(chips * pair_shape[0], half)
         states = []
-        for tokens, embed, _, _, _ in prepared[step]:
-            hid, slope, stats = forward(tokens, embed, weights, factor, terms)
+        for inputs_t, _ in prepared[step]:
+            hid, slope, stats = forward(inputs_t, weights, factor, terms)
             states.append(((hid, slope), (stats, core_swap(stats, width))))
         gradient = ()
-        for (state, stats), (_, _, tokens_t, embed_t, target) in zip(states, prepared[step]):
+        for (state, stats), (inputs_t, target_t) in zip(states, prepared[step]):
             gradient = (
                 backward(
-                    stats, target, state, weights, factor, shift, tokens_t, embed_t, gradient, sizes
+                    stats, target_t, state, weights, factor, shift, inputs_t, gradient, sizes
                 ),
             )
         pair_sum = gradient[0]

time: 150 us -> 146 us (0.973)
  local copies, waits for them, and re-layouts: 16 us -> 9.99 us
  Pallas kernels: 22.3 us -> 24.1 us
    unnamed x88 -> x52, local copies, waits for them, and re-layouts: 16 us -> 9.98 us
    pallas_call x17, Pallas kernels: 22.3 us -> 24.1 us  [local_call(): pl.pallas_call(kernel, in_specs=specs, out_specs=[VMEM] * len(outs), out_...]
  transfers between devices with their start and end apart: 15 -> 15, of which waited for: 5 -> 5; matrix products, arithmetic and copies ran while one was open for 0% -> 0% of each run, Pallas kernels for 8% -> 9%
where the time goes in v4:
time: 146 us; the launch traced here: 145 us
  blocking collectives  72.1 us (49%)
  starting transfers between devices  29.1 us (20%)
  Pallas kernels  24.1 us (17%)
  local copies, waits for them, and re-layouts  9.99 us (7%)
  waiting for transfers between devices  8.45 us (6%)
  between operations  1.62 us (1%)
    all_to_all x3, blocking collectives, chip_exchange(): return lax.all_to_all(blocks, 'fsdp', 0, 0, axis_index_groups=groups)  58.8 us
    pallas_call x17, Pallas kernels, local_call(): pl.pallas_call(kernel, in_specs=specs, out_specs=[VMEM] * len(outs), out_...  24.1 us
    ppermute x13, starting transfers between devices, core_swap(): return lax.ppermute(values, 'fsdp', [(i, i ^ 1) for i in range(width)])  15.3 us
    all_to_all x1, blocking collectives, on_device(): strips = lax.all_to_all(strips, 'replica', 0, 0)  13.3 us
    unnamed x52, local copies, waits for them, and re-layouts  9.98 us
    all_to_all x1, starting transfers between devices, on_device(): strips = lax.all_to_all(strips, 'replica', 0, 0)  9.98 us
    all_to_all x1, waiting for transfers between devices, on_device(): strips = lax.all_to_all(strips, 'replica', 0, 0)  5.45 us
    all_to_all x1, starting transfers between devices, chip_exchange(): return lax.all_to_all(blocks, 'fsdp', 0, 0, axis_index_groups=groups)  3.81 us
  transfers between devices with their start and end apart: 15, of which 5 were waited for; matrix products, arithmetic and copies ran while one was open for 0% of the time, Pallas kernels for 9%

profile of v4, /device:TPU:1, one launch (start us, length us, event | category | flops | bytes accessed | tf_op | source)
XLA Modules:
  0.0 145.4 jit_solution(6243764437012498206)
XLA Ops:
  0.6 0.0 copy-start
  0.6 3.3 %collective-permute-start = (f32[24,3072]{1,0:T(8,128)}, f32[24,3072]{1,0:T(8,128)S(1)}, u32[]{:S(2)}, u32[]{:S(2)}) collective-permute-start(f32[24,3072]{1,0:T(8,128)} %params.1), channel_id=1, source_target_pairs={{0,1},{1,0},{2,3},{3,2},{4,5},{5,4},{6,7},{7,6},{8,9},{9,8},{10,11... | collective-permute-start | bytes 884744 | tf_op jit(solution)/shard_map/ppermute | solution.py:57
  4.0 1.0 copy-done.1
  5.0 0.0 copy-start.25
  5.0 0.0 copy-start.17
  5.0 0.0 copy-start.19
  5.0 0.0 copy-start.4
  5.0 0.4 collective-permute-done.got
  5.4 1.2 start.1
  6.6 3.8 %all-to-all-start = ((bf16[8,48,1536]{2,1,0:T(8,128)(2,1)}), bf16[8,48,1536]{2,1,0:T(8,128)(2,1)S(1)}, u32[]{:S(2)}, u32[]{:S(2)}) async-start(bf16[8,48,1536]{2,1,0:T(8,128)(2,1)} %get-tuple-element.59), calls=%async_computation | async-start | bytes 2359296 | tf_op jit(solution)/shard_map/all_to_all | solution.py:62
  10.4 0.7 collective-permute-start.3
  11.1 0.1 collective-permute-start.1
  11.2 0.4 collective-permute-start.2
  11.6 0.1 collective-permute-start.4
  11.7 0.4 collective-permute-start.5
  12.8 0.0 collective-permute-done.1.latents_got
  12.9 0.0 copy-start.21
  12.9 0.6 copy-done.21
  13.5 0.7 copy-done.23
  14.2 0.9 copy-done.18
  15.1 0.9 copy-done.20
  16.0 0.9 copy-done.22
  16.9 0.9 copy-done.24
  17.8 4.2 %prepare.1 = (bf16[320,512]{1,0:T(8,128)(2,1)S(1)}, f32[64,512]{1,0:T(8,128)S(1)}, bf16[320,512]{1,0:T(8,128)(2,1)S(1)}, f32[64,512]{1,0:T(8,128)S(1)}, bf16[320...) custom-call(s32[1]{0:T(128)} %bitcast.core, ...), custom_call_target="tpu_custom_call" | custom-call | flops 4294967296 | bytes 3813376 | tf_op jit(solution)/shard_map/prepare/pallas_call | solution.py:44
  22.0 0.6 copy-done.9
  22.7 0.7 copy-done.11
  23.3 0.7 copy-done.13
  24.0 0.7 copy-done.15
  24.7 1.2 moments.1
  25.8 0.0 copy-start.5
  25.9 0.7 copy-done.5
  26.6 0.7 copy-done.7
  27.3 1.6 %forward.5 = (bf16[512,1536]{1,0:T(8,128)(2,1)S(1)}, bf16[512,1536]{1,0:T(8,128)(2,1)S(1)}, f32[528,128]{1,0:T(8,128)S(1)}) custom-call(bf16[320,512]{1,0:T(8,128)(2,1)S(1)} %get-tuple-element.83.inputs_t, bf16[384,1536]{1,0:T(8,128)(2,1)S(1)} %bitcast.17, f32[1,1536]{1,0:T(1,128)S(1)} %get-tuple-element.76.factor, bf16[16,1536]{1,0:T(8,128)(2,1)S(1)} %get-tuple-element.77.shift), custom_call_target="tpu_custom_call" | custom-call | flops 603979776 | bytes 8124416 | tf_op jit(solution)/shard_map/forward/pallas_call | solution.py:44
  28.9 0.0 copy-start.16
  28.9 1.5 %collective-permute-start.7 = (f32[528,128]{1,0:T(8,128)S(1)}, f32[528,128]{1,0:T(8,128)S(1)}, u32[]{:S(2)}, u32[]{:S(2)}) collective-permute-start(f32[528,128]{1,0:T(8,128)S(1)} %get-tuple-element.84.own), channel_id=1, source_target_pairs={{0,1},{1,0},{2,3},{3,2},{4,5},{5,4},{6,7},{7,6},{8,9},{9,8},{10,11... | collective-permute-start | bytes 811016 | tf_op jit(solution)/shard_map/ppermute | solution.py:57
  30.3 1.6 %forward.4 = (bf16[512,1536]{1,0:T(8,128)(2,1)S(1)}, bf16[512,1536]{1,0:T(8,128)(2,1)S(1)}, f32[528,128]{1,0:T(8,128)S(1)}) custom-call(bf16[320,512]{1,0:T(8,128)(2,1)S(1)} %get-tuple-element.74.inputs_t, bf16[384,1536]{1,0:T(8,128)(2,1)S(1)} %bitcast.18, f32[1,1536]{1,0:T(1,128)S(1)} %get-tuple-element.76.factor, bf16[16,1536]{1,0:T(8,128)(2,1)S(1)} %get-tuple-element.77.shift), custom_call_target="tpu_custom_call" | custom-call | flops 603979776 | bytes 8124416 | tf_op jit(solution)/shard_map/forward/pallas_call | solution.py:44
  31.9 0.1 collective-permute-start.6
  32.1 0.0 copy-start.14
  32.1 1.9 %backward.4.rest_0_ = f32[384,1536]{1,0:T(8,128)S(1)} custom-call(f32[528,128]{1,0:T(8,128)S(1)} %get-tuple-element.84.own, f32[528,128]{1,0:T(8,128)S(1)} %collective-permute-done.7.got, f32[64,512]{1,0:T(8,128)S(1)} %copy-done.16, bf16[512,1536]{1,0:T(8,128)(2,1)S(1)} %get-tuple-element.86.hid, bf16[512,1536]{1,0:T(8,128)(2,1)S(1)} %get-tuple-element.87.slope, ...), custom_call_target="tpu_custom_call" | custom-call | flops 704643072 | bytes 7696384 | tf_op jit(solution)/shard_map/backward/pallas_call | solution.py:44
  34.0 2.0 %backward.5 = bf16[384,1536]{1,0:T(8,128)(2,1)S(1)} custom-call(f32[528,128]{1,0:T(8,128)S(1)} %get-tuple-element.78.own, f32[528,128]{1,0:T(8,128)S(1)} %collective-permute-done.6.got, f32[64,512]{1,0:T(8,128)S(1)} %copy-done.14, bf16[512,1536]{1,0:T(8,128)(2,1)S(1)} %get-tuple-element.80.hid, bf16[512,1536]{1,0:T(8,128)(2,1)S(1)} %get-tuple-element.81.slope, ...), custom_call_target="tpu_custom_call" | custom-call | flops 704643072 | bytes 10055680 | tf_op jit(solution)/shard_map/backward/pallas_call | solution.py:44
  36.0 0.0 copy-start.6
  36.0 0.0 copy-start.8
  36.0 21.4 %all_to_all.30.blocks = bf16[8,48,1536]{2,1,0:T(8,128)(2,1)S(1)} all-to-all(bf16[8,48,1536]{2,1,0:T(8,128)(2,1)S(1)} %bitcast.26), channel_id=1, replica_groups={{0,2,4,6,8,10,12,14},{1,3,5,7,9,11,13,15},{16,18,20,22,24,26,28,30},{17..., dimensions={0} | all-to-all | bytes 2359296 | tf_op jit(solution)/shard_map/all_to_all | solution.py:62
  57.5 0.5 update.1
  57.9 18.2 %all_to_all.31 = bf16[8,48,1536]{2,1,0:T(8,128)(2,1)S(1)} all-to-all(bf16[8,48,1536]{2,1,0:T(8,128)(2,1)S(1)} %get-tuple-element.91), channel_id=1, replica_groups={{0,2,4,6,8,10,12,14},{1,3,5,7,9,11,13,15},{16,18,20,22,24,26,28,30},{17..., dimensions={0} | all-to-all | bytes 2359296 | tf_op jit(solution)/shard_map/all_to_all | solution.py:62
  76.2 1.6 %forward.7 = (bf16[512,1536]{1,0:T(8,128)(2,1)S(1)}, bf16[512,1536]{1,0:T(8,128)(2,1)S(1)}, f32[528,128]{1,0:T(8,128)S(1)}) custom-call(bf16[320,512]{1,0:T(8,128)(2,1)S(1)} %get-tuple-element.96.inputs_t, bf16[384,1536]{1,0:T(8,128)(2,1)S(1)} %bitcast.21, f32[1,1536]{1,0:T(1,128)S(1)} %get-tuple-element.76.factor, bf16[16,1536]{1,0:T(8,128)(2,1)S(1)} %get-tuple-element.77.shift), custom_call_target="tpu_custom_call" | custom-call | flops 603979776 | bytes 8124416 | tf_op jit(solution)/shard_map/forward/pallas_call | solution.py:44
  77.8 2.4 %collective-permute-start.9 = (f32[528,128]{1,0:T(8,128)S(1)}, f32[528,128]{1,0:T(8,128)S(1)}, u32[]{:S(2)}, u32[]{:S(2)}) collective-permute-start(f32[528,128]{1,0:T(8,128)S(1)} %get-tuple-element.97.own), channel_id=1, source_target_pairs={{0,1},{1,0},{2,3},{3,2},{4,5},{5,4},{6,7},{7,6},{8,9},{9,8},{10,11... | collective-permute-start | bytes 811016 | tf_op jit(solution)/shard_map/ppermute | solution.py:57
  80.2 1.6 %forward.6 = (bf16[512,1536]{1,0:T(8,128)(2,1)S(1)}, bf16[512,1536]{1,0:T(8,128)(2,1)S(1)}, f32[528,128]{1,0:T(8,128)S(1)}) custom-call(bf16[320,512]{1,0:T(8,128)(2,1)S(1)} %get-tuple-element.73.inputs_t, bf16[384,1536]{1,0:T(8,128)(2,1)S(1)} %bitcast.22, f32[1,1536]{1,0:T(1,128)S(1)} %get-tuple-element.76.factor, bf16[16,1536]{1,0:T(8,128)(2,1)S(1)} %get-tuple-element.77.shift), custom_call_target="tpu_custom_call" | custom-call | flops 603979776 | bytes 8124416 | tf_op jit(solution)/shard_map/forward/pallas_call | solution.py:44
  81.8 0.3 collective-permute-start.8
  82.1 1.9 %backward.6.rest_0_ = f32[384,1536]{1,0:T(8,128)S(1)} custom-call(f32[528,128]{1,0:T(8,128)S(1)} %get-tuple-element.97.own, f32[528,128]{1,0:T(8,128)S(1)} %collective-permute-done.9.got, f32[64,512]{1,0:T(8,128)S(1)} %copy-done.12, bf16[512,1536]{1,0:T(8,128)(2,1)S(1)} %get-tuple-element.99.hid, bf16[512,1536]{1,0:T(8,128)(2,1)S(1)} %get-tuple-element.100.slope, ...), custom_call_target="tpu_custom_call" | custom-call | flops 704643072 | bytes 7696384 | tf_op jit(solution)/shard_map/backward/pallas_call | solution.py:44
  84.1 2.0 %backward.7 = bf16[384,1536]{1,0:T(8,128)(2,1)S(1)} custom-call(f32[528,128]{1,0:T(8,128)S(1)} %get-tuple-element.92.own, f32[528,128]{1,0:T(8,128)S(1)} %collective-permute-done.8.got, f32[64,512]{1,0:T(8,128)S(1)} %copy-done.10, bf16[512,1536]{1,0:T(8,128)(2,1)S(1)} %get-tuple-element.94.hid, bf16[512,1536]{1,0:T(8,128)(2,1)S(1)} %get-tuple-element.95.slope, ...), custom_call_target="tpu_custom_call" | custom-call | flops 704643072 | bytes 10055680 | tf_op jit(solution)/shard_map/backward/pallas_call | solution.py:44
  86.1 19.1 %all_to_all.32.blocks = bf16[8,48,1536]{2,1,0:T(8,128)(2,1)S(1)} all-to-all(bf16[8,48,1536]{2,1,0:T(8,128)(2,1)S(1)} %bitcast.25), channel_id=1, replica_groups={{0,2,4,6,8,10,12,14},{1,3,5,7,9,11,13,15},{16,18,20,22,24,26,28,30},{17..., dimensions={0} | all-to-all | bytes 2359296 | tf_op jit(solution)/shard_map/all_to_all | solution.py:62
  105.2 1.1 update_last.1
  106.3 10.0 %all-to-all-start.4 = ((bf16[16,16,384]{2,1,0:T(8,128)(2,1)}), bf16[16,16,384]{2,1,0:T(8,128)(2,1)S(1)}, u32[]{:S(2)}, u32[]{:S(2)}) async-start(bf16[16,16,384]{2,1,0:T(8,128)(2,1)} %get-tuple-element.104), calls=%async_computation.4 | async-start | bytes 393216 | tf_op jit(solution)/shard_map/all_to_all | solution.py:490
  116.3 1.8 %collective-permute-start.10 = (f32[48,1536]{1,0:T(8,128)S(1)}, f32[48,1536]{1,0:T(8,128)S(1)}, u32[]{:S(2)}, u32[]{:S(2)}) collective-permute-start(f32[48,1536]{1,0:T(8,128)S(1)} %get-tuple-element.105.mean), channel_id=1, source_target_pairs={{0,1},{1,0},{2,3},{3,2},{4,5},{5,4},{6,7},{7,6},{8,9},{9,8},{10,11... | collective-permute-start | bytes 884744 | tf_op jit(solution)/shard_map/ppermute | solution.py:57
  118.1 0.1 collective-permute-start.11
  118.2 1.1 collective-permute-done.10.mean_got
  119.3 0.4 collective-permute-done.11.square_got
  119.7 0.9 unpair.1
  120.6 5.5 %all-to-all-done.4.strips = bf16[16,16,384]{2,1,0:T(8,128)(2,1)S(1)} async-done(((bf16[16,16,384]{2,1,0:T(8,128)(2,1)}), bf16[16,16,384]{2,1,0:T(8,128)(2,1)S(1)}, u32[]{:S(2)}, u32[]{:S(2)}) %all-to-all-start.4) | async-done | bytes 196640 | tf_op jit(solution)/shard_map/all_to_all | solution.py:490
  126.1 13.3 %all_to_all.33.own = bf16[16,16,384]{2,1,0:T(8,128)(2,1)S(1)} all-to-all(bf16[16,16,384]{2,1,0:T(8,128)(2,1)S(1)} %strip_sum.1), channel_id=1, replica_groups=mesh['replica'=16,'fsdp'=16] {'replica'}, dimensions={0} | all-to-all | bytes 393216 | tf_op jit(solution)/shard_map/all_to_all | solution.py:501
  139.4 4.0 %collective-permute-start.12 = (bf16[16,16,384]{2,1,0:T(8,128)(2,1)S(1)}, bf16[16,16,384]{2,1,0:T(8,128)(2,1)S(1)}, u32[]{:S(2)}, u32[]{:S(2)}) collective-permute-start(bf16[16,16,384]{2,1,0:T(8,128)(2,1)S(1)} %all_to_all.33.own), channel_id=1, source_target_pairs={{0,1},{1,0},{2,3},{3,2},{4,5},{5,4},{6,7},{7,6},{8,9},{9,8},{10,11... | collective-permute-start | bytes 589832 | tf_op jit(solution)/shard_map/ppermute | solution.py:57
  143.4 1.1 collective-permute-done.12.got
  144.4 0.9 outer.1
  (40 shorter events, 0.1 us)
Async XLA Ops:
  0.6 12.2 %copy-start = (f32[15,2,3072]{2,1,0:T(2,128)S(1)}, f32[15,2,3072]{2,1,0:T(2,128)}, u32[]{:S(2)}) copy-start(f32[15,2,3072]{2,1,0:T(2,128)} %param.17) | copy-start | bytes 1105924
  0.6 4.7 %collective-permute-start = (f32[24,3072]{1,0:T(8,128)}, f32[24,3072]{1,0:T(8,128)S(1)}, u32[]{:S(2)}, u32[]{:S(2)}) collective-permute-start(f32[24,3072]{1,0:T(8,128)} %params.1), channel_id=1, source_target_pairs={{0,1},{1,0},{2,3},{3,2},{4,5},{5,4},{6,7},{7,6},{8,9},{9,8},{10,11... | collective-permute-start | bytes 884744 | tf_op jit(solution)/shard_map/ppermute | solution.py:57
  4.0 1.0 copy-start.1
  5.0 5.4 %copy-start.25 = (s32[2,512]{1,0:T(2,128)S(1)}, s32[2,512]{1,0:T(2,128)}, u32[]{:S(2)}) copy-start(s32[2,512]{1,0:T(2,128)} %levels.1) | copy-start | bytes 12292
  5.0 6.2 %copy-start.17 = (bf16[2,512,64]{1,2,0:T(8,128)(2,1)S(1)}, bf16[2,512,64]{1,2,0:T(8,128)(2,1)}, u32[]{:S(2)}) copy-start(bf16[2,512,64]{1,2,0:T(8,128)(2,1)} %param.13) | copy-start | bytes 393220
  5.0 6.2 %copy-start.19 = (bf16[2,512,64]{1,2,0:T(8,128)(2,1)S(1)}, bf16[2,512,64]{1,2,0:T(8,128)(2,1)}, u32[]{:S(2)}) copy-start(bf16[2,512,64]{1,2,0:T(8,128)(2,1)} %param.14) | copy-start | bytes 393220
  5.0 6.6 %copy-start.4 = (f32[1,24,3072]{2,1,0:T(8,128)S(1)}, f32[1,24,3072]{2,1,0:T(8,128)}, u32[]{:S(2)}) copy-start(f32[1,24,3072]{2,1,0:T(8,128)} %param.11) | copy-start | bytes 884740
  6.6 20.7 %all-to-all-start = ((bf16[8,48,1536]{2,1,0:T(8,128)(2,1)}), bf16[8,48,1536]{2,1,0:T(8,128)(2,1)S(1)}, u32[]{:S(2)}, u32[]{:S(2)}) async-start(bf16[8,48,1536]{2,1,0:T(8,128)(2,1)} %get-tuple-element.59), calls=%async_computation | async-start | bytes 2359296 | tf_op jit(solution)/shard_map/all_to_all | solution.py:62
  10.4 2.5 %collective-permute-start.3 = (s32[2,512]{1,0:T(2,128)S(1)}, s32[2,512]{1,0:T(2,128)S(1)}, u32[]{:S(2)}, u32[]{:S(2)}) collective-permute-start(s32[2,512]{1,0:T(2,128)S(1)} %copy-done.25), channel_id=1, source_target_pairs={{0,1},{1,0},{2,3},{3,2},{4,5},{5,4},{6,7},{7,6},{8,9},{9,8},{10,11... | collective-permute-start | bytes 12296 | tf_op jit(solution)/shard_map/ppermute | solution.py:57
  11.1 1.7 %collective-permute-start.1 = (bf16[2,64,512]{2,1,0:T(8,128)(2,1)S(1)}, bf16[2,64,512]{2,1,0:T(8,128)(2,1)S(1)}, u32[]{:S(2)}, u32[]{:S(2)}) collective-permute-start(bf16[2,64,512]{2,1,0:T(8,128)(2,1)S(1)} %bitcast.29), channel_id=1, source_target_pairs={{0,1},{1,0},{2,3},{3,2},{4,5},{5,4},{6,7},{7,6},{8,9},{9,8},{10,11... | collective-permute-start | bytes 393224 | tf_op jit(solution)/shard_map/ppermute | solution.py:57
  11.2 2.3 %collective-permute-start.2 = (bf16[2,64,512]{2,1,0:T(8,128)(2,1)S(1)}, bf16[2,64,512]{2,1,0:T(8,128)(2,1)S(1)}, u32[]{:S(2)}, u32[]{:S(2)}) collective-permute-start(bf16[2,64,512]{2,1,0:T(8,128)(2,1)S(1)} %bitcast.31), channel_id=1, source_target_pairs={{0,1},{1,0},{2,3},{3,2},{4,5},{5,4},{6,7},{7,6},{8,9},{9,8},{10,11... | collective-permute-start | bytes 393224 | tf_op jit(solution)/shard_map/ppermute | solution.py:57
  11.6 13.0 %collective-permute-start.4 = (f32[24,3072]{1,0:T(8,128)S(1)}, f32[24,3072]{1,0:T(8,128)}, u32[]{:S(2)}, u32[]{:S(2)}) collective-permute-start(f32[24,3072]{1,0:T(8,128)S(1)} %bitcast.27), channel_id=1, source_target_pairs={{0,1},{1,0},{2,3},{3,2},{4,5},{5,4},{6,7},{7,6},{8,9},{9,8},{10,11... | collective-permute-start | bytes 884744 | tf_op jit(solution)/shard_map/ppermute | solution.py:57
  11.7 12.9 %collective-permute-start.5 = (f32[24,3072]{1,0:T(8,128)}, f32[24,3072]{1,0:T(8,128)}, u32[]{:S(2)}, u32[]{:S(2)}) collective-permute-start(f32[24,3072]{1,0:T(8,128)} %bitcast.6.square), channel_id=1, source_target_pairs={{0,1},{1,0},{2,3},{3,2},{4,5},{5,4},{6,7},{7,6},{8,9},{9,8},{10,11... | collective-permute-start | bytes 884744 | tf_op jit(solution)/shard_map/ppermute | solution.py:57
  12.9 0.7 copy-start.21
  13.5 0.7 copy-start.23
  14.2 0.9 copy-start.18
  15.1 0.9 copy-start.20
  16.0 0.9 copy-start.22
  16.9 0.9 copy-start.24
  22.0 0.6 copy-start.9
  22.7 0.7 copy-start.11
  23.3 0.7 copy-start.13
  24.0 0.7 copy-start.15
  25.8 0.7 copy-start.5
  26.6 0.7 copy-start.7
  28.9 3.2 %copy-start.16 = (f32[64,512]{1,0:T(8,128)S(1)}, f32[64,512]{1,0:T(8,128)}, u32[]{:S(2)}) copy-start(f32[64,512]{1,0:T(8,128)} %copy-done.15) | copy-start | bytes 393220
  28.9 3.2 %collective-permute-start.7 = (f32[528,128]{1,0:T(8,128)S(1)}, f32[528,128]{1,0:T(8,128)S(1)}, u32[]{:S(2)}, u32[]{:S(2)}) collective-permute-start(f32[528,128]{1,0:T(8,128)S(1)} %get-tuple-element.84.own), channel_id=1, source_target_pairs={{0,1},{1,0},{2,3},{3,2},{4,5},{5,4},{6,7},{7,6},{8,9},{9,8},{10,11... | collective-permute-start | bytes 811016 | tf_op jit(solution)/shard_map/ppermute | solution.py:57
  31.9 2.1 %collective-permute-start.6 = (f32[528,128]{1,0:T(8,128)S(1)}, f32[528,128]{1,0:T(8,128)S(1)}, u32[]{:S(2)}, u32[]{:S(2)}) collective-permute-start(f32[528,128]{1,0:T(8,128)S(1)} %get-tuple-element.78.own), channel_id=1, source_target_pairs={{0,1},{1,0},{2,3},{3,2},{4,5},{5,4},{6,7},{7,6},{8,9},{9,8},{10,11... | collective-permute-start | bytes 811016 | tf_op jit(solution)/shard_map/ppermute | solution.py:57
  32.1 2.0 %copy-start.14 = (f32[64,512]{1,0:T(8,128)S(1)}, f32[64,512]{1,0:T(8,128)}, u32[]{:S(2)}) copy-start(f32[64,512]{1,0:T(8,128)} %copy-done.13) | copy-start | bytes 393220
  36.0 21.5 %copy-start.6 = (f32[48,1536]{1,0:T(8,128)S(1)}, f32[48,1536]{1,0:T(8,128)}, u32[]{:S(2)}) copy-start(f32[48,1536]{1,0:T(8,128)} %copy-done.5) | copy-start | bytes 884740
  36.0 21.5 %copy-start.8 = (f32[48,1536]{1,0:T(8,128)S(1)}, f32[48,1536]{1,0:T(8,128)}, u32[]{:S(2)}) copy-start(f32[48,1536]{1,0:T(8,128)} %copy-done.7) | copy-start | bytes 884740
  77.8 4.4 %copy-start.12 = (f32[64,512]{1,0:T(8,128)S(1)}, f32[64,512]{1,0:T(8,128)}, u32[]{:S(2)}) copy-start(f32[64,512]{1,0:T(8,128)} %copy-done.11) | copy-start | bytes 393220
  77.8 4.3 %collective-permute-start.9 = (f32[528,128]{1,0:T(8,128)S(1)}, f32[528,128]{1,0:T(8,128)S(1)}, u32[]{:S(2)}, u32[]{:S(2)}) collective-permute-start(f32[528,128]{1,0:T(8,128)S(1)} %get-tuple-element.97.own), channel_id=1, source_target_pairs={{0,1},{1,0},{2,3},{3,2},{4,5},{5,4},{6,7},{7,6},{8,9},{9,8},{10,11... | collective-permute-start | bytes 811016 | tf_op jit(solution)/shard_map/ppermute | solution.py:57
  81.8 2.3 %collective-permute-start.8 = (f32[528,128]{1,0:T(8,128)S(1)}, f32[528,128]{1,0:T(8,128)S(1)}, u32[]{:S(2)}, u32[]{:S(2)}) collective-permute-start(f32[528,128]{1,0:T(8,128)S(1)} %get-tuple-element.92.own), channel_id=1, source_target_pairs={{0,1},{1,0},{2,3},{3,2},{4,5},{5,4},{6,7},{7,6},{8,9},{9,8},{10,11... | collective-permute-start | bytes 811016 | tf_op jit(solution)/shard_map/ppermute | solution.py:57
  82.1 2.0 %copy-start.10 = (f32[64,512]{1,0:T(8,128)S(1)}, f32[64,512]{1,0:T(8,128)}, u32[]{:S(2)}) copy-start(f32[64,512]{1,0:T(8,128)} %copy-done.9) | copy-start | bytes 393220
  106.3 38.2 %copy-start.2 = (f32[24,3072]{1,0:T(8,128)S(1)}, f32[24,3072]{1,0:T(8,128)}, u32[]{:S(2)}) copy-start(f32[24,3072]{1,0:T(8,128)} %params.1) | copy-start | bytes 884740
  106.3 38.2 %copy-start.3 = (f32[24,3072]{1,0:T(8,128)S(1)}, f32[24,3072]{1,0:T(8,128)}, u32[]{:S(2)}) copy-start(f32[24,3072]{1,0:T(8,128)} %momentum.1) | copy-start | bytes 884740
  106.3 19.7 %all-to-all-start.4 = ((bf16[16,16,384]{2,1,0:T(8,128)(2,1)}), bf16[16,16,384]{2,1,0:T(8,128)(2,1)S(1)}, u32[]{:S(2)}, u32[]{:S(2)}) async-start(bf16[16,16,384]{2,1,0:T(8,128)(2,1)} %get-tuple-element.104), calls=%async_computation.4 | async-start | bytes 393216 | tf_op jit(solution)/shard_map/all_to_all | solution.py:490
  116.3 3.0 %collective-permute-start.10 = (f32[48,1536]{1,0:T(8,128)S(1)}, f32[48,1536]{1,0:T(8,128)S(1)}, u32[]{:S(2)}, u32[]{:S(2)}) collective-permute-start(f32[48,1536]{1,0:T(8,128)S(1)} %get-tuple-element.105.mean), channel_id=1, source_target_pairs={{0,1},{1,0},{2,3},{3,2},{4,5},{5,4},{6,7},{7,6},{8,9},{9,8},{10,11... | collective-permute-start | bytes 884744 | tf_op jit(solution)/shard_map/ppermute | solution.py:57
  118.1 1.6 %collective-permute-start.11 = (f32[48,1536]{1,0:T(8,128)S(1)}, f32[48,1536]{1,0:T(8,128)S(1)}, u32[]{:S(2)}, u32[]{:S(2)}) collective-permute-start(f32[48,1536]{1,0:T(8,128)S(1)} %get-tuple-element.106.square), channel_id=1, source_target_pairs={{0,1},{1,0},{2,3},{3,2},{4,5},{5,4},{6,7},{7,6},{8,9},{9,8},{10,11... | collective-permute-start | bytes 884744 | tf_op jit(solution)/shard_map/ppermute | solution.py:57
  139.4 5.1 %collective-permute-start.12 = (bf16[16,16,384]{2,1,0:T(8,128)(2,1)S(1)}, bf16[16,16,384]{2,1,0:T(8,128)(2,1)S(1)}, u32[]{:S(2)}, u32[]{:S(2)}) collective-permute-start(bf16[16,16,384]{2,1,0:T(8,128)(2,1)S(1)} %all_to_all.33.own), channel_id=1, source_target_pairs={{0,1},{1,0},{2,3},{3,2},{4,5},{5,4},{6,7},{7,6},{8,9},{9,8},{10,11... | collective-permute-start | bytes 589832 | tf_op jit(solution)/shard_map/ppermute | solution.py:57

commit v5 on v4

--- a/solution.py
+++ b/solution.py
@@ -24,8 +24,7 @@
 LANES = 128
 ROW_CHUNK = 16
 FWD_COLUMNS = 256
-STRIP_ROWS = 16
-STRIP_PARTS = 4
+STRIP_COLUMNS = 256
 KERNEL_VMEM = 24 * 2**20
 
 BF16 = jnp.bfloat16
@@ -57,64 +56,20 @@
     return lax.ppermute(values, "fsdp", [(i, i ^ 1) for i in range(width)])
 
 
-def chip_exchange(blocks, width):
-    groups = [list(range(core, width, CORES)) for core in range(CORES)]
-    return lax.all_to_all(blocks, "fsdp", 0, 0, axis_index_groups=groups)
-
-
-def hold_kernel(values, held):
-    held[...] = values[...]
-
-
-def hold(values):
-    return local_call(hold_kernel, "hold", (values,), [(values.shape, values.dtype)])[0]
-
-
-def pair_halves(core, own, got, pair):
-    rows = own.shape[0]
-    half = own.shape[1] // CORES
-
-    @pl.when(core[0] == 0)
-    def _():
-        pair[0:rows] = own[:, 0:half]
-        pair[rows:] = got[:, 0:half]
-
-    @pl.when(core[0] != 0)
-    def _():
-        pair[0:rows] = got[:, half:]
-        pair[rows:] = own[:, half:]
-
-
-def start_kernel(core, own, got, pair, copies):
-    pair_halves(core, own, got, pair)
-    block = pair[...].astype(BF16)
-    for chip in range(copies.shape[0]):
-        copies[chip] = block
-
-
-def moments_kernel(core, mean, mean_got, square, square_got, mean_pair, square_pair):
-    pair_halves(core, mean, mean_got, mean_pair)
-    pair_halves(core, square, square_got, square_pair)
-
-
-def unpair_halves(core, own, got, out):
-    rows = out.shape[0]
-    half = out.shape[1] // CORES
-
-    @pl.when(core[0] == 0)
-    def _():
-        out[:, 0:half] = own[0:rows]
-        out[:, half:] = got[0:rows]
-
-    @pl.when(core[0] != 0)
-    def _():
-        out[:, 0:half] = got[rows:]
-        out[:, half:] = own[rows:]
-
-
-def unpair_kernel(core, mean, mean_got, square, square_got, new_mean, new_square):
-    unpair_halves(core, mean, mean_got, new_mean)
-    unpair_halves(core, square, square_got, new_square)
+def exchange(blocks, axis):
+    return lax.all_to_all(blocks, axis, 0, 0)
+
+
+def spread_halves(values, copies):
+    half = values.shape[1] // CORES
+    for core in range(CORES):
+        block = values[:, core * half : (core + 1) * half].astype(BF16)
+        for index in range(core, copies.shape[0], CORES):
+            copies[index] = block
+
+
+def start_kernel(params, copies):
+    spread_halves(params[...], copies)
 
 
 def scaled_out_weight(weights, factor, time_end):
@@ -327,40 +282,40 @@
     return [sets[CORES * s : CORES * (s + 1)] for s in range(steps)], results[-3:]
 
 
+def adam(blocks, params, mean, square):
+    halves = []
+    for core in range(CORES):
+        total = blocks[core].astype(F32)
+        for index in range(core + CORES, blocks.shape[0], CORES):
+            total = total + blocks[index].astype(F32)
+        halves.append(total)
+    gradient = jnp.concatenate(halves, axis=1)
+    old = params[...]
+    first = BETA_ONE * mean[...] + (1.0 - BETA_ONE) * gradient
+    second = BETA_TWO * square[...] + (1.0 - BETA_TWO) * gradient * gradient
+    new = old - INNER_RATE * (first / (jnp.sqrt(second) + ADAM_EPS) + DECAY_RATE * old)
+    return first, second, new
+
+
 def step_kernel(blocks, params, mean, square, new_mean, new_square, new_params, copies):
     first, second, new = adam(blocks, params, mean, square)
     new_mean[...] = first
     new_square[...] = second
     new_params[...] = new
-    block = new.astype(BF16)
-    for chip in range(copies.shape[0]):
-        copies[chip] = block
+    spread_halves(new, copies)
 
 
 def last_kernel(blocks, params, mean, square, start, new_mean, new_square, strips):
     first, second, new = adam(blocks, params, mean, square)
     new_mean[...] = first
     new_square[...] = second
-    drift = (start[...] - new).astype(BF16)
-    rows, columns = strips.shape[1:]
-    used = 0
-    for top in range(0, drift.shape[0], rows):
-        for left in range(0, drift.shape[1], columns):
-            strips[used] = drift[top : top + rows, left : left + columns]
-            used += 1
-    for index in range(used, strips.shape[0]):
-        strips[index] = jnp.zeros((rows, columns), BF16)
-
-
-def adam(blocks, params, mean, square):
-    gradient = blocks[0].astype(F32)
-    for chip in range(1, blocks.shape[0]):
-        gradient = gradient + blocks[chip].astype(F32)
-    old = params[...]
-    first = BETA_ONE * mean[...] + (1.0 - BETA_ONE) * gradient
-    second = BETA_TWO * square[...] + (1.0 - BETA_TWO) * gradient * gradient
-    new = old - INNER_RATE * (first / (jnp.sqrt(second) + ADAM_EPS) + DECAY_RATE * old)
-    return first, second, new
+    drift = start[...] - new
+    width = strips.shape[2]
+    for index in range(strips.shape[0]):
+        if index * width < drift.shape[1]:
+            strips[index] = drift[:, index * width : (index + 1) * width].astype(BF16)
+        else:
+            strips[index] = jnp.zeros(strips.shape[1:], BF16)
 
 
 def strip_sum_kernel(strips, copies):
@@ -373,33 +328,14 @@
 
 
 def make_outer_kernel(replicas):
-    def outer_kernel(core, own, got, params, momentum, new_params, new_momentum, own_buf, got_buf):
-        strip_rows, strip_columns = own.shape[1:]
-        rows = params.shape[0]
-        half = params.shape[1] // CORES
-        index = 0
-        for top in range(0, rows * CORES, strip_rows):
-            for left in range(0, half, strip_columns):
-                place = (slice(top, top + strip_rows), slice(left, left + strip_columns))
-                own_buf[place] = own[index].astype(F32)
-                got_buf[place] = got[index].astype(F32)
-                index += 1
-
-        def finish(cols, values):
-            average = values * (1.0 / replicas)
+    def outer_kernel(strips, params, momentum, new_params, new_momentum):
+        width = strips.shape[2]
+        for index in range(params.shape[1] // width):
+            cols = slice(index * width, (index + 1) * width)
+            average = strips[index].astype(F32) * (1.0 / replicas)
             moved = NESTEROV * momentum[:, cols] + average
             new_momentum[:, cols] = moved
             new_params[:, cols] = params[:, cols] - OUTER_RATE * (average + NESTEROV * moved)
-
-        @pl.when(core[0] == 0)
-        def _():
-            finish(slice(0, half), own_buf[0:rows])
-            finish(slice(half, 2 * half), got_buf[0:rows])
-
-        @pl.when(core[0] != 0)
-        def _():
-            finish(slice(0, half), got_buf[rows:])
-            finish(slice(half, 2 * half), own_buf[rows:])
 
     return outer_kernel
 
@@ -417,50 +353,28 @@
 ):
     width = lax.axis_size("fsdp")
     replicas = lax.axis_size("replica")
-    chips = width // CORES
-    core = (lax.axis_index("fsdp") % CORES).astype(jnp.int32)
-    core_arg = core.reshape(1)
+    core = (lax.axis_index("fsdp") % CORES).astype(jnp.int32).reshape(1)
     rows, model_width = outer_params.shape
     half = model_width // CORES
     channels = latents.shape[2]
     time_width = rows * width - 2 * channels
     total_rows = latents.shape[1] * width
-
-    pair_shape = (rows * CORES, half)
-    start, copies = local_call(
-        start_kernel,
-        "start",
-        (hold(outer_params), core_swap(outer_params, width)),
-        [(pair_shape, F32), ((chips,) + pair_shape, BF16)],
-        scalars=(core_arg,),
-    )
-    gathered = chip_exchange(copies, width)
-
+    blocks_shape = (width, rows, half)
+
+    copies = local_call(start_kernel, "start", (outer_params,), [(blocks_shape, BF16)])[0]
+    gathered = exchange(copies, "fsdp")
     mod_rows = lax.dynamic_index_in_dim(modulation, fragment[0], 0, keepdims=False)
     prepared, mods = prepare(
-        core_arg, latents, noise_draw, timesteps, mod_rows, time_width, width
-    )
-    params = start
-    mean, square = local_call(
-        moments_kernel,
-        "moments",
-        (
-            inner_mean[0],
-            core_swap(inner_mean[0], width),
-            inner_square[0],
-            core_swap(inner_square[0], width),
-        ),
-        [(pair_shape, F32)] * 2,
-        scalars=(core_arg,),
-    )
-    gathered, prepared, mods, mean, square = lax.optimization_barrier(
-        (gathered, prepared, mods, mean, square)
-    )
-
+        core, latents, noise_draw, timesteps, mod_rows, time_width, width
+    )
+    gathered, prepared, mods = lax.optimization_barrier((gathered, prepared, mods))
+
+    params, mean, square = outer_params, inner_mean[0], inner_square[0]
     sizes = (model_width, total_rows)
     factor, shift, terms = mods
+    moments = [(params.shape, F32)] * 2
     for step in range(STEPS):
-        weights = gathered.reshape(chips * pair_shape[0], half)
+        weights = gathered.reshape(width * rows, half)
         states = []
         for inputs_t, _ in prepared[step]:
             hid, slope, stats = forward(inputs_t, weights, factor, terms)
@@ -472,43 +386,34 @@
                     stats, target_t, state, weights, factor, shift, inputs_t, gradient, sizes
                 ),
             )
-        pair_sum = gradient[0]
-        blocks = chip_exchange(pair_sum.reshape((chips,) + pair_shape), width)
-        moments = [(pair_shape, F32)] * 2
+        blocks = exchange(gradient[0].reshape(blocks_shape), "fsdp")
         if step + 1 < STEPS:
-            outs = moments + [(pair_shape, F32), ((chips,) + pair_shape, BF16)]
             mean, square, params, copies = local_call(
-                step_kernel, "update", (blocks, params, mean, square), outs
+                step_kernel,
+                "update",
+                (blocks, params, mean, square),
+                moments + [(params.shape, F32), (blocks_shape, BF16)],
             )
-            gathered = chip_exchange(copies, width)
+            gathered = exchange(copies, "fsdp")
         else:
-            strip = (STRIP_ROWS, half // STRIP_PARTS)
-            outs = moments + [((replicas,) + strip, BF16)]
+            strips_shape = (replicas, rows, STRIP_COLUMNS)
             mean, square, strips = local_call(
-                last_kernel, "update_last", (blocks, params, mean, square, start), outs
+                last_kernel,
+                "update_last",
+                (blocks, params, mean, square, outer_params),
+                moments + [(strips_shape, BF16)],
             )
-    strips = lax.all_to_all(strips, "replica", 0, 0)
-    new_mean, new_square = local_call(
-        unpair_kernel,
-        "unpair",
-        (mean, core_swap(mean, width), square, core_swap(square, width)),
-        [(outer_params.shape, F32)] * 2,
-        scalars=(core_arg,),
-        hbm_outs=True,
-    )
-    strips, new_mean, new_square = lax.optimization_barrier((strips, new_mean, new_square))
-    strips = local_call(strip_sum_kernel, "strip_sum", (strips,), [(strips.shape, BF16)])[0]
-    strips = lax.all_to_all(strips, "replica", 0, 0)
+    strips = exchange(strips, "replica")
+    strips = local_call(strip_sum_kernel, "strip_sum", (strips,), [(strips_shape, BF16)])[0]
+    strips = exchange(strips, "replica")
     new_params, new_momentum = local_call(
         make_outer_kernel(replicas),
         "outer",
-        (strips, core_swap(strips, width), outer_params, outer_momentum),
-        [(outer_params.shape, F32)] * 2,
-        [pltpu.VMEM(pair_shape, F32)] * 2,
-        scalars=(core_arg,),
+        (strips, outer_params, outer_momentum),
+        [(params.shape, F32)] * 2,
         hbm_outs=True,
     )
-    return (new_params, new_momentum, new_mean[None], new_square[None])
+    return (new_params, new_momentum, mean[None], square[None])
 
 
 def solution(mesh):

time: 146 us -> 144 us (0.986)
  starting transfers between devices: 29.1 us -> 14.7 us
  blocking collectives: 72.1 us -> 80.9 us
  waiting for transfers between devices: 8.45 us -> 13.4 us
  Pallas kernels: 24.1 us -> 22 us
    ppermute x13 -> x7, starting transfers between devices: 15.3 us -> 2.84 us  [core_swap(): return lax.ppermute(values, 'fsdp', [(i, i ^ 1) for i in range(width)])]
    all_to_all x4, blocking collectives: 72.1 us -> 80.9 us  [exchange(): return lax.all_to_all(blocks, axis, 0, 0)]
    all_to_all x2, waiting for transfers between devices: 5.46 us -> 13.4 us  [exchange(): return lax.all_to_all(blocks, axis, 0, 0)]
    ppermute x13 -> x7, waiting for transfers between devices: 3 us -> 0.02 us  [core_swap(): return lax.ppermute(values, 'fsdp', [(i, i ^ 1) for i in range(width)])]
    pallas_call x17 -> x14, Pallas kernels: 24.1 us -> 22 us  [local_call(): pl.pallas_call(kernel, in_specs=specs, out_specs=[VMEM] * len(outs), out_...]
    all_to_all x2, starting transfers between devices: 13.8 us -> 11.8 us  [exchange(): return lax.all_to_all(blocks, axis, 0, 0)]
    unnamed x52 -> x42, local copies, waits for them, and re-layouts: 9.98 us -> 9.88 us
  transfers between devices with their start and end apart: 15 -> 9, of which waited for: 5 -> 2; matrix products, arithmetic and copies ran while one was open for 0% -> 1% of each run, Pallas kernels for 9% -> 8%
where the time goes in v5:
time: 144 us; the launch traced here: 142 us
  blocking collectives  80.9 us (56%)
  Pallas kernels  22 us (15%)
  starting transfers between devices  14.7 us (10%)
  waiting for transfers between devices  13.4 us (9%)
  local copies, waits for them, and re-layouts  9.89 us (7%)
  between operations  1.52 us (1%)
    all_to_all x4, blocking collectives, exchange(): return lax.all_to_all(blocks, axis, 0, 0)  80.9 us
    pallas_call x14, Pallas kernels, local_call(): pl.pallas_call(kernel, in_specs=specs, out_specs=[VMEM] * len(outs), out_...  22 us
    all_to_all x2, waiting for transfers between devices, exchange(): return lax.all_to_all(blocks, axis, 0, 0)  13.4 us
    all_to_all x2, starting transfers between devices, exchange(): return lax.all_to_all(blocks, axis, 0, 0)  11.8 us
    unnamed x42, local copies, waits for them, and re-layouts  9.88 us
  transfers between devices with their start and end apart: 9, of which 2 were waited for; matrix products, arithmetic and copies ran while one was open for 1% of the time, Pallas kernels for 8%

profile of v5, /device:TPU:1, one launch (start us, length us, event | category | flops | bytes accessed | tf_op | source)
XLA Modules:
  0.0 142.3 jit_solution(14211706624881963386)
XLA Ops:
  0.6 0.0 copy-start
  0.6 0.0 copy-start.1
  0.7 1.0 copy-done.1
  1.7 1.1 start.2
  2.8 7.3 %all-to-all-start = ((bf16[16,24,1536]{2,1,0:T(8,128)(2,1)}), bf16[16,24,1536]{2,1,0:T(8,128)(2,1)S(1)}, u32[]{:S(2)}, u32[]{:S(2)}) async-start(bf16[16,24,1536]{2,1,0:T(8,128)(2,1)} %start.2), calls=%async_computation | async-start | bytes 2359296 | tf_op jit(solution)/shard_map/all_to_all | solution.py:60
  10.1 0.0 copy-done.13
  10.1 0.2 collective-permute-start.2
  10.3 0.0 copy-done.6
  10.3 0.4 collective-permute-start
  10.7 0.0 copy-done.7
  10.7 0.1 collective-permute-start.1
  11.5 0.0 copy-done
  11.5 0.0 collective-permute-done.2.levels_got
  11.6 0.0 copy-start.15
  11.6 0.6 copy-done.15
  12.2 0.0 collective-permute-done.latents_got
  12.2 0.7 copy-done.9
  12.8 0.0 collective-permute-done.1.noise_got
  12.8 0.7 copy-done.11
  13.5 0.9 copy-done.8
  14.4 0.9 copy-done.10
  15.3 0.9 copy-done.12
  16.2 0.7 copy-done.14
  16.9 0.7 copy-done.16
  17.6 4.2 %prepare.1 = (bf16[320,512]{1,0:T(8,128)(2,1)S(1)}, f32[64,512]{1,0:T(8,128)S(1)}, bf16[320,512]{1,0:T(8,128)(2,1)S(1)}, f32[64,512]{1,0:T(8,128)S(1)}, bf16[320...) custom-call(s32[1]{0:T(128)} %bitcast.core, ...), custom_call_target="tpu_custom_call" | custom-call | flops 4294967296 | bytes 3813376 | tf_op jit(solution)/shard_map/prepare/pallas_call | solution.py:43
  21.8 0.0 copy-start.17
  21.8 0.6 copy-done.17
  22.4 5.0 %all-to-all-done = bf16[16,24,1536]{2,1,0:T(8,128)(2,1)S(1)} async-done(((bf16[16,24,1536]{2,1,0:T(8,128)(2,1)}), bf16[16,24,1536]{2,1,0:T(8,128)(2,1)S(1)}, u32[]{:S(2)}, u32[]{:S(2)}) %all-to-all-start) | async-done | bytes 1179680 | tf_op jit(solution)/shard_map/all_to_all | solution.py:60
  27.4 0.8 copy-done.18
  28.2 1.6 %forward.5 = (bf16[512,1536]{1,0:T(8,128)(2,1)S(1)}, bf16[512,1536]{1,0:T(8,128)(2,1)S(1)}, f32[528,128]{1,0:T(8,128)S(1)}) custom-call(bf16[320,512]{1,0:T(8,128)(2,1)S(1)} %get-tuple-element.69.inputs_t, bf16[384,1536]{1,0:T(8,128)(2,1)S(1)} %bitcast.19, f32[1,1536]{1,0:T(1,128)S(1)} %get-tuple-element.62.factor, bf16[16,1536]{1,0:T(8,128)(2,1)S(1)} %copy-done.18), custom_call_target="tpu_custom_call" | custom-call | flops 603979776 | bytes 8124416 | tf_op jit(solution)/shard_map/forward/pallas_call | solution.py:43
  29.8 1.0 collective-permute-start.4
  30.8 0.0 copy-done.19
  30.8 1.6 %forward.4 = (bf16[512,1536]{1,0:T(8,128)(2,1)S(1)}, bf16[512,1536]{1,0:T(8,128)(2,1)S(1)}, f32[528,128]{1,0:T(8,128)S(1)}) custom-call(bf16[320,512]{1,0:T(8,128)(2,1)S(1)} %get-tuple-element.60.inputs_t, bf16[384,1536]{1,0:T(8,128)(2,1)S(1)} %bitcast.20, f32[1,1536]{1,0:T(1,128)S(1)} %get-tuple-element.62.factor, bf16[16,1536]{1,0:T(8,128)(2,1)S(1)} %copy-done.19), custom_call_target="tpu_custom_call" | custom-call | flops 603979776 | bytes 8124416 | tf_op jit(solution)/shard_map/forward/pallas_call | solution.py:43
  32.4 0.3 collective-permute-start.3
  32.7 0.0 collective-permute-done.4.got
  32.7 1.9 %backward.4.rest_0_ = f32[384,1536]{1,0:T(8,128)S(1)} custom-call(f32[528,128]{1,0:T(8,128)S(1)} %get-tuple-element.70.own, f32[528,128]{1,0:T(8,128)S(1)} %collective-permute-done.4.got, f32[64,512]{1,0:T(8,128)S(1)} %get-tuple-element.71.target_t, bf16[512,1536]{1,0:T(8,128)(2,1)S(1)} %get-tuple-element.72.hid, ...), custom_call_target="tpu_custom_call" | custom-call | flops 704643072 | bytes 7696384 | tf_op jit(solution)/shard_map/backward/pallas_call | solution.py:43
  34.6 0.0 collective-permute-done.3.got
  34.6 2.0 %backward.5 = bf16[384,1536]{1,0:T(8,128)(2,1)S(1)} custom-call(f32[528,128]{1,0:T(8,128)S(1)} %get-tuple-element.64.own, f32[528,128]{1,0:T(8,128)S(1)} %collective-permute-done.3.got, f32[64,512]{1,0:T(8,128)S(1)} %get-tuple-element.65.target_t, bf16[512,1536]{1,0:T(8,128)(2,1)S(1)} %get-tuple-element.66.hid, ...), custom_call_target="tpu_custom_call" | custom-call | flops 704643072 | bytes 10055680 | tf_op jit(solution)/shard_map/backward/pallas_call | solution.py:43
  36.6 0.0 copy-start.2
  36.6 0.0 copy-start.4
  36.6 0.0 copy-start.5
  36.6 20.5 %all_to_all.30.blocks = bf16[16,24,1536]{2,1,0:T(8,128)(2,1)S(1)} all-to-all(bf16[16,24,1536]{2,1,0:T(8,128)(2,1)S(1)} %bitcast.28), channel_id=1, replica_groups=mesh['replica'=16,'fsdp'=16] {'fsdp'}, dimensions={0} | all-to-all | bytes 2359296 | tf_op jit(solution)/shard_map/all_to_all | solution.py:60
  57.1 0.0 copy-done.2
  57.1 0.0 copy-done.4
  57.1 0.4 update.1
  57.6 20.6 %all_to_all.31 = bf16[16,24,1536]{2,1,0:T(8,128)(2,1)S(1)} all-to-all(bf16[16,24,1536]{2,1,0:T(8,128)(2,1)S(1)} %get-tuple-element.74), channel_id=1, replica_groups=mesh['replica'=16,'fsdp'=16] {'fsdp'}, dimensions={0} | all-to-all | bytes 2359296 | tf_op jit(solution)/shard_map/all_to_all | solution.py:60
  78.2 1.6 %forward.7 = (bf16[512,1536]{1,0:T(8,128)(2,1)S(1)}, bf16[512,1536]{1,0:T(8,128)(2,1)S(1)}, f32[528,128]{1,0:T(8,128)S(1)}) custom-call(bf16[320,512]{1,0:T(8,128)(2,1)S(1)} %get-tuple-element.79.inputs_t, bf16[384,1536]{1,0:T(8,128)(2,1)S(1)} %bitcast.23, f32[1,1536]{1,0:T(1,128)S(1)} %get-tuple-element.62.factor, bf16[16,1536]{1,0:T(8,128)(2,1)S(1)} %copy-done.19), custom_call_target="tpu_custom_call" | custom-call | flops 603979776 | bytes 8124416 | tf_op jit(solution)/shard_map/forward/pallas_call | solution.py:43
  79.7 0.8 collective-permute-start.6
  80.5 1.6 %forward.6 = (bf16[512,1536]{1,0:T(8,128)(2,1)S(1)}, bf16[512,1536]{1,0:T(8,128)(2,1)S(1)}, f32[528,128]{1,0:T(8,128)S(1)}) custom-call(bf16[320,512]{1,0:T(8,128)(2,1)S(1)} %get-tuple-element.59.inputs_t, bf16[384,1536]{1,0:T(8,128)(2,1)S(1)} %bitcast.24, f32[1,1536]{1,0:T(1,128)S(1)} %get-tuple-element.62.factor, bf16[16,1536]{1,0:T(8,128)(2,1)S(1)} %copy-done.19), custom_call_target="tpu_custom_call" | custom-call | flops 603979776 | bytes 8124416 | tf_op jit(solution)/shard_map/forward/pallas_call | solution.py:43
  82.1 0.1 collective-permute-start.5
  82.2 0.0 collective-permute-done.6.got
  82.2 1.9 %backward.6.rest_0_ = f32[384,1536]{1,0:T(8,128)S(1)} custom-call(f32[528,128]{1,0:T(8,128)S(1)} %get-tuple-element.80.own, f32[528,128]{1,0:T(8,128)S(1)} %collective-permute-done.6.got, f32[64,512]{1,0:T(8,128)S(1)} %get-tuple-element.81.target_t, bf16[512,1536]{1,0:T(8,128)(2,1)S(1)} %get-tuple-element.82.hid, ...), custom_call_target="tpu_custom_call" | custom-call | flops 704643072 | bytes 7696384 | tf_op jit(solution)/shard_map/backward/pallas_call | solution.py:43
  84.1 0.0 collective-permute-done.5.got
  84.2 2.0 %backward.7 = bf16[384,1536]{1,0:T(8,128)(2,1)S(1)} custom-call(f32[528,128]{1,0:T(8,128)S(1)} %get-tuple-element.75.own, f32[528,128]{1,0:T(8,128)S(1)} %collective-permute-done.5.got, f32[64,512]{1,0:T(8,128)S(1)} %get-tuple-element.76.target_t, bf16[512,1536]{1,0:T(8,128)(2,1)S(1)} %get-tuple-element.77.hid, ...), custom_call_target="tpu_custom_call" | custom-call | flops 704643072 | bytes 10055680 | tf_op jit(solution)/shard_map/backward/pallas_call | solution.py:43
  86.1 20.4 %all_to_all.32.blocks = bf16[16,24,1536]{2,1,0:T(8,128)(2,1)S(1)} all-to-all(bf16[16,24,1536]{2,1,0:T(8,128)(2,1)S(1)} %bitcast.27), channel_id=1, replica_groups=mesh['replica'=16,'fsdp'=16] {'fsdp'}, dimensions={0} | all-to-all | bytes 2359296 | tf_op jit(solution)/shard_map/all_to_all | solution.py:60
  106.5 0.4 update_last.1
  106.9 0.0 copy-start.3
  106.9 19.5 %all_to_all.33.strips = bf16[16,24,256]{2,1,0:T(8,128)(2,1)S(1)} all-to-all(bf16[16,24,256]{2,1,0:T(8,128)(2,1)S(1)} %get-tuple-element.87), channel_id=1, replica_groups=mesh['replica'=16,'fsdp'=16] {'replica'}, dimensions={0} | all-to-all | bytes 393216 | tf_op jit(solution)/shard_map/all_to_all | solution.py:60
  126.4 0.7 strip_sum.1
  127.1 4.5 %all-to-all-start.5 = ((bf16[16,24,256]{2,1,0:T(8,128)(2,1)}), bf16[16,24,256]{2,1,0:T(8,128)(2,1)S(1)}, u32[]{:S(2)}, u32[]{:S(2)}) async-start(bf16[16,24,256]{2,1,0:T(8,128)(2,1)} %strip_sum.1), calls=%async_computation.5 | async-start | bytes 393216 | tf_op jit(solution)/shard_map/all_to_all | solution.py:60
  131.6 0.7 copy.13
  132.3 0.7 copy.14
  133.1 8.4 %all-to-all-done.5.strips = bf16[16,24,256]{2,1,0:T(8,128)(2,1)S(1)} async-done(((bf16[16,24,256]{2,1,0:T(8,128)(2,1)}), bf16[16,24,256]{2,1,0:T(8,128)(2,1)S(1)}, u32[]{:S(2)}, u32[]{:S(2)}) %all-to-all-start.5) | async-done | bytes 196640 | tf_op jit(solution)/shard_map/all_to_all | solution.py:60
  141.4 0.9 outer.1
  (15 shorter events, 0.0 us)
Async XLA Ops:
  0.6 10.9 %copy-start = (f32[15,2,3072]{2,1,0:T(2,128)S(1)}, f32[15,2,3072]{2,1,0:T(2,128)}, u32[]{:S(2)}) copy-start(f32[15,2,3072]{2,1,0:T(2,128)} %param.17) | copy-start | bytes 1105924
  0.6 1.0 copy-start.1
  1.7 8.5 %copy-start.13 = (s32[2,512]{1,0:T(2,128)S(1)}, s32[2,512]{1,0:T(2,128)}, u32[]{:S(2)}) copy-start(s32[2,512]{1,0:T(2,128)} %levels.1) | copy-start | bytes 12292
  1.7 8.7 %copy-start.6 = (bf16[2,512,64]{1,2,0:T(8,128)(2,1)S(1)}, bf16[2,512,64]{1,2,0:T(8,128)(2,1)}, u32[]{:S(2)}) copy-start(bf16[2,512,64]{1,2,0:T(8,128)(2,1)} %param.13) | copy-start | bytes 393220
  1.7 9.1 %copy-start.7 = (bf16[2,512,64]{1,2,0:T(8,128)(2,1)S(1)}, bf16[2,512,64]{1,2,0:T(8,128)(2,1)}, u32[]{:S(2)}) copy-start(bf16[2,512,64]{1,2,0:T(8,128)(2,1)} %param.14) | copy-start | bytes 393220
  2.8 24.6 %all-to-all-start = ((bf16[16,24,1536]{2,1,0:T(8,128)(2,1)}), bf16[16,24,1536]{2,1,0:T(8,128)(2,1)S(1)}, u32[]{:S(2)}, u32[]{:S(2)}) async-start(bf16[16,24,1536]{2,1,0:T(8,128)(2,1)} %start.2), calls=%async_computation | async-start | bytes 2359296 | tf_op jit(solution)/shard_map/all_to_all | solution.py:60
  10.1 1.4 collective-permute-start.2
  10.3 1.8 %collective-permute-start = (bf16[2,64,512]{2,1,0:T(8,128)(2,1)S(1)}, bf16[2,64,512]{2,1,0:T(8,128)(2,1)S(1)}, u32[]{:S(2)}, u32[]{:S(2)}) collective-permute-start(bf16[2,64,512]{2,1,0:T(8,128)(2,1)S(1)} %bitcast.31), channel_id=1, source_target_pairs={{0,1},{1,0},{2,3},{3,2},{4,5},{5,4},{6,7},{7,6},{8,9},{9,8},{10,11... | collective-permute-start | bytes 393224 | tf_op jit(solution)/shard_map/ppermute | solution.py:56
  10.7 2.1 %collective-permute-start.1 = (bf16[2,64,512]{2,1,0:T(8,128)(2,1)S(1)}, bf16[2,64,512]{2,1,0:T(8,128)(2,1)S(1)}, u32[]{:S(2)}, u32[]{:S(2)}) collective-permute-start(bf16[2,64,512]{2,1,0:T(8,128)(2,1)S(1)} %bitcast.33), channel_id=1, source_target_pairs={{0,1},{1,0},{2,3},{3,2},{4,5},{5,4},{6,7},{7,6},{8,9},{9,8},{10,11... | collective-permute-start | bytes 393224 | tf_op jit(solution)/shard_map/ppermute | solution.py:56
  11.6 0.6 copy-start.15
  12.2 0.7 copy-start.9
  12.8 0.7 copy-start.11
  13.5 0.9 copy-start.8
  14.4 0.9 copy-start.10
  15.3 0.9 copy-start.12
  16.2 0.7 copy-start.14
  16.9 0.7 copy-start.16
  21.8 0.6 copy-start.17
  27.4 0.8 copy-start.18
  28.2 2.6 %copy-start.19 = (bf16[16,1536]{1,0:T(8,128)(2,1)S(1)}, bf16[16,1536]{1,0:T(8,128)(2,1)}, u32[]{:S(2)}) copy-start(bf16[16,1536]{1,0:T(8,128)(2,1)} %copy-done.17) | copy-start | bytes 147460
  29.8 2.8 %collective-permute-start.4 = (f32[528,128]{1,0:T(8,128)S(1)}, f32[528,128]{1,0:T(8,128)S(1)}, u32[]{:S(2)}, u32[]{:S(2)}) collective-permute-start(f32[528,128]{1,0:T(8,128)S(1)} %get-tuple-element.70.own), channel_id=1, source_target_pairs={{0,1},{1,0},{2,3},{3,2},{4,5},{5,4},{6,7},{7,6},{8,9},{9,8},{10,11... | collective-permute-start | bytes 811016 | tf_op jit(solution)/shard_map/ppermute | solution.py:56
  32.4 2.2 %collective-permute-start.3 = (f32[528,128]{1,0:T(8,128)S(1)}, f32[528,128]{1,0:T(8,128)S(1)}, u32[]{:S(2)}, u32[]{:S(2)}) collective-permute-start(f32[528,128]{1,0:T(8,128)S(1)} %get-tuple-element.64.own), channel_id=1, source_target_pairs={{0,1},{1,0},{2,3},{3,2},{4,5},{5,4},{6,7},{7,6},{8,9},{9,8},{10,11... | collective-permute-start | bytes 811016 | tf_op jit(solution)/shard_map/ppermute | solution.py:56
  36.6 20.5 %copy-start.2 = (f32[24,3072]{1,0:T(8,128)S(1)}, f32[24,3072]{1,0:T(8,128)}, u32[]{:S(2)}) copy-start(f32[24,3072]{1,0:T(8,128)} %params.5) | copy-start | bytes 884740
  36.6 20.5 %copy-start.4 = (f32[1,24,3072]{2,1,0:T(8,128)S(1)}, f32[1,24,3072]{2,1,0:T(8,128)}, u32[]{:S(2)}) copy-start(f32[1,24,3072]{2,1,0:T(8,128)} %param.11) | copy-start | bytes 884740
  36.6 20.5 %copy-start.5 = (f32[1,24,3072]{2,1,0:T(8,128)S(1)}, f32[1,24,3072]{2,1,0:T(8,128)}, u32[]{:S(2)}) copy-start(f32[1,24,3072]{2,1,0:T(8,128)} %param.12) | copy-start | bytes 884740
  79.7 2.5 %collective-permute-start.6 = (f32[528,128]{1,0:T(8,128)S(1)}, f32[528,128]{1,0:T(8,128)S(1)}, u32[]{:S(2)}, u32[]{:S(2)}) collective-permute-start(f32[528,128]{1,0:T(8,128)S(1)} %get-tuple-element.80.own), channel_id=1, source_target_pairs={{0,1},{1,0},{2,3},{3,2},{4,5},{5,4},{6,7},{7,6},{8,9},{9,8},{10,11... | collective-permute-start | bytes 811016 | tf_op jit(solution)/shard_map/ppermute | solution.py:56
  82.1 2.0 %collective-permute-start.5 = (f32[528,128]{1,0:T(8,128)S(1)}, f32[528,128]{1,0:T(8,128)S(1)}, u32[]{:S(2)}, u32[]{:S(2)}) collective-permute-start(f32[528,128]{1,0:T(8,128)S(1)} %get-tuple-element.75.own), channel_id=1, source_target_pairs={{0,1},{1,0},{2,3},{3,2},{4,5},{5,4},{6,7},{7,6},{8,9},{9,8},{10,11... | collective-permute-start | bytes 811016 | tf_op jit(solution)/shard_map/ppermute | solution.py:56
  106.9 34.5 %copy-start.3 = (f32[24,3072]{1,0:T(8,128)S(1)}, f32[24,3072]{1,0:T(8,128)}, u32[]{:S(2)}) copy-start(f32[24,3072]{1,0:T(8,128)} %momentum.1) | copy-start | bytes 884740
  127.1 14.3 %all-to-all-start.5 = ((bf16[16,24,256]{2,1,0:T(8,128)(2,1)}), bf16[16,24,256]{2,1,0:T(8,128)(2,1)S(1)}, u32[]{:S(2)}, u32[]{:S(2)}) async-start(bf16[16,24,256]{2,1,0:T(8,128)(2,1)} %strip_sum.1), calls=%async_computation.5 | async-start | bytes 393216 | tf_op jit(solution)/shard_map/all_to_all | solution.py:60

commit v6 on v5

--- a/solution.py
+++ b/solution.py
@@ -31,8 +31,9 @@
 F32 = jnp.float32
 VMEM = pl.BlockSpec(memory_space=pltpu.VMEM)
 SMEM = pl.BlockSpec(memory_space=pltpu.SMEM)
-TRANSPOSED = (((1,), (1,)), ((), ()))
-BOTH_TRANSPOSED = (((0,), (0,)), ((), ()))
+RIGHT_TRANSPOSED = (((1,), (1,)), ((), ()))
+LEFT_TRANSPOSED = (((0,), (0,)), ((), ()))
+SHIFT_ROWS = 16
 
 
 def local_call(kernel, name, args, outs, scratch=(), scalars=(), flops=0, hbm_outs=False):
@@ -69,11 +70,25 @@
 
 
 def start_kernel(params, copies):
-    spread_halves(params[...], copies)
-
-
-def scaled_out_weight(weights, factor, time_end):
-    return (weights[time_end:, :].astype(F32) * factor[0:1, :]).astype(BF16)
+    block = params[...].astype(BF16)
+    for index in range(copies.shape[0]):
+        copies[index, 0] = block
+
+
+def spread_start(params, width):
+    rows, columns = params.shape
+    half = columns // CORES
+    shape = (width // CORES, CORES, rows, half)
+    copies = pl.pallas_call(
+        start_kernel,
+        grid=(CORES,),
+        in_specs=[pl.BlockSpec((rows, half), lambda core: (0, core))],
+        out_specs=pl.BlockSpec((shape[0], 1, rows, half), lambda core: (0, core, 0, 0)),
+        out_shape=jax.ShapeDtypeStruct(shape, BF16),
+        compiler_params=pltpu.CompilerParams(vmem_limit_bytes=KERNEL_VMEM),
+        name="start",
+    )(pltpu.with_memory_space_constraint(params, pltpu.HBM))
+    return copies.reshape(width, rows, half)
 
 
 def forward_kernel(inputs_t, weights, factor, shift, hid, slope, stats, pre_buf, in_buf, square):
@@ -86,13 +101,13 @@
         pre_buf[slot] = lax.dot_general(
             inputs_t[channels:, :],
             weights[channels:time_end, cols],
-            BOTH_TRANSPOSED,
+            LEFT_TRANSPOSED,
             preferred_element_type=F32,
         )
         in_buf[slot] = lax.dot_general(
             inputs_t[0:channels, :],
             weights[0:channels, cols],
-            BOTH_TRANSPOSED,
+            LEFT_TRANSPOSED,
             preferred_element_type=F32,
         )
         for start in range(0, rows_here, ROW_CHUNK):
@@ -109,11 +124,14 @@
             for lane in range(LANES, FWD_COLUMNS, LANES):
                 partial = partial + power[:, lane : lane + LANES]
             square[rows, :] += partial
-    scaled = scaled_out_weight(weights, factor, time_end)
-    out = lax.dot_general(hid[...], scaled, TRANSPOSED, preferred_element_type=F32)
-    bias = lax.dot_general(
-        shift[...], weights[time_end:, :], TRANSPOSED, preferred_element_type=F32
-    )
+    out_weight = weights[time_end:, :]
+    scaled = (out_weight.astype(F32) * factor[0:1, :]).astype(BF16)
+    out = lax.dot_general(hid[...], scaled, RIGHT_TRANSPOSED, preferred_element_type=F32)
+    wide = jnp.broadcast_to(shift[0:1, :], (SHIFT_ROWS, shift.shape[1]))
+    high = wide.astype(BF16).astype(F32)
+    row = lax.broadcasted_iota(jnp.int32, wide.shape, 0)
+    terms = jnp.where(row == 0, high, jnp.where(row == 1, wide - high, 0.0)).astype(BF16)
+    bias = lax.dot_general(terms, out_weight, RIGHT_TRANSPOSED, preferred_element_type=F32)
     power = jnp.sum(square[...], axis=1, keepdims=True)
     stats[0:rows_here, :] = jnp.concatenate(
         [out, jnp.broadcast_to(power, (rows_here, LANES - channels))], axis=1
@@ -123,7 +141,7 @@
 
 def forward(inputs_t, weights, factor, shift):
     rows, columns = inputs_t.shape[1], weights.shape[1]
-    outs = [((rows, columns), BF16)] * 2 + [((rows + shift.shape[0], LANES), F32)]
+    outs = [((rows, columns), BF16)] * 2 + [((rows + SHIFT_ROWS, LANES), F32)]
     scratch = [pltpu.VMEM((2, rows, FWD_COLUMNS), F32)] * 2 + [pltpu.VMEM((rows, LANES), F32)]
     flops = 2 * rows * columns * weights.shape[0]
     args = (inputs_t, weights, factor, shift)
@@ -156,7 +174,7 @@
         pull[...] = jnp.broadcast_to(pulled, pull.shape)
         grad_sum = jnp.sum(out_grad.T, axis=1, keepdims=True) * root
 
-        scaled = scaled_out_weight(weights, factor, time_end)
+        scaled = (weights[time_end:, :].astype(F32) * factor[0:1, :]).astype(BF16)
         mod_buf[...] = jnp.dot(grad, scaled, preferred_element_type=F32)
         for start in range(0, rows_here, ROW_CHUNK):
             rows = pl.ds(start, ROW_CHUNK)
@@ -241,7 +259,7 @@
                 inputs_t[pl.ds(channels + part * half_width, half_width), :] = wave.astype(BF16)
     rows = modulation[...]
     half = rows.shape[1] // CORES
-    factor, shift, terms = outs[place:]
+    factor, shift = outs[place:]
 
     for side in range(CORES):
 
@@ -250,11 +268,6 @@
             here = rows[:, side * half : (side + 1) * half]
             factor[...] = 1.0 + here[1:2]
             shift[...] = here[0:1]
-            wide = jnp.broadcast_to(here[0:1], terms.shape)
-            high = wide.astype(BF16).astype(F32)
-            index = lax.broadcasted_iota(jnp.int32, terms.shape, 0)
-            split = jnp.where(index == 0, high, jnp.where(index == 1, wide - high, 0.0))
-            terms[...] = split.astype(BF16)
 
 
 def prepare(core, latents, noise_draw, timesteps, mod_rows, time_width, width):
@@ -263,7 +276,7 @@
     outs = [
         ((channels + time_width, tokens), BF16),
         ((channels, tokens), F32),
-    ] * (steps * CORES) + [((1, half), F32), ((1, half), F32), ((16, half), BF16)]
+    ] * (steps * CORES) + [((1, half), F32)] * 2
     args = []
     scratch = []
     for values in (latents.transpose(0, 2, 1), noise_draw.transpose(0, 2, 1), timesteps):
@@ -279,7 +292,7 @@
         flops=2**32,
     )
     sets = [results[2 * i : 2 * i + 2] for i in range(steps * CORES)]
-    return [sets[CORES * s : CORES * (s + 1)] for s in range(steps)], results[-3:]
+    return [sets[CORES * s : CORES * (s + 1)] for s in range(steps)], results[-2:]
 
 
 def adam(blocks, params, mean, square):
@@ -328,7 +341,9 @@
 
 
 def make_outer_kernel(replicas):
-    def outer_kernel(strips, params, momentum, new_params, new_momentum):
+    def outer_kernel(strips, params, momentum, mean, square, new_params, new_momentum, *moments):
+        moments[0][...] = mean[...]
+        moments[1][...] = square[...]
         width = strips.shape[2]
         for index in range(params.shape[1] // width):
             cols = slice(index * width, (index + 1) * width)
@@ -361,8 +376,7 @@
     total_rows = latents.shape[1] * width
     blocks_shape = (width, rows, half)
 
-    copies = local_call(start_kernel, "start", (outer_params,), [(blocks_shape, BF16)])[0]
-    gathered = exchange(copies, "fsdp")
+    gathered = exchange(spread_start(outer_params, width), "fsdp")
     mod_rows = lax.dynamic_index_in_dim(modulation, fragment[0], 0, keepdims=False)
     prepared, mods = prepare(
         core, latents, noise_draw, timesteps, mod_rows, time_width, width
@@ -371,13 +385,13 @@
 
     params, mean, square = outer_params, inner_mean[0], inner_square[0]
     sizes = (model_width, total_rows)
-    factor, shift, terms = mods
+    factor, shift = mods
     moments = [(params.shape, F32)] * 2
     for step in range(STEPS):
         weights = gathered.reshape(width * rows, half)
         states = []
         for inputs_t, _ in prepared[step]:
-            hid, slope, stats = forward(inputs_t, weights, factor, terms)
+            hid, slope, stats = forward(inputs_t, weights, factor, shift)
             states.append(((hid, slope), (stats, core_swap(stats, width))))
         gradient = ()
         for (state, stats), (inputs_t, target_t) in zip(states, prepared[step]):
@@ -406,11 +420,11 @@
     strips = exchange(strips, "replica")
     strips = local_call(strip_sum_kernel, "strip_sum", (strips,), [(strips_shape, BF16)])[0]
     strips = exchange(strips, "replica")
-    new_params, new_momentum = local_call(
+    new_params, new_momentum, mean, square = local_call(
         make_outer_kernel(replicas),
         "outer",
-        (strips, outer_params, outer_momentum),
-        [(params.shape, F32)] * 2,
+        (strips, outer_params, outer_momentum, mean, square),
+        [(params.shape, F32)] * 4,
         hbm_outs=True,
     )
     return (new_params, new_momentum, mean[None], square[None])

time: 144 us -> 142 us (0.986)
  blocking collectives: 80.9 us -> 94.9 us
  waiting for transfers between devices: 13.4 us -> 5.65 us
  starting transfers between devices: 14.7 us -> 10.2 us
  local copies, waits for them, and re-layouts: 9.89 us -> 6.04 us
    all_to_all x4 -> x5, blocking collectives: 80.9 us -> 94.9 us  [exchange(): return lax.all_to_all(blocks, axis, 0, 0)]
    all_to_all x2 -> x1, waiting for transfers between devices: 13.4 us -> 5.63 us  [exchange(): return lax.all_to_all(blocks, axis, 0, 0)]
    all_to_all x2 -> x1, starting transfers between devices: 11.8 us -> 7.34 us  [exchange(): return lax.all_to_all(blocks, axis, 0, 0)]
    unnamed x42 -> x32, local copies, waits for them, and re-layouts: 9.88 us -> 6.03 us
    pallas_call x0 -> x1, Pallas kernels: none -> 2.04 us  [spread_start(): pl.pallas_call(start_kernel, grid=(CORES,), in_specs=[pl.BlockSpec((rows,...]
    pallas_call x14 -> x13, Pallas kernels: 22 us -> 20.3 us  [local_call(): pl.pallas_call(kernel, in_specs=specs, out_specs=[VMEM] * len(outs), out_...]
  transfers between devices with their start and end apart: 9 -> 8, of which waited for: 2 -> 1; matrix products, arithmetic and copies ran while one was open for 1% -> 0% of each run, Pallas kernels for 8% -> 8%
where the time goes in v6:
time: 142 us; the launch traced here: 141 us
  blocking collectives  94.9 us (67%)
  Pallas kernels  22.4 us (16%)
  starting transfers between devices  10.2 us (7%)
  local copies, waits for them, and re-layouts  6.04 us (4%)
  waiting for transfers between devices  5.65 us (4%)
  between operations  1.52 us (1%)
    all_to_all x5, blocking collectives, exchange(): return lax.all_to_all(blocks, axis, 0, 0)  94.9 us
    pallas_call x13, Pallas kernels, local_call(): pl.pallas_call(kernel, in_specs=specs, out_specs=[VMEM] * len(outs), out_...  20.3 us
    all_to_all x1, starting transfers between devices, exchange(): return lax.all_to_all(blocks, axis, 0, 0)  7.34 us
    unnamed x32, local copies, waits for them, and re-layouts  6.03 us
    all_to_all x1, waiting for transfers between devices, exchange(): return lax.all_to_all(blocks, axis, 0, 0)  5.63 us
  transfers between devices with their start and end apart: 8, of which 1 were waited for; matrix products, arithmetic and copies ran while one was open for 0% of the time, Pallas kernels for 8%

profile of v6, /device:TPU:1, one launch (start us, length us, event | category | flops | bytes accessed | tf_op | source)
XLA Modules:
  0.0 140.6 jit_solution(5009747933247299049)
XLA Ops:
  0.6 0.0 copy-start
  0.6 0.0 copy-start.12
  0.7 0.0 copy-start.5
  0.7 0.0 copy-start.6
  0.7 2.0 %start.2 = bf16[8,2,24,1536]{3,2,1,0:T(8,128)(2,1)} custom-call(f32[24,3072]{1,0:T(8,128)} %params.5), custom_call_target="tpu_custom_call" | custom-call | tf_op jit(solution)/shard_map/start/pallas_call | solution.py:82
  2.7 7.3 %all-to-all-start = ((bf16[16,24,1536]{2,1,0:T(8,128)(2,1)}), bf16[16,24,1536]{2,1,0:T(8,128)(2,1)S(1)}, u32[]{:S(2)}, u32[]{:S(2)}) async-start(bf16[16,24,1536]{2,1,0:T(8,128)(2,1)} %bitcast), calls=%async_computation | async-start | bytes 2359296 | tf_op jit(solution)/shard_map/all_to_all | solution.py:61
  10.1 0.0 copy-done.12
  10.1 0.2 collective-permute-start.2
  10.3 0.0 copy-done.5
  10.3 0.4 collective-permute-start
  10.7 0.0 copy-done.6
  10.7 0.1 collective-permute-start.1
  11.4 0.0 copy-done
  11.5 0.0 collective-permute-done.2.levels_got
  11.5 0.0 copy-start.14
  11.5 0.6 copy-done.14
  12.1 0.0 collective-permute-done.latents_got
  12.1 0.0 copy-start.8
  12.1 0.7 copy-done.8
  12.7 0.0 collective-permute-done.1.noise_got
  12.7 0.0 copy-start.10
  12.7 0.7 copy-done.10
  13.4 0.9 copy-done.7
  14.3 0.0 copy-start.9
  14.3 0.9 copy-done.9
  15.2 0.0 copy-start.11
  15.2 0.9 copy-done.11
  16.1 0.0 copy-start.13
  16.1 0.7 copy-done.13
  16.8 0.0 copy-start.15
  16.8 0.7 copy-done.15
  17.5 4.2 %prepare.1 = (bf16[320,512]{1,0:T(8,128)(2,1)S(1)}, f32[64,512]{1,0:T(8,128)S(1)}, bf16[320,512]{1,0:T(8,128)(2,1)S(1)}, f32[64,512]{1,0:T(8,128)S(1)}, bf16[320...) custom-call(s32[1]{0:T(128)} %bitcast.1.core, ...), custom_call_target="tpu_custom_call" | custom-call | flops 4294967296 | bytes 3715072 | tf_op jit(solution)/shard_map/prepare/pallas_call | solution.py:44
  21.7 5.6 %all-to-all-done = bf16[16,24,1536]{2,1,0:T(8,128)(2,1)S(1)} async-done(((bf16[16,24,1536]{2,1,0:T(8,128)(2,1)}), bf16[16,24,1536]{2,1,0:T(8,128)(2,1)S(1)}, u32[]{:S(2)}, u32[]{:S(2)}) %all-to-all-start) | async-done | bytes 1179680 | tf_op jit(solution)/shard_map/all_to_all | solution.py:61
  27.3 1.6 %forward.5 = (bf16[512,1536]{1,0:T(8,128)(2,1)S(1)}, bf16[512,1536]{1,0:T(8,128)(2,1)S(1)}, f32[528,128]{1,0:T(8,128)S(1)}) custom-call(bf16[320,512]{1,0:T(8,128)(2,1)S(1)} %get-tuple-element.67.inputs_t, bf16[384,1536]{1,0:T(8,128)(2,1)S(1)} %bitcast.18, f32[1,1536]{1,0:T(1,128)S(1)} %get-tuple-element.61.factor, f32[1,1536]{1,0:T(1,128)S(1)} %get-tuple-element.62.shift), custom_call_target="tpu_custom_call" | custom-call | flops 603979776 | bytes 8081408 | tf_op jit(solution)/shard_map/forward/pallas_call | solution.py:44
  28.9 1.0 collective-permute-start.4
  29.9 1.6 %forward.4 = (bf16[512,1536]{1,0:T(8,128)(2,1)S(1)}, bf16[512,1536]{1,0:T(8,128)(2,1)S(1)}, f32[528,128]{1,0:T(8,128)S(1)}) custom-call(bf16[320,512]{1,0:T(8,128)(2,1)S(1)} %get-tuple-element.59.inputs_t, bf16[384,1536]{1,0:T(8,128)(2,1)S(1)} %bitcast.19, f32[1,1536]{1,0:T(1,128)S(1)} %get-tuple-element.61.factor, f32[1,1536]{1,0:T(1,128)S(1)} %get-tuple-element.62.shift), custom_call_target="tpu_custom_call" | custom-call | flops 603979776 | bytes 8081408 | tf_op jit(solution)/shard_map/forward/pallas_call | solution.py:44
  31.5 0.3 collective-permute-start.3
  31.8 0.0 collective-permute-done.4.got
  31.8 1.9 %backward.4.rest_0_ = f32[384,1536]{1,0:T(8,128)S(1)} custom-call(f32[528,128]{1,0:T(8,128)S(1)} %get-tuple-element.68.own, f32[528,128]{1,0:T(8,128)S(1)} %collective-permute-done.4.got, f32[64,512]{1,0:T(8,128)S(1)} %get-tuple-element.69.target_t, bf16[512,1536]{1,0:T(8,128)(2,1)S(1)} %get-tuple-element.70.hid, ...), custom_call_target="tpu_custom_call" | custom-call | flops 704643072 | bytes 7696384 | tf_op jit(solution)/shard_map/backward/pallas_call | solution.py:44
  33.7 0.0 collective-permute-done.3.got
  33.7 2.0 %backward.5 = bf16[384,1536]{1,0:T(8,128)(2,1)S(1)} custom-call(f32[528,128]{1,0:T(8,128)S(1)} %get-tuple-element.63.own, f32[528,128]{1,0:T(8,128)S(1)} %collective-permute-done.3.got, f32[64,512]{1,0:T(8,128)S(1)} %get-tuple-element.64.target_t, bf16[512,1536]{1,0:T(8,128)(2,1)S(1)} %get-tuple-element.65.hid, ...), custom_call_target="tpu_custom_call" | custom-call | flops 704643072 | bytes 10055680 | tf_op jit(solution)/shard_map/backward/pallas_call | solution.py:44
  35.7 0.0 copy-start.1
  35.7 0.0 copy-start.2
  35.7 0.0 copy-start.3
  35.8 20.5 %all_to_all.30.blocks = bf16[16,24,1536]{2,1,0:T(8,128)(2,1)S(1)} all-to-all(bf16[16,24,1536]{2,1,0:T(8,128)(2,1)S(1)} %bitcast.27), channel_id=1, replica_groups=mesh['replica'=16,'fsdp'=16] {'fsdp'}, dimensions={0} | all-to-all | bytes 2359296 | tf_op jit(solution)/shard_map/all_to_all | solution.py:61
  56.2 0.0 copy-done.1
  56.2 0.0 copy-done.2
  56.2 0.0 copy-done.3
  56.3 0.5 update.1
  56.7 20.6 %all_to_all.31 = bf16[16,24,1536]{2,1,0:T(8,128)(2,1)S(1)} all-to-all(bf16[16,24,1536]{2,1,0:T(8,128)(2,1)S(1)} %get-tuple-element.72), channel_id=1, replica_groups=mesh['replica'=16,'fsdp'=16] {'fsdp'}, dimensions={0} | all-to-all | bytes 2359296 | tf_op jit(solution)/shard_map/all_to_all | solution.py:61
  77.3 1.6 %forward.7 = (bf16[512,1536]{1,0:T(8,128)(2,1)S(1)}, bf16[512,1536]{1,0:T(8,128)(2,1)S(1)}, f32[528,128]{1,0:T(8,128)S(1)}) custom-call(bf16[320,512]{1,0:T(8,128)(2,1)S(1)} %get-tuple-element.77.inputs_t, bf16[384,1536]{1,0:T(8,128)(2,1)S(1)} %bitcast.22, f32[1,1536]{1,0:T(1,128)S(1)} %get-tuple-element.61.factor, f32[1,1536]{1,0:T(1,128)S(1)} %get-tuple-element.62.shift), custom_call_target="tpu_custom_call" | custom-call | flops 603979776 | bytes 8081408 | tf_op jit(solution)/shard_map/forward/pallas_call | solution.py:44
  78.9 0.8 collective-permute-start.6
  79.6 1.6 %forward.6 = (bf16[512,1536]{1,0:T(8,128)(2,1)S(1)}, bf16[512,1536]{1,0:T(8,128)(2,1)S(1)}, f32[528,128]{1,0:T(8,128)S(1)}) custom-call(bf16[320,512]{1,0:T(8,128)(2,1)S(1)} %get-tuple-element.58.inputs_t, bf16[384,1536]{1,0:T(8,128)(2,1)S(1)} %bitcast.23, f32[1,1536]{1,0:T(1,128)S(1)} %get-tuple-element.61.factor, f32[1,1536]{1,0:T(1,128)S(1)} %get-tuple-element.62.shift), custom_call_target="tpu_custom_call" | custom-call | flops 603979776 | bytes 8081408 | tf_op jit(solution)/shard_map/forward/pallas_call | solution.py:44
  81.2 0.1 collective-permute-start.5
  81.3 0.0 collective-permute-done.6.got
  81.3 1.9 %backward.6.rest_0_ = f32[384,1536]{1,0:T(8,128)S(1)} custom-call(f32[528,128]{1,0:T(8,128)S(1)} %get-tuple-element.78.own, f32[528,128]{1,0:T(8,128)S(1)} %collective-permute-done.6.got, f32[64,512]{1,0:T(8,128)S(1)} %get-tuple-element.79.target_t, bf16[512,1536]{1,0:T(8,128)(2,1)S(1)} %get-tuple-element.80.hid, ...), custom_call_target="tpu_custom_call" | custom-call | flops 704643072 | bytes 7696384 | tf_op jit(solution)/shard_map/backward/pallas_call | solution.py:44
  83.3 0.0 collective-permute-done.5.got
  83.3 2.0 %backward.7 = bf16[384,1536]{1,0:T(8,128)(2,1)S(1)} custom-call(f32[528,128]{1,0:T(8,128)S(1)} %get-tuple-element.73.own, f32[528,128]{1,0:T(8,128)S(1)} %collective-permute-done.5.got, f32[64,512]{1,0:T(8,128)S(1)} %get-tuple-element.74.target_t, bf16[512,1536]{1,0:T(8,128)(2,1)S(1)} %get-tuple-element.75.hid, ...), custom_call_target="tpu_custom_call" | custom-call | flops 704643072 | bytes 10055680 | tf_op jit(solution)/shard_map/backward/pallas_call | solution.py:44
  85.3 20.4 %all_to_all.32.blocks = bf16[16,24,1536]{2,1,0:T(8,128)(2,1)S(1)} all-to-all(bf16[16,24,1536]{2,1,0:T(8,128)(2,1)S(1)} %bitcast.26), channel_id=1, replica_groups=mesh['replica'=16,'fsdp'=16] {'fsdp'}, dimensions={0} | all-to-all | bytes 2359296 | tf_op jit(solution)/shard_map/all_to_all | solution.py:61
  105.6 0.4 update_last.1
  106.0 19.3 %all_to_all.33.strips = bf16[16,24,256]{2,1,0:T(8,128)(2,1)S(1)} all-to-all(bf16[16,24,256]{2,1,0:T(8,128)(2,1)S(1)} %get-tuple-element.85), channel_id=1, replica_groups=mesh['replica'=16,'fsdp'=16] {'replica'}, dimensions={0} | all-to-all | bytes 393216 | tf_op jit(solution)/shard_map/all_to_all | solution.py:61
  125.4 14.1 %all_to_all.34.strips = bf16[16,24,256]{2,1,0:T(8,128)(2,1)S(1)} all-to-all(bf16[16,24,256]{2,1,0:T(8,128)(2,1)S(1)} %strip_sum.1), channel_id=1, replica_groups=mesh['replica'=16,'fsdp'=16] {'replica'}, dimensions={0} | all-to-all | bytes 393216 | tf_op jit(solution)/shard_map/all_to_all | solution.py:61
  139.5 0.0 copy-done.4
  139.5 1.1 outer.1
  (4 shorter events, 0.0 us)
Async XLA Ops:
  0.6 10.8 %copy-start = (f32[15,2,3072]{2,1,0:T(2,128)S(1)}, f32[15,2,3072]{2,1,0:T(2,128)}, u32[]{:S(2)}) copy-start(f32[15,2,3072]{2,1,0:T(2,128)} %param.17) | copy-start | bytes 1105924
  0.6 9.4 %copy-start.12 = (s32[2,512]{1,0:T(2,128)S(1)}, s32[2,512]{1,0:T(2,128)}, u32[]{:S(2)}) copy-start(s32[2,512]{1,0:T(2,128)} %levels.1) | copy-start | bytes 12292
  0.7 9.6 %copy-start.5 = (bf16[2,512,64]{1,2,0:T(8,128)(2,1)S(1)}, bf16[2,512,64]{1,2,0:T(8,128)(2,1)}, u32[]{:S(2)}) copy-start(bf16[2,512,64]{1,2,0:T(8,128)(2,1)} %param.13) | copy-start | bytes 393220
  0.7 10.0 %copy-start.6 = (bf16[2,512,64]{1,2,0:T(8,128)(2,1)S(1)}, bf16[2,512,64]{1,2,0:T(8,128)(2,1)}, u32[]{:S(2)}) copy-start(bf16[2,512,64]{1,2,0:T(8,128)(2,1)} %param.14) | copy-start | bytes 393220
  2.7 24.6 %all-to-all-start = ((bf16[16,24,1536]{2,1,0:T(8,128)(2,1)}), bf16[16,24,1536]{2,1,0:T(8,128)(2,1)S(1)}, u32[]{:S(2)}, u32[]{:S(2)}) async-start(bf16[16,24,1536]{2,1,0:T(8,128)(2,1)} %bitcast), calls=%async_computation | async-start | bytes 2359296 | tf_op jit(solution)/shard_map/all_to_all | solution.py:61
  10.1 1.4 %collective-permute-start.2 = (s32[2,512]{1,0:T(2,128)S(1)}, s32[2,512]{1,0:T(2,128)S(1)}, u32[]{:S(2)}, u32[]{:S(2)}) collective-permute-start(s32[2,512]{1,0:T(2,128)S(1)} %copy-done.12), channel_id=1, source_target_pairs={{0,1},{1,0},{2,3},{3,2},{4,5},{5,4},{6,7},{7,6},{8,9},{9,8},{10,11... | collective-permute-start | bytes 12296 | tf_op jit(solution)/shard_map/ppermute | solution.py:57
  10.3 1.8 %collective-permute-start = (bf16[2,64,512]{2,1,0:T(8,128)(2,1)S(1)}, bf16[2,64,512]{2,1,0:T(8,128)(2,1)S(1)}, u32[]{:S(2)}, u32[]{:S(2)}) collective-permute-start(bf16[2,64,512]{2,1,0:T(8,128)(2,1)S(1)} %bitcast.30), channel_id=1, source_target_pairs={{0,1},{1,0},{2,3},{3,2},{4,5},{5,4},{6,7},{7,6},{8,9},{9,8},{10,11... | collective-permute-start | bytes 393224 | tf_op jit(solution)/shard_map/ppermute | solution.py:57
  10.7 2.1 %collective-permute-start.1 = (bf16[2,64,512]{2,1,0:T(8,128)(2,1)S(1)}, bf16[2,64,512]{2,1,0:T(8,128)(2,1)S(1)}, u32[]{:S(2)}, u32[]{:S(2)}) collective-permute-start(bf16[2,64,512]{2,1,0:T(8,128)(2,1)S(1)} %bitcast.32), channel_id=1, source_target_pairs={{0,1},{1,0},{2,3},{3,2},{4,5},{5,4},{6,7},{7,6},{8,9},{9,8},{10,11... | collective-permute-start | bytes 393224 | tf_op jit(solution)/shard_map/ppermute | solution.py:57
  11.5 0.6 copy-start.14
  12.1 0.7 copy-start.8
  12.7 0.7 copy-start.10
  13.4 0.9 copy-start.7
  14.3 0.9 copy-start.9
  15.2 0.9 copy-start.11
  16.1 0.7 copy-start.13
  16.8 0.7 copy-start.15
  28.9 2.8 %collective-permute-start.4 = (f32[528,128]{1,0:T(8,128)S(1)}, f32[528,128]{1,0:T(8,128)S(1)}, u32[]{:S(2)}, u32[]{:S(2)}) collective-permute-start(f32[528,128]{1,0:T(8,128)S(1)} %get-tuple-element.68.own), channel_id=1, source_target_pairs={{0,1},{1,0},{2,3},{3,2},{4,5},{5,4},{6,7},{7,6},{8,9},{9,8},{10,11... | collective-permute-start | bytes 811016 | tf_op jit(solution)/shard_map/ppermute | solution.py:57
  31.5 2.2 %collective-permute-start.3 = (f32[528,128]{1,0:T(8,128)S(1)}, f32[528,128]{1,0:T(8,128)S(1)}, u32[]{:S(2)}, u32[]{:S(2)}) collective-permute-start(f32[528,128]{1,0:T(8,128)S(1)} %get-tuple-element.63.own), channel_id=1, source_target_pairs={{0,1},{1,0},{2,3},{3,2},{4,5},{5,4},{6,7},{7,6},{8,9},{9,8},{10,11... | collective-permute-start | bytes 811016 | tf_op jit(solution)/shard_map/ppermute | solution.py:57
  35.7 20.5 %copy-start.1 = (f32[24,3072]{1,0:T(8,128)S(1)}, f32[24,3072]{1,0:T(8,128)}, u32[]{:S(2)}) copy-start(f32[24,3072]{1,0:T(8,128)} %params.5) | copy-start | bytes 884740
  35.7 20.5 %copy-start.2 = (f32[1,24,3072]{2,1,0:T(8,128)S(1)}, f32[1,24,3072]{2,1,0:T(8,128)}, u32[]{:S(2)}) copy-start(f32[1,24,3072]{2,1,0:T(8,128)} %param.11) | copy-start | bytes 884740
  35.7 20.5 %copy-start.3 = (f32[1,24,3072]{2,1,0:T(8,128)S(1)}, f32[1,24,3072]{2,1,0:T(8,128)}, u32[]{:S(2)}) copy-start(f32[1,24,3072]{2,1,0:T(8,128)} %param.12) | copy-start | bytes 884740
  78.9 2.5 %collective-permute-start.6 = (f32[528,128]{1,0:T(8,128)S(1)}, f32[528,128]{1,0:T(8,128)S(1)}, u32[]{:S(2)}, u32[]{:S(2)}) collective-permute-start(f32[528,128]{1,0:T(8,128)S(1)} %get-tuple-element.78.own), channel_id=1, source_target_pairs={{0,1},{1,0},{2,3},{3,2},{4,5},{5,4},{6,7},{7,6},{8,9},{9,8},{10,11... | collective-permute-start | bytes 811016 | tf_op jit(solution)/shard_map/ppermute | solution.py:57
  81.2 2.0 %collective-permute-start.5 = (f32[528,128]{1,0:T(8,128)S(1)}, f32[528,128]{1,0:T(8,128)S(1)}, u32[]{:S(2)}, u32[]{:S(2)}) collective-permute-start(f32[528,128]{1,0:T(8,128)S(1)} %get-tuple-element.73.own), channel_id=1, source_target_pairs={{0,1},{1,0},{2,3},{3,2},{4,5},{5,4},{6,7},{7,6},{8,9},{9,8},{10,11... | collective-permute-start | bytes 811016 | tf_op jit(solution)/shard_map/ppermute | solution.py:57
  105.6 33.9 %copy-start.4 = (f32[24,3072]{1,0:T(8,128)S(1)}, f32[24,3072]{1,0:T(8,128)}, u32[]{:S(2)}) copy-start(f32[24,3072]{1,0:T(8,128)} %momentum.1) | copy-start | bytes 884740

commit v7 on v6

--- a/solution.py
+++ b/solution.py
@@ -24,7 +24,6 @@
 LANES = 128
 ROW_CHUNK = 16
 FWD_COLUMNS = 256
-STRIP_COLUMNS = 256
 KERNEL_VMEM = 24 * 2**20
 
 BF16 = jnp.bfloat16
@@ -318,36 +317,46 @@
     spread_halves(new, copies)
 
 
-def last_kernel(blocks, params, mean, square, start, new_mean, new_square, strips):
+def last_kernel(blocks, params, mean, square, start, new_mean, new_square, *drifts):
     first, second, new = adam(blocks, params, mean, square)
     new_mean[...] = first
     new_square[...] = second
-    drift = start[...] - new
-    width = strips.shape[2]
-    for index in range(strips.shape[0]):
-        if index * width < drift.shape[1]:
-            strips[index] = drift[:, index * width : (index + 1) * width].astype(BF16)
-        else:
-            strips[index] = jnp.zeros(strips.shape[1:], BF16)
-
-
-def strip_sum_kernel(strips, copies):
-    total = strips[0].astype(F32)
-    for index in range(1, strips.shape[0]):
-        total = total + strips[index].astype(F32)
-    block = total.astype(BF16)
-    for index in range(copies.shape[0]):
-        copies[index] = block
+    drift = (start[...] - new).astype(BF16)
+    for index, part in enumerate(drifts):
+        columns = part.shape[1]
+        part[...] = drift[:, index * columns : (index + 1) * columns]
+
+
+def pair_add_kernel(mine, got, out):
+    out[...] = (mine[...].astype(F32) + got[...].astype(F32)).astype(BF16)
+
+
+def replica_sum(parts, replicas):
+    bits = [1 << stage for stage in range(replicas.bit_length() - 1)]
+    middle = len(bits) // 2
+    parts = list(parts)
+    for stage in zip(bits, bits[middle:] + bits[:middle]):
+        got = [
+            lax.ppermute(part, "replica", [(i, i ^ bit) for i in range(replicas)])
+            for part, bit in zip(parts, stage)
+        ]
+        parts = [
+            local_call(pair_add_kernel, "pair_add", pair, [(pair[0].shape, BF16)])[0]
+            for pair in zip(parts, got)
+        ]
+    return parts
 
 
 def make_outer_kernel(replicas):
-    def outer_kernel(strips, params, momentum, mean, square, new_params, new_momentum, *moments):
+    def outer_kernel(
+        left, right, params, momentum, mean, square, new_params, new_momentum, *moments
+    ):
         moments[0][...] = mean[...]
         moments[1][...] = square[...]
-        width = strips.shape[2]
-        for index in range(params.shape[1] // width):
-            cols = slice(index * width, (index + 1) * width)
-            average = strips[index].astype(F32) * (1.0 / replicas)
+        for index, part in enumerate((left, right)):
+            columns = part.shape[1]
+            cols = slice(index * columns, (index + 1) * columns)
+            average = part[...].astype(F32) * (1.0 / replicas)
             moved = NESTEROV * momentum[:, cols] + average
             new_momentum[:, cols] = moved
             new_params[:, cols] = params[:, cols] - OUTER_RATE * (average + NESTEROV * moved)
@@ -410,20 +419,17 @@
             )
             gathered = exchange(copies, "fsdp")
         else:
-            strips_shape = (replicas, rows, STRIP_COLUMNS)
-            mean, square, strips = local_call(
+            mean, square, *drifts = local_call(
                 last_kernel,
                 "update_last",
                 (blocks, params, mean, square, outer_params),
-                moments + [(strips_shape, BF16)],
+                moments + [((rows, half), BF16)] * 2,
             )
-    strips = exchange(strips, "replica")
-    strips = local_call(strip_sum_kernel, "strip_sum", (strips,), [(strips_shape, BF16)])[0]
-    strips = exchange(strips, "replica")
+    drifts = replica_sum(drifts, replicas)
     new_params, new_momentum, mean, square = local_call(
         make_outer_kernel(replicas),
         "outer",
-        (strips, outer_params, outer_momentum, mean, square),
+        (*drifts, outer_params, outer_momentum, mean, square),
         [(params.shape, F32)] * 4,
         hbm_outs=True,
     )

time: 142 us -> 137 us (0.965)
  blocking collectives: 94.9 us -> 61.4 us
  starting transfers between devices: 10.2 us -> 27.2 us
  waiting for transfers between devices: 5.65 us -> 16.7 us
    all_to_all x5 -> x3, blocking collectives: 94.9 us -> 61.4 us  [exchange(): return lax.all_to_all(blocks, axis, 0, 0)]
    ppermute x0 -> x8, starting transfers between devices: none -> 17.1 us  [replica_sum(): lax.ppermute(part, 'replica', [(i, i ^ bit) for i in range(replicas)])]
    ppermute x0 -> x8, waiting for transfers between devices: none -> 11 us  [replica_sum(): lax.ppermute(part, 'replica', [(i, i ^ bit) for i in range(replicas)])]
    pallas_call x13 -> x20, Pallas kernels: 20.3 us -> 20.4 us  [local_call(): pl.pallas_call(kernel, in_specs=specs, out_specs=[VMEM] * len(outs), out_...]
  transfers between devices with their start and end apart: 8 -> 16, of which waited for: 1 -> 5; matrix products, arithmetic and copies ran while one was open for 0% -> 0% of each run, Pallas kernels for 8% -> 8%
where the time goes in v7:
time: 137 us; the launch traced here: 135 us
  blocking collectives  61.4 us (45%)
  starting transfers between devices  27.2 us (20%)
  Pallas kernels  22.5 us (16%)
  waiting for transfers between devices  16.7 us (12%)
  local copies, waits for them, and re-layouts  6.04 us (4%)
  between operations  1.58 us (1%)
    all_to_all x3, blocking collectives, exchange(): return lax.all_to_all(blocks, axis, 0, 0)  61.4 us
    pallas_call x20, Pallas kernels, local_call(): pl.pallas_call(kernel, in_specs=specs, out_specs=[VMEM] * len(outs), out_...  20.4 us
    ppermute x8, starting transfers between devices, replica_sum(): lax.ppermute(part, 'replica', [(i, i ^ bit) for i in range(replicas)])  17.1 us
    ppermute x8, waiting for transfers between devices, replica_sum(): lax.ppermute(part, 'replica', [(i, i ^ bit) for i in range(replicas)])  11 us
    all_to_all x1, starting transfers between devices, exchange(): return lax.all_to_all(blocks, axis, 0, 0)  7.34 us
    unnamed x32, local copies, waits for them, and re-layouts  6.03 us
    all_to_all x1, waiting for transfers between devices, exchange(): return lax.all_to_all(blocks, axis, 0, 0)  5.63 us
    ppermute x7, starting transfers between devices, core_swap(): return lax.ppermute(values, 'fsdp', [(i, i ^ 1) for i in range(width)])  2.83 us
  transfers between devices with their start and end apart: 16, of which 5 were waited for; matrix products, arithmetic and copies ran while one was open for 0% of the time, Pallas kernels for 8%

profile of v7, /device:TPU:1, one launch (start us, length us, event | category | flops | bytes accessed | tf_op | source)
XLA Modules:
  0.0 135.4 jit_solution(11734951493048753819)
XLA Ops:
  0.6 0.0 copy-start
  0.6 0.0 copy-start.12
  0.7 0.0 copy-start.5
  0.7 0.0 copy-start.6
  0.7 2.0 %start.2 = bf16[8,2,24,1536]{3,2,1,0:T(8,128)(2,1)} custom-call(f32[24,3072]{1,0:T(8,128)} %params.5), custom_call_target="tpu_custom_call" | custom-call | tf_op jit(solution)/shard_map/start/pallas_call | solution.py:81
  2.7 7.3 %all-to-all-start = ((bf16[16,24,1536]{2,1,0:T(8,128)(2,1)}), bf16[16,24,1536]{2,1,0:T(8,128)(2,1)S(1)}, u32[]{:S(2)}, u32[]{:S(2)}) async-start(bf16[16,24,1536]{2,1,0:T(8,128)(2,1)} %bitcast), calls=%async_computation | async-start | bytes 2359296 | tf_op jit(solution)/shard_map/all_to_all | solution.py:60
  10.1 0.2 collective-permute-start.2
  10.3 0.4 collective-permute-start
  10.7 0.1 collective-permute-start.1
  11.5 0.0 collective-permute-done.2.levels_got
  11.5 0.0 copy-start.14
  11.5 0.6 copy-done.14
  12.1 0.0 collective-permute-done.latents_got
  12.1 0.7 copy-done.8
  12.7 0.0 collective-permute-done.1.noise_got
  12.7 0.7 copy-done.10
  13.4 0.9 copy-done.7
  14.3 0.9 copy-done.9
  15.2 0.9 copy-done.11
  16.1 0.7 copy-done.13
  16.8 0.7 copy-done.15
  17.5 4.2 %prepare.1 = (bf16[320,512]{1,0:T(8,128)(2,1)S(1)}, f32[64,512]{1,0:T(8,128)S(1)}, bf16[320,512]{1,0:T(8,128)(2,1)S(1)}, f32[64,512]{1,0:T(8,128)S(1)}, bf16[320...) custom-call(s32[1]{0:T(128)} %bitcast.1.core, ...), custom_call_target="tpu_custom_call" | custom-call | flops 4294967296 | bytes 3715072 | tf_op jit(solution)/shard_map/prepare/pallas_call | solution.py:43
  21.7 5.6 %all-to-all-done = bf16[16,24,1536]{2,1,0:T(8,128)(2,1)S(1)} async-done(((bf16[16,24,1536]{2,1,0:T(8,128)(2,1)}), bf16[16,24,1536]{2,1,0:T(8,128)(2,1)S(1)}, u32[]{:S(2)}, u32[]{:S(2)}) %all-to-all-start) | async-done | bytes 1179680 | tf_op jit(solution)/shard_map/all_to_all | solution.py:60
  27.4 1.6 %forward.5 = (bf16[512,1536]{1,0:T(8,128)(2,1)S(1)}, bf16[512,1536]{1,0:T(8,128)(2,1)S(1)}, f32[528,128]{1,0:T(8,128)S(1)}) custom-call(bf16[320,512]{1,0:T(8,128)(2,1)S(1)} %get-tuple-element.68.inputs_t, bf16[384,1536]{1,0:T(8,128)(2,1)S(1)} %bitcast.18, f32[1,1536]{1,0:T(1,128)S(1)} %get-tuple-element.62.factor, f32[1,1536]{1,0:T(1,128)S(1)} %get-tuple-element.63.shift), custom_call_target="tpu_custom_call" | custom-call | flops 603979776 | bytes 8081408 | tf_op jit(solution)/shard_map/forward/pallas_call | solution.py:43
  28.9 1.0 collective-permute-start.4
  29.9 1.6 %forward.4 = (bf16[512,1536]{1,0:T(8,128)(2,1)S(1)}, bf16[512,1536]{1,0:T(8,128)(2,1)S(1)}, f32[528,128]{1,0:T(8,128)S(1)}) custom-call(bf16[320,512]{1,0:T(8,128)(2,1)S(1)} %get-tuple-element.60.inputs_t, bf16[384,1536]{1,0:T(8,128)(2,1)S(1)} %bitcast.19, f32[1,1536]{1,0:T(1,128)S(1)} %get-tuple-element.62.factor, f32[1,1536]{1,0:T(1,128)S(1)} %get-tuple-element.63.shift), custom_call_target="tpu_custom_call" | custom-call | flops 603979776 | bytes 8081408 | tf_op jit(solution)/shard_map/forward/pallas_call | solution.py:43
  31.5 0.3 collective-permute-start.3
  31.8 0.0 collective-permute-done.4.got
  31.8 1.9 %backward.4.rest_0_ = f32[384,1536]{1,0:T(8,128)S(1)} custom-call(f32[528,128]{1,0:T(8,128)S(1)} %get-tuple-element.69.own, f32[528,128]{1,0:T(8,128)S(1)} %collective-permute-done.4.got, f32[64,512]{1,0:T(8,128)S(1)} %get-tuple-element.70.target_t, bf16[512,1536]{1,0:T(8,128)(2,1)S(1)} %get-tuple-element.71.hid, ...), custom_call_target="tpu_custom_call" | custom-call | flops 704643072 | bytes 7696384 | tf_op jit(solution)/shard_map/backward/pallas_call | solution.py:43
  33.7 0.0 collective-permute-done.3.got
  33.7 2.0 %backward.5 = bf16[384,1536]{1,0:T(8,128)(2,1)S(1)} custom-call(f32[528,128]{1,0:T(8,128)S(1)} %get-tuple-element.64.own, f32[528,128]{1,0:T(8,128)S(1)} %collective-permute-done.3.got, f32[64,512]{1,0:T(8,128)S(1)} %get-tuple-element.65.target_t, bf16[512,1536]{1,0:T(8,128)(2,1)S(1)} %get-tuple-element.66.hid, ...), custom_call_target="tpu_custom_call" | custom-call | flops 704643072 | bytes 10055680 | tf_op jit(solution)/shard_map/backward/pallas_call | solution.py:43
  35.7 0.0 copy-start.1
  35.7 0.0 copy-start.2
  35.7 0.0 copy-start.3
  35.8 20.5 %all_to_all.20.blocks = bf16[16,24,1536]{2,1,0:T(8,128)(2,1)S(1)} all-to-all(bf16[16,24,1536]{2,1,0:T(8,128)(2,1)S(1)} %bitcast.27), channel_id=1, replica_groups=mesh['replica'=16,'fsdp'=16] {'fsdp'}, dimensions={0} | all-to-all | bytes 2359296 | tf_op jit(solution)/shard_map/all_to_all | solution.py:60
  56.3 0.5 update.1
  56.7 20.6 %all_to_all.21 = bf16[16,24,1536]{2,1,0:T(8,128)(2,1)S(1)} all-to-all(bf16[16,24,1536]{2,1,0:T(8,128)(2,1)S(1)} %get-tuple-element.73), channel_id=1, replica_groups=mesh['replica'=16,'fsdp'=16] {'fsdp'}, dimensions={0} | all-to-all | bytes 2359296 | tf_op jit(solution)/shard_map/all_to_all | solution.py:60
  77.3 1.6 %forward.7 = (bf16[512,1536]{1,0:T(8,128)(2,1)S(1)}, bf16[512,1536]{1,0:T(8,128)(2,1)S(1)}, f32[528,128]{1,0:T(8,128)S(1)}) custom-call(bf16[320,512]{1,0:T(8,128)(2,1)S(1)} %get-tuple-element.78.inputs_t, bf16[384,1536]{1,0:T(8,128)(2,1)S(1)} %bitcast.22, f32[1,1536]{1,0:T(1,128)S(1)} %get-tuple-element.62.factor, f32[1,1536]{1,0:T(1,128)S(1)} %get-tuple-element.63.shift), custom_call_target="tpu_custom_call" | custom-call | flops 603979776 | bytes 8081408 | tf_op jit(solution)/shard_map/forward/pallas_call | solution.py:43
  78.9 0.8 collective-permute-start.6
  79.7 1.6 %forward.6 = (bf16[512,1536]{1,0:T(8,128)(2,1)S(1)}, bf16[512,1536]{1,0:T(8,128)(2,1)S(1)}, f32[528,128]{1,0:T(8,128)S(1)}) custom-call(bf16[320,512]{1,0:T(8,128)(2,1)S(1)} %get-tuple-element.59.inputs_t, bf16[384,1536]{1,0:T(8,128)(2,1)S(1)} %bitcast.23, f32[1,1536]{1,0:T(1,128)S(1)} %get-tuple-element.62.factor, f32[1,1536]{1,0:T(1,128)S(1)} %get-tuple-element.63.shift), custom_call_target="tpu_custom_call" | custom-call | flops 603979776 | bytes 8081408 | tf_op jit(solution)/shard_map/forward/pallas_call | solution.py:43
  81.2 0.1 collective-permute-start.5
  81.3 0.0 collective-permute-done.6.got
  81.3 1.9 %backward.6.rest_0_ = f32[384,1536]{1,0:T(8,128)S(1)} custom-call(f32[528,128]{1,0:T(8,128)S(1)} %get-tuple-element.79.own, f32[528,128]{1,0:T(8,128)S(1)} %collective-permute-done.6.got, f32[64,512]{1,0:T(8,128)S(1)} %get-tuple-element.80.target_t, bf16[512,1536]{1,0:T(8,128)(2,1)S(1)} %get-tuple-element.81.hid, ...), custom_call_target="tpu_custom_call" | custom-call | flops 704643072 | bytes 7696384 | tf_op jit(solution)/shard_map/backward/pallas_call | solution.py:43
  83.3 0.0 collective-permute-done.5.got
  83.3 2.0 %backward.7 = bf16[384,1536]{1,0:T(8,128)(2,1)S(1)} custom-call(f32[528,128]{1,0:T(8,128)S(1)} %get-tuple-element.74.own, f32[528,128]{1,0:T(8,128)S(1)} %collective-permute-done.5.got, f32[64,512]{1,0:T(8,128)S(1)} %get-tuple-element.75.target_t, bf16[512,1536]{1,0:T(8,128)(2,1)S(1)} %get-tuple-element.76.hid, ...), custom_call_target="tpu_custom_call" | custom-call | flops 704643072 | bytes 10055680 | tf_op jit(solution)/shard_map/backward/pallas_call | solution.py:43
  85.3 20.4 %all_to_all.22.blocks = bf16[16,24,1536]{2,1,0:T(8,128)(2,1)S(1)} all-to-all(bf16[16,24,1536]{2,1,0:T(8,128)(2,1)S(1)} %bitcast.26), channel_id=1, replica_groups=mesh['replica'=16,'fsdp'=16] {'fsdp'}, dimensions={0} | all-to-all | bytes 2359296 | tf_op jit(solution)/shard_map/all_to_all | solution.py:60
  105.6 0.4 update_last.1
  106.0 1.3 collective-permute-start.7
  107.3 3.0 %collective-permute-start.11 = (bf16[24,1536]{1,0:T(8,128)(2,1)S(1)}, bf16[24,1536]{1,0:T(8,128)(2,1)S(1)}, u32[]{:S(2)}, u32[]{:S(2)}) collective-permute-start(bf16[24,1536]{1,0:T(8,128)(2,1)S(1)} %get-tuple-element.87.mine), channel_id=1, source_target_pairs={{0,64},{16,80},{32,96},{48,112},{64,0},{80,16},{96,32},{112,48},{1... | collective-permute-start | bytes 221192 | tf_op jit(solution)/shard_map/ppermute | solution.py:340
  110.3 0.0 collective-permute-done.7.got
  110.4 2.5 %collective-permute-start.8 = (bf16[24,1536]{1,0:T(8,128)(2,1)S(1)}, bf16[24,1536]{1,0:T(8,128)(2,1)S(1)}, u32[]{:S(2)}, u32[]{:S(2)}) collective-permute-start(bf16[24,1536]{1,0:T(8,128)(2,1)S(1)} %pair_add.8.mine), channel_id=1, source_target_pairs={{0,32},{16,48},{32,0},{48,16},{64,96},{80,112},{96,64},{112,80},{1... | collective-permute-start | bytes 221192 | tf_op jit(solution)/shard_map/ppermute | solution.py:340
  112.9 1.3 collective-permute-done.11.got
  114.2 5.3 %collective-permute-start.12 = (bf16[24,1536]{1,0:T(8,128)(2,1)S(1)}, bf16[24,1536]{1,0:T(8,128)(2,1)S(1)}, u32[]{:S(2)}, u32[]{:S(2)}) collective-permute-start(bf16[24,1536]{1,0:T(8,128)(2,1)S(1)} %pair_add.12.mine), channel_id=1, source_target_pairs={{0,128},{16,144},{32,160},{48,176},{64,192},{80,208},{96,224},{112... | collective-permute-start | bytes 221192 | tf_op jit(solution)/shard_map/ppermute | solution.py:340
  119.5 0.0 collective-permute-done.8.got
  119.5 0.1 collective-permute-start.9
  119.6 1.8 %collective-permute-done.12.got = bf16[24,1536]{1,0:T(8,128)(2,1)S(1)} collective-permute-done((bf16[24,1536]{1,0:T(8,128)(2,1)S(1)}, bf16[24,1536]{1,0:T(8,128)(2,1)S(1)}, u32[]{:S(2)}, u32[]{:S(2)}) %collective-permute-start.12) | collective-permute-done | bytes 73760 | tf_op jit(solution)/shard_map/ppermute | solution.py:340
  121.4 0.3 collective-permute-start.13
  121.8 5.3 %collective-permute-done.9.got = bf16[24,1536]{1,0:T(8,128)(2,1)S(1)} collective-permute-done((bf16[24,1536]{1,0:T(8,128)(2,1)S(1)}, bf16[24,1536]{1,0:T(8,128)(2,1)S(1)}, u32[]{:S(2)}, u32[]{:S(2)}) %collective-permute-start.9) | collective-permute-done | bytes 73760 | tf_op jit(solution)/shard_map/ppermute | solution.py:340
  127.1 0.1 collective-permute-start.10
  127.2 0.0 collective-permute-done.13.got
  127.2 4.4 %collective-permute-start.14 = (bf16[24,1536]{1,0:T(8,128)(2,1)S(1)}, bf16[24,1536]{1,0:T(8,128)(2,1)S(1)}, u32[]{:S(2)}, u32[]{:S(2)}) collective-permute-start(bf16[24,1536]{1,0:T(8,128)(2,1)S(1)} %pair_add.14.mine), channel_id=1, source_target_pairs={{0,32},{16,48},{32,0},{48,16},{64,96},{80,112},{96,64},{112,80},{1... | collective-permute-start | bytes 221192 | tf_op jit(solution)/shard_map/ppermute | solution.py:340
  131.6 2.7 %collective-permute-done.10.got = bf16[24,1536]{1,0:T(8,128)(2,1)S(1)} collective-permute-done((bf16[24,1536]{1,0:T(8,128)(2,1)S(1)}, bf16[24,1536]{1,0:T(8,128)(2,1)S(1)}, u32[]{:S(2)}, u32[]{:S(2)}) %collective-permute-start.10) | collective-permute-done | bytes 73760 | tf_op jit(solution)/shard_map/ppermute | solution.py:340
  134.3 0.0 collective-permute-done.14.got
  134.4 1.1 outer.1
  (25 shorter events, 0.2 us)
Async XLA Ops:
  0.6 10.8 %copy-start = (f32[15,2,3072]{2,1,0:T(2,128)S(1)}, f32[15,2,3072]{2,1,0:T(2,128)}, u32[]{:S(2)}) copy-start(f32[15,2,3072]{2,1,0:T(2,128)} %param.17) | copy-start | bytes 1105924
  0.6 9.4 %copy-start.12 = (s32[2,512]{1,0:T(2,128)S(1)}, s32[2,512]{1,0:T(2,128)}, u32[]{:S(2)}) copy-start(s32[2,512]{1,0:T(2,128)} %levels.1) | copy-start | bytes 12292
  0.7 9.6 %copy-start.5 = (bf16[2,512,64]{1,2,0:T(8,128)(2,1)S(1)}, bf16[2,512,64]{1,2,0:T(8,128)(2,1)}, u32[]{:S(2)}) copy-start(bf16[2,512,64]{1,2,0:T(8,128)(2,1)} %param.13) | copy-start | bytes 393220
  0.7 10.0 %copy-start.6 = (bf16[2,512,64]{1,2,0:T(8,128)(2,1)S(1)}, bf16[2,512,64]{1,2,0:T(8,128)(2,1)}, u32[]{:S(2)}) copy-start(bf16[2,512,64]{1,2,0:T(8,128)(2,1)} %param.14) | copy-start | bytes 393220
  2.7 24.6 %all-to-all-start = ((bf16[16,24,1536]{2,1,0:T(8,128)(2,1)}), bf16[16,24,1536]{2,1,0:T(8,128)(2,1)S(1)}, u32[]{:S(2)}, u32[]{:S(2)}) async-start(bf16[16,24,1536]{2,1,0:T(8,128)(2,1)} %bitcast), calls=%async_computation | async-start | bytes 2359296 | tf_op jit(solution)/shard_map/all_to_all | solution.py:60
  10.1 1.4 %collective-permute-start.2 = (s32[2,512]{1,0:T(2,128)S(1)}, s32[2,512]{1,0:T(2,128)S(1)}, u32[]{:S(2)}, u32[]{:S(2)}) collective-permute-start(s32[2,512]{1,0:T(2,128)S(1)} %copy-done.12), channel_id=1, source_target_pairs={{0,1},{1,0},{2,3},{3,2},{4,5},{5,4},{6,7},{7,6},{8,9},{9,8},{10,11... | collective-permute-start | bytes 12296 | tf_op jit(solution)/shard_map/ppermute | solution.py:56
  10.3 1.8 %collective-permute-start = (bf16[2,64,512]{2,1,0:T(8,128)(2,1)S(1)}, bf16[2,64,512]{2,1,0:T(8,128)(2,1)S(1)}, u32[]{:S(2)}, u32[]{:S(2)}) collective-permute-start(bf16[2,64,512]{2,1,0:T(8,128)(2,1)S(1)} %bitcast.30), channel_id=1, source_target_pairs={{0,1},{1,0},{2,3},{3,2},{4,5},{5,4},{6,7},{7,6},{8,9},{9,8},{10,11... | collective-permute-start | bytes 393224 | tf_op jit(solution)/shard_map/ppermute | solution.py:56
  10.7 2.1 %collective-permute-start.1 = (bf16[2,64,512]{2,1,0:T(8,128)(2,1)S(1)}, bf16[2,64,512]{2,1,0:T(8,128)(2,1)S(1)}, u32[]{:S(2)}, u32[]{:S(2)}) collective-permute-start(bf16[2,64,512]{2,1,0:T(8,128)(2,1)S(1)} %bitcast.32), channel_id=1, source_target_pairs={{0,1},{1,0},{2,3},{3,2},{4,5},{5,4},{6,7},{7,6},{8,9},{9,8},{10,11... | collective-permute-start | bytes 393224 | tf_op jit(solution)/shard_map/ppermute | solution.py:56
  11.5 0.6 copy-start.14
  12.1 0.7 copy-start.8
  12.7 0.7 copy-start.10
  13.4 0.9 copy-start.7
  14.3 0.9 copy-start.9
  15.2 0.9 copy-start.11
  16.1 0.7 copy-start.13
  16.8 0.7 copy-start.15
  28.9 2.8 %collective-permute-start.4 = (f32[528,128]{1,0:T(8,128)S(1)}, f32[528,128]{1,0:T(8,128)S(1)}, u32[]{:S(2)}, u32[]{:S(2)}) collective-permute-start(f32[528,128]{1,0:T(8,128)S(1)} %get-tuple-element.69.own), channel_id=1, source_target_pairs={{0,1},{1,0},{2,3},{3,2},{4,5},{5,4},{6,7},{7,6},{8,9},{9,8},{10,11... | collective-permute-start | bytes 811016 | tf_op jit(solution)/shard_map/ppermute | solution.py:56
  31.5 2.2 %collective-permute-start.3 = (f32[528,128]{1,0:T(8,128)S(1)}, f32[528,128]{1,0:T(8,128)S(1)}, u32[]{:S(2)}, u32[]{:S(2)}) collective-permute-start(f32[528,128]{1,0:T(8,128)S(1)} %get-tuple-element.64.own), channel_id=1, source_target_pairs={{0,1},{1,0},{2,3},{3,2},{4,5},{5,4},{6,7},{7,6},{8,9},{9,8},{10,11... | collective-permute-start | bytes 811016 | tf_op jit(solution)/shard_map/ppermute | solution.py:56
  35.7 20.5 %copy-start.1 = (f32[24,3072]{1,0:T(8,128)S(1)}, f32[24,3072]{1,0:T(8,128)}, u32[]{:S(2)}) copy-start(f32[24,3072]{1,0:T(8,128)} %params.5) | copy-start | bytes 884740
  35.7 20.5 %copy-start.2 = (f32[1,24,3072]{2,1,0:T(8,128)S(1)}, f32[1,24,3072]{2,1,0:T(8,128)}, u32[]{:S(2)}) copy-start(f32[1,24,3072]{2,1,0:T(8,128)} %param.11) | copy-start | bytes 884740
  35.7 20.5 %copy-start.3 = (f32[1,24,3072]{2,1,0:T(8,128)S(1)}, f32[1,24,3072]{2,1,0:T(8,128)}, u32[]{:S(2)}) copy-start(f32[1,24,3072]{2,1,0:T(8,128)} %param.12) | copy-start | bytes 884740
  78.9 2.5 %collective-permute-start.6 = (f32[528,128]{1,0:T(8,128)S(1)}, f32[528,128]{1,0:T(8,128)S(1)}, u32[]{:S(2)}, u32[]{:S(2)}) collective-permute-start(f32[528,128]{1,0:T(8,128)S(1)} %get-tuple-element.79.own), channel_id=1, source_target_pairs={{0,1},{1,0},{2,3},{3,2},{4,5},{5,4},{6,7},{7,6},{8,9},{9,8},{10,11... | collective-permute-start | bytes 811016 | tf_op jit(solution)/shard_map/ppermute | solution.py:56
  81.2 2.0 %collective-permute-start.5 = (f32[528,128]{1,0:T(8,128)S(1)}, f32[528,128]{1,0:T(8,128)S(1)}, u32[]{:S(2)}, u32[]{:S(2)}) collective-permute-start(f32[528,128]{1,0:T(8,128)S(1)} %get-tuple-element.74.own), channel_id=1, source_target_pairs={{0,1},{1,0},{2,3},{3,2},{4,5},{5,4},{6,7},{7,6},{8,9},{9,8},{10,11... | collective-permute-start | bytes 811016 | tf_op jit(solution)/shard_map/ppermute | solution.py:56
  105.6 28.7 %copy-start.4 = (f32[24,3072]{1,0:T(8,128)S(1)}, f32[24,3072]{1,0:T(8,128)}, u32[]{:S(2)}) copy-start(f32[24,3072]{1,0:T(8,128)} %momentum.1) | copy-start | bytes 884740
  106.0 4.3 %collective-permute-start.7 = (bf16[24,1536]{1,0:T(8,128)(2,1)S(1)}, bf16[24,1536]{1,0:T(8,128)(2,1)S(1)}, u32[]{:S(2)}, u32[]{:S(2)}) collective-permute-start(bf16[24,1536]{1,0:T(8,128)(2,1)S(1)} %get-tuple-element.86.mine), channel_id=1, source_target_pairs={{0,16},{16,0},{32,48},{48,32},{64,80},{80,64},{96,112},{112,96},{1... | collective-permute-start | bytes 221192 | tf_op jit(solution)/shard_map/ppermute | solution.py:340
  107.3 6.8 %collective-permute-start.11 = (bf16[24,1536]{1,0:T(8,128)(2,1)S(1)}, bf16[24,1536]{1,0:T(8,128)(2,1)S(1)}, u32[]{:S(2)}, u32[]{:S(2)}) collective-permute-start(bf16[24,1536]{1,0:T(8,128)(2,1)S(1)} %get-tuple-element.87.mine), channel_id=1, source_target_pairs={{0,64},{16,80},{32,96},{48,112},{64,0},{80,16},{96,32},{112,48},{1... | collective-permute-start | bytes 221192 | tf_op jit(solution)/shard_map/ppermute | solution.py:340
  110.4 9.2 %collective-permute-start.8 = (bf16[24,1536]{1,0:T(8,128)(2,1)S(1)}, bf16[24,1536]{1,0:T(8,128)(2,1)S(1)}, u32[]{:S(2)}, u32[]{:S(2)}) collective-permute-start(bf16[24,1536]{1,0:T(8,128)(2,1)S(1)} %pair_add.8.mine), channel_id=1, source_target_pairs={{0,32},{16,48},{32,0},{48,16},{64,96},{80,112},{96,64},{112,80},{1... | collective-permute-start | bytes 221192 | tf_op jit(solution)/shard_map/ppermute | solution.py:340
  114.2 7.2 %collective-permute-start.12 = (bf16[24,1536]{1,0:T(8,128)(2,1)S(1)}, bf16[24,1536]{1,0:T(8,128)(2,1)S(1)}, u32[]{:S(2)}, u32[]{:S(2)}) collective-permute-start(bf16[24,1536]{1,0:T(8,128)(2,1)S(1)} %pair_add.12.mine), channel_id=1, source_target_pairs={{0,128},{16,144},{32,160},{48,176},{64,192},{80,208},{96,224},{112... | collective-permute-start | bytes 221192 | tf_op jit(solution)/shard_map/ppermute | solution.py:340
  119.5 7.5 %collective-permute-start.9 = (bf16[24,1536]{1,0:T(8,128)(2,1)S(1)}, bf16[24,1536]{1,0:T(8,128)(2,1)S(1)}, u32[]{:S(2)}, u32[]{:S(2)}) collective-permute-start(bf16[24,1536]{1,0:T(8,128)(2,1)S(1)} %pair_add.9.mine), channel_id=1, source_target_pairs={{0,64},{16,80},{32,96},{48,112},{64,0},{80,16},{96,32},{112,48},{1... | collective-permute-start | bytes 221192 | tf_op jit(solution)/shard_map/ppermute | solution.py:340
  121.4 5.8 %collective-permute-start.13 = (bf16[24,1536]{1,0:T(8,128)(2,1)S(1)}, bf16[24,1536]{1,0:T(8,128)(2,1)S(1)}, u32[]{:S(2)}, u32[]{:S(2)}) collective-permute-start(bf16[24,1536]{1,0:T(8,128)(2,1)S(1)} %pair_add.13.mine), channel_id=1, source_target_pairs={{0,16},{16,0},{32,48},{48,32},{64,80},{80,64},{96,112},{112,96},{1... | collective-permute-start | bytes 221192 | tf_op jit(solution)/shard_map/ppermute | solution.py:340
  127.1 7.2 %collective-permute-start.10 = (bf16[24,1536]{1,0:T(8,128)(2,1)S(1)}, bf16[24,1536]{1,0:T(8,128)(2,1)S(1)}, u32[]{:S(2)}, u32[]{:S(2)}) collective-permute-start(bf16[24,1536]{1,0:T(8,128)(2,1)S(1)} %pair_add.10.mine), channel_id=1, source_target_pairs={{0,128},{16,144},{32,160},{48,176},{64,192},{80,208},{96,224},{112... | collective-permute-start | bytes 221192 | tf_op jit(solution)/shard_map/ppermute | solution.py:340
  127.2 7.1 %collective-permute-start.14 = (bf16[24,1536]{1,0:T(8,128)(2,1)S(1)}, bf16[24,1536]{1,0:T(8,128)(2,1)S(1)}, u32[]{:S(2)}, u32[]{:S(2)}) collective-permute-start(bf16[24,1536]{1,0:T(8,128)(2,1)S(1)} %pair_add.14.mine), channel_id=1, source_target_pairs={{0,32},{16,48},{32,0},{48,16},{64,96},{80,112},{96,64},{112,80},{1... | collective-permute-start | bytes 221192 | tf_op jit(solution)/shard_map/ppermute | solution.py:340

commit v8 on v7

--- a/solution.py
+++ b/solution.py
@@ -24,6 +24,8 @@
 LANES = 128
 ROW_CHUNK = 16
 FWD_COLUMNS = 256
+BACK_COLUMNS = 512
+START_PARTS = 2
 KERNEL_VMEM = 24 * 2**20
 
 BF16 = jnp.bfloat16
@@ -77,12 +79,17 @@
 def spread_start(params, width):
     rows, columns = params.shape
     half = columns // CORES
+    part = half // START_PARTS
     shape = (width // CORES, CORES, rows, half)
     copies = pl.pallas_call(
         start_kernel,
-        grid=(CORES,),
-        in_specs=[pl.BlockSpec((rows, half), lambda core: (0, core))],
-        out_specs=pl.BlockSpec((shape[0], 1, rows, half), lambda core: (0, core, 0, 0)),
+        grid=(CORES, START_PARTS),
+        in_specs=[
+            pl.BlockSpec((rows, part), lambda core, place: (0, core * START_PARTS + place))
+        ],
+        out_specs=pl.BlockSpec(
+            (shape[0], 1, rows, part), lambda core, place: (0, core, 0, place)
+        ),
         out_shape=jax.ShapeDtypeStruct(shape, BF16),
         compiler_params=pltpu.CompilerParams(vmem_limit_bytes=KERNEL_VMEM),
         name="start",
@@ -174,13 +181,17 @@
         grad_sum = jnp.sum(out_grad.T, axis=1, keepdims=True) * root
 
         scaled = (weights[time_end:, :].astype(F32) * factor[0:1, :]).astype(BF16)
-        mod_buf[...] = jnp.dot(grad, scaled, preferred_element_type=F32)
-        for start in range(0, rows_here, ROW_CHUNK):
-            rows = pl.ds(start, ROW_CHUNK)
-            spread = jnp.concatenate([pull[rows, :]] * (columns // LANES), axis=1)
-            hid_grad = mod_buf[rows, :] - hid[rows, :].astype(F32) * spread
-            hid_buf[rows, :] = hid_grad.astype(BF16)
-            pre_buf[rows, :] = (hid_grad * slope[rows, :].astype(F32)).astype(BF16)
+        for left in range(0, columns, BACK_COLUMNS):
+            cols = pl.ds(left, BACK_COLUMNS)
+            mod_buf[:, cols] = jnp.dot(
+                grad, scaled[:, left : left + BACK_COLUMNS], preferred_element_type=F32
+            )
+            for start in range(0, rows_here, ROW_CHUNK):
+                rows = pl.ds(start, ROW_CHUNK)
+                spread = jnp.concatenate([pull[rows, :]] * (BACK_COLUMNS // LANES), axis=1)
+                hid_grad = mod_buf[rows, cols] - hid[rows, cols].astype(F32) * spread
+                hid_buf[rows, cols] = hid_grad.astype(BF16)
+                pre_buf[rows, cols] = (hid_grad * slope[rows, cols].astype(F32)).astype(BF16)
 
         def put(rows, values):
             if added:

time: 137 us -> 138 us (level)
  no operation moved by 1% of the time
where the time goes in v8:
time: 138 us; the launch traced here: 137 us
  blocking collectives  61.4 us (44%)
  starting transfers between devices  27.2 us (20%)
  Pallas kernels  23.8 us (17%)
  waiting for transfers between devices  16.7 us (12%)
  local copies, waits for them, and re-layouts  6.04 us (4%)
  between operations  1.58 us (1%)
    all_to_all x3, blocking collectives, exchange(): return lax.all_to_all(blocks, axis, 0, 0)  61.4 us
    pallas_call x20, Pallas kernels, local_call(): pl.pallas_call(kernel, in_specs=specs, out_specs=[VMEM] * len(outs), out_...  20.4 us
    ppermute x8, starting transfers between devices, replica_sum(): lax.ppermute(part, 'replica', [(i, i ^ bit) for i in range(replicas)])  17.1 us
    ppermute x8, waiting for transfers between devices, replica_sum(): lax.ppermute(part, 'replica', [(i, i ^ bit) for i in range(replicas)])  11 us
    all_to_all x1, starting transfers between devices, exchange(): return lax.all_to_all(blocks, axis, 0, 0)  7.34 us
    unnamed x32, local copies, waits for them, and re-layouts  6.03 us
    all_to_all x1, waiting for transfers between devices, exchange(): return lax.all_to_all(blocks, axis, 0, 0)  5.63 us
    pallas_call x1, Pallas kernels, spread_start(): pl.pallas_call(start_kernel, grid=(CORES, START_PARTS), in_specs=[pl.Bloc...  3.38 us
  transfers between devices with their start and end apart: 16, of which 5 were waited for; matrix products, arithmetic and copies ran while one was open for 0% of the time, Pallas kernels for 8%

profile of v8, /device:TPU:1, one launch (start us, length us, event | category | flops | bytes accessed | tf_op | source)
XLA Modules:
  0.0 136.8 jit_solution(7432092435536769955)
XLA Ops:
  0.6 0.0 copy-start
  0.6 0.0 copy-start.12
  0.7 0.0 copy-start.5
  0.7 0.0 copy-start.6
  0.7 3.4 %start.2 = bf16[8,2,24,1536]{3,2,1,0:T(8,128)(2,1)} custom-call(f32[24,3072]{1,0:T(8,128)} %params.5), custom_call_target="tpu_custom_call" | custom-call | tf_op jit(solution)/shard_map/start/pallas_call | solution.py:84
  4.1 7.3 %all-to-all-start = ((bf16[16,24,1536]{2,1,0:T(8,128)(2,1)}), bf16[16,24,1536]{2,1,0:T(8,128)(2,1)S(1)}, u32[]{:S(2)}, u32[]{:S(2)}) async-start(bf16[16,24,1536]{2,1,0:T(8,128)(2,1)} %bitcast), calls=%async_computation | async-start | bytes 2359296 | tf_op jit(solution)/shard_map/all_to_all | solution.py:62
  11.4 0.2 collective-permute-start.2
  11.6 0.4 collective-permute-start
  12.0 0.1 collective-permute-start.1
  12.8 0.0 collective-permute-done.2.levels_got
  12.8 0.0 copy-start.14
  12.8 0.6 copy-done.14
  13.4 0.0 collective-permute-done.latents_got
  13.4 0.7 copy-done.8
  14.1 0.0 collective-permute-done.1.noise_got
  14.1 0.7 copy-done.10
  14.7 0.9 copy-done.7
  15.6 0.9 copy-done.9
  16.5 0.9 copy-done.11
  17.5 0.7 copy-done.13
  18.1 0.7 copy-done.15
  18.8 4.2 %prepare.1 = (bf16[320,512]{1,0:T(8,128)(2,1)S(1)}, f32[64,512]{1,0:T(8,128)S(1)}, bf16[320,512]{1,0:T(8,128)(2,1)S(1)}, f32[64,512]{1,0:T(8,128)S(1)}, bf16[320...) custom-call(s32[1]{0:T(128)} %bitcast.1.core, ...), custom_call_target="tpu_custom_call" | custom-call | flops 4294967296 | bytes 3715072 | tf_op jit(solution)/shard_map/prepare/pallas_call | solution.py:45
  23.1 5.6 %all-to-all-done = bf16[16,24,1536]{2,1,0:T(8,128)(2,1)S(1)} async-done(((bf16[16,24,1536]{2,1,0:T(8,128)(2,1)}), bf16[16,24,1536]{2,1,0:T(8,128)(2,1)S(1)}, u32[]{:S(2)}, u32[]{:S(2)}) %all-to-all-start) | async-done | bytes 1179680 | tf_op jit(solution)/shard_map/all_to_all | solution.py:62
  28.7 1.6 %forward.5 = (bf16[512,1536]{1,0:T(8,128)(2,1)S(1)}, bf16[512,1536]{1,0:T(8,128)(2,1)S(1)}, f32[528,128]{1,0:T(8,128)S(1)}) custom-call(bf16[320,512]{1,0:T(8,128)(2,1)S(1)} %get-tuple-element.68.inputs_t, bf16[384,1536]{1,0:T(8,128)(2,1)S(1)} %bitcast.18, f32[1,1536]{1,0:T(1,128)S(1)} %get-tuple-element.62.factor, f32[1,1536]{1,0:T(1,128)S(1)} %get-tuple-element.63.shift), custom_call_target="tpu_custom_call" | custom-call | flops 603979776 | bytes 8081408 | tf_op jit(solution)/shard_map/forward/pallas_call | solution.py:45
  30.3 1.0 collective-permute-start.4
  31.2 1.6 %forward.4 = (bf16[512,1536]{1,0:T(8,128)(2,1)S(1)}, bf16[512,1536]{1,0:T(8,128)(2,1)S(1)}, f32[528,128]{1,0:T(8,128)S(1)}) custom-call(bf16[320,512]{1,0:T(8,128)(2,1)S(1)} %get-tuple-element.60.inputs_t, bf16[384,1536]{1,0:T(8,128)(2,1)S(1)} %bitcast.19, f32[1,1536]{1,0:T(1,128)S(1)} %get-tuple-element.62.factor, f32[1,1536]{1,0:T(1,128)S(1)} %get-tuple-element.63.shift), custom_call_target="tpu_custom_call" | custom-call | flops 603979776 | bytes 8081408 | tf_op jit(solution)/shard_map/forward/pallas_call | solution.py:45
  32.8 0.3 collective-permute-start.3
  33.1 0.0 collective-permute-done.4.got
  33.1 1.9 %backward.4.rest_0_ = f32[384,1536]{1,0:T(8,128)S(1)} custom-call(f32[528,128]{1,0:T(8,128)S(1)} %get-tuple-element.69.own, f32[528,128]{1,0:T(8,128)S(1)} %collective-permute-done.4.got, f32[64,512]{1,0:T(8,128)S(1)} %get-tuple-element.70.target_t, bf16[512,1536]{1,0:T(8,128)(2,1)S(1)} %get-tuple-element.71.hid, ...), custom_call_target="tpu_custom_call" | custom-call | flops 704643072 | bytes 7696384 | tf_op jit(solution)/shard_map/backward/pallas_call | solution.py:45
  35.1 0.0 collective-permute-done.3.got
  35.1 2.0 %backward.5 = bf16[384,1536]{1,0:T(8,128)(2,1)S(1)} custom-call(f32[528,128]{1,0:T(8,128)S(1)} %get-tuple-element.64.own, f32[528,128]{1,0:T(8,128)S(1)} %collective-permute-done.3.got, f32[64,512]{1,0:T(8,128)S(1)} %get-tuple-element.65.target_t, bf16[512,1536]{1,0:T(8,128)(2,1)S(1)} %get-tuple-element.66.hid, ...), custom_call_target="tpu_custom_call" | custom-call | flops 704643072 | bytes 10055680 | tf_op jit(solution)/shard_map/backward/pallas_call | solution.py:45
  37.1 0.0 copy-start.1
  37.1 0.0 copy-start.2
  37.1 0.0 copy-start.3
  37.1 20.5 %all_to_all.20.blocks = bf16[16,24,1536]{2,1,0:T(8,128)(2,1)S(1)} all-to-all(bf16[16,24,1536]{2,1,0:T(8,128)(2,1)S(1)} %bitcast.27), channel_id=1, replica_groups=mesh['replica'=16,'fsdp'=16] {'fsdp'}, dimensions={0} | all-to-all | bytes 2359296 | tf_op jit(solution)/shard_map/all_to_all | solution.py:62
  57.6 0.5 update.1
  58.1 20.6 %all_to_all.21 = bf16[16,24,1536]{2,1,0:T(8,128)(2,1)S(1)} all-to-all(bf16[16,24,1536]{2,1,0:T(8,128)(2,1)S(1)} %get-tuple-element.73), channel_id=1, replica_groups=mesh['replica'=16,'fsdp'=16] {'fsdp'}, dimensions={0} | all-to-all | bytes 2359296 | tf_op jit(solution)/shard_map/all_to_all | solution.py:62
  78.6 1.6 %forward.7 = (bf16[512,1536]{1,0:T(8,128)(2,1)S(1)}, bf16[512,1536]{1,0:T(8,128)(2,1)S(1)}, f32[528,128]{1,0:T(8,128)S(1)}) custom-call(bf16[320,512]{1,0:T(8,128)(2,1)S(1)} %get-tuple-element.78.inputs_t, bf16[384,1536]{1,0:T(8,128)(2,1)S(1)} %bitcast.22, f32[1,1536]{1,0:T(1,128)S(1)} %get-tuple-element.62.factor, f32[1,1536]{1,0:T(1,128)S(1)} %get-tuple-element.63.shift), custom_call_target="tpu_custom_call" | custom-call | flops 603979776 | bytes 8081408 | tf_op jit(solution)/shard_map/forward/pallas_call | solution.py:45
  80.2 0.8 collective-permute-start.6
  81.0 1.6 %forward.6 = (bf16[512,1536]{1,0:T(8,128)(2,1)S(1)}, bf16[512,1536]{1,0:T(8,128)(2,1)S(1)}, f32[528,128]{1,0:T(8,128)S(1)}) custom-call(bf16[320,512]{1,0:T(8,128)(2,1)S(1)} %get-tuple-element.59.inputs_t, bf16[384,1536]{1,0:T(8,128)(2,1)S(1)} %bitcast.23, f32[1,1536]{1,0:T(1,128)S(1)} %get-tuple-element.62.factor, f32[1,1536]{1,0:T(1,128)S(1)} %get-tuple-element.63.shift), custom_call_target="tpu_custom_call" | custom-call | flops 603979776 | bytes 8081408 | tf_op jit(solution)/shard_map/forward/pallas_call | solution.py:45
  82.6 0.1 collective-permute-start.5
  82.7 0.0 collective-permute-done.6.got
  82.7 1.9 %backward.6.rest_0_ = f32[384,1536]{1,0:T(8,128)S(1)} custom-call(f32[528,128]{1,0:T(8,128)S(1)} %get-tuple-element.79.own, f32[528,128]{1,0:T(8,128)S(1)} %collective-permute-done.6.got, f32[64,512]{1,0:T(8,128)S(1)} %get-tuple-element.80.target_t, bf16[512,1536]{1,0:T(8,128)(2,1)S(1)} %get-tuple-element.81.hid, ...), custom_call_target="tpu_custom_call" | custom-call | flops 704643072 | bytes 7696384 | tf_op jit(solution)/shard_map/backward/pallas_call | solution.py:45
  84.6 0.0 collective-permute-done.5.got
  84.6 2.0 %backward.7 = bf16[384,1536]{1,0:T(8,128)(2,1)S(1)} custom-call(f32[528,128]{1,0:T(8,128)S(1)} %get-tuple-element.74.own, f32[528,128]{1,0:T(8,128)S(1)} %collective-permute-done.5.got, f32[64,512]{1,0:T(8,128)S(1)} %get-tuple-element.75.target_t, bf16[512,1536]{1,0:T(8,128)(2,1)S(1)} %get-tuple-element.76.hid, ...), custom_call_target="tpu_custom_call" | custom-call | flops 704643072 | bytes 10055680 | tf_op jit(solution)/shard_map/backward/pallas_call | solution.py:45
  86.6 20.4 %all_to_all.22.blocks = bf16[16,24,1536]{2,1,0:T(8,128)(2,1)S(1)} all-to-all(bf16[16,24,1536]{2,1,0:T(8,128)(2,1)S(1)} %bitcast.26), channel_id=1, replica_groups=mesh['replica'=16,'fsdp'=16] {'fsdp'}, dimensions={0} | all-to-all | bytes 2359296 | tf_op jit(solution)/shard_map/all_to_all | solution.py:62
  107.0 0.4 update_last.1
  107.4 1.3 collective-permute-start.7
  108.7 3.0 %collective-permute-start.11 = (bf16[24,1536]{1,0:T(8,128)(2,1)S(1)}, bf16[24,1536]{1,0:T(8,128)(2,1)S(1)}, u32[]{:S(2)}, u32[]{:S(2)}) collective-permute-start(bf16[24,1536]{1,0:T(8,128)(2,1)S(1)} %get-tuple-element.87.mine), channel_id=1, source_target_pairs={{0,64},{16,80},{32,96},{48,112},{64,0},{80,16},{96,32},{112,48},{1... | collective-permute-start | bytes 221192 | tf_op jit(solution)/shard_map/ppermute | solution.py:351
  111.7 0.0 collective-permute-done.7.got
  111.7 2.5 %collective-permute-start.8 = (bf16[24,1536]{1,0:T(8,128)(2,1)S(1)}, bf16[24,1536]{1,0:T(8,128)(2,1)S(1)}, u32[]{:S(2)}, u32[]{:S(2)}) collective-permute-start(bf16[24,1536]{1,0:T(8,128)(2,1)S(1)} %pair_add.8.mine), channel_id=1, source_target_pairs={{0,32},{16,48},{32,0},{48,16},{64,96},{80,112},{96,64},{112,80},{1... | collective-permute-start | bytes 221192 | tf_op jit(solution)/shard_map/ppermute | solution.py:351
  114.2 1.3 collective-permute-done.11.got
  115.5 5.3 %collective-permute-start.12 = (bf16[24,1536]{1,0:T(8,128)(2,1)S(1)}, bf16[24,1536]{1,0:T(8,128)(2,1)S(1)}, u32[]{:S(2)}, u32[]{:S(2)}) collective-permute-start(bf16[24,1536]{1,0:T(8,128)(2,1)S(1)} %pair_add.12.mine), channel_id=1, source_target_pairs={{0,128},{16,144},{32,160},{48,176},{64,192},{80,208},{96,224},{112... | collective-permute-start | bytes 221192 | tf_op jit(solution)/shard_map/ppermute | solution.py:351
  120.8 0.0 collective-permute-done.8.got
  120.9 0.1 collective-permute-start.9
  121.0 1.8 %collective-permute-done.12.got = bf16[24,1536]{1,0:T(8,128)(2,1)S(1)} collective-permute-done((bf16[24,1536]{1,0:T(8,128)(2,1)S(1)}, bf16[24,1536]{1,0:T(8,128)(2,1)S(1)}, u32[]{:S(2)}, u32[]{:S(2)}) %collective-permute-start.12) | collective-permute-done | bytes 73760 | tf_op jit(solution)/shard_map/ppermute | solution.py:351
  122.8 0.3 collective-permute-start.13
  123.1 5.3 %collective-permute-done.9.got = bf16[24,1536]{1,0:T(8,128)(2,1)S(1)} collective-permute-done((bf16[24,1536]{1,0:T(8,128)(2,1)S(1)}, bf16[24,1536]{1,0:T(8,128)(2,1)S(1)}, u32[]{:S(2)}, u32[]{:S(2)}) %collective-permute-start.9) | collective-permute-done | bytes 73760 | tf_op jit(solution)/shard_map/ppermute | solution.py:351
  128.4 0.1 collective-permute-start.10
  128.5 0.0 collective-permute-done.13.got
  128.6 4.4 %collective-permute-start.14 = (bf16[24,1536]{1,0:T(8,128)(2,1)S(1)}, bf16[24,1536]{1,0:T(8,128)(2,1)S(1)}, u32[]{:S(2)}, u32[]{:S(2)}) collective-permute-start(bf16[24,1536]{1,0:T(8,128)(2,1)S(1)} %pair_add.14.mine), channel_id=1, source_target_pairs={{0,32},{16,48},{32,0},{48,16},{64,96},{80,112},{96,64},{112,80},{1... | collective-permute-start | bytes 221192 | tf_op jit(solution)/shard_map/ppermute | solution.py:351
  133.0 2.7 %collective-permute-done.10.got = bf16[24,1536]{1,0:T(8,128)(2,1)S(1)} collective-permute-done((bf16[24,1536]{1,0:T(8,128)(2,1)S(1)}, bf16[24,1536]{1,0:T(8,128)(2,1)S(1)}, u32[]{:S(2)}, u32[]{:S(2)}) %collective-permute-start.10) | collective-permute-done | bytes 73760 | tf_op jit(solution)/shard_map/ppermute | solution.py:351
  135.6 0.0 collective-permute-done.14.got
  135.7 1.1 outer.1
  (25 shorter events, 0.2 us)
Async XLA Ops:
  0.6 12.1 %copy-start = (f32[15,2,3072]{2,1,0:T(2,128)S(1)}, f32[15,2,3072]{2,1,0:T(2,128)}, u32[]{:S(2)}) copy-start(f32[15,2,3072]{2,1,0:T(2,128)} %param.17) | copy-start | bytes 1105924
  0.6 10.8 %copy-start.12 = (s32[2,512]{1,0:T(2,128)S(1)}, s32[2,512]{1,0:T(2,128)}, u32[]{:S(2)}) copy-start(s32[2,512]{1,0:T(2,128)} %levels.1) | copy-start | bytes 12292
  0.7 10.9 %copy-start.5 = (bf16[2,512,64]{1,2,0:T(8,128)(2,1)S(1)}, bf16[2,512,64]{1,2,0:T(8,128)(2,1)}, u32[]{:S(2)}) copy-start(bf16[2,512,64]{1,2,0:T(8,128)(2,1)} %param.13) | copy-start | bytes 393220
  0.7 11.3 %copy-start.6 = (bf16[2,512,64]{1,2,0:T(8,128)(2,1)S(1)}, bf16[2,512,64]{1,2,0:T(8,128)(2,1)}, u32[]{:S(2)}) copy-start(bf16[2,512,64]{1,2,0:T(8,128)(2,1)} %param.14) | copy-start | bytes 393220
  4.1 24.6 %all-to-all-start = ((bf16[16,24,1536]{2,1,0:T(8,128)(2,1)}), bf16[16,24,1536]{2,1,0:T(8,128)(2,1)S(1)}, u32[]{:S(2)}, u32[]{:S(2)}) async-start(bf16[16,24,1536]{2,1,0:T(8,128)(2,1)} %bitcast), calls=%async_computation | async-start | bytes 2359296 | tf_op jit(solution)/shard_map/all_to_all | solution.py:62
  11.4 1.4 %collective-permute-start.2 = (s32[2,512]{1,0:T(2,128)S(1)}, s32[2,512]{1,0:T(2,128)S(1)}, u32[]{:S(2)}, u32[]{:S(2)}) collective-permute-start(s32[2,512]{1,0:T(2,128)S(1)} %copy-done.12), channel_id=1, source_target_pairs={{0,1},{1,0},{2,3},{3,2},{4,5},{5,4},{6,7},{7,6},{8,9},{9,8},{10,11... | collective-permute-start | bytes 12296 | tf_op jit(solution)/shard_map/ppermute | solution.py:58
  11.6 1.8 %collective-permute-start = (bf16[2,64,512]{2,1,0:T(8,128)(2,1)S(1)}, bf16[2,64,512]{2,1,0:T(8,128)(2,1)S(1)}, u32[]{:S(2)}, u32[]{:S(2)}) collective-permute-start(bf16[2,64,512]{2,1,0:T(8,128)(2,1)S(1)} %bitcast.30), channel_id=1, source_target_pairs={{0,1},{1,0},{2,3},{3,2},{4,5},{5,4},{6,7},{7,6},{8,9},{9,8},{10,11... | collective-permute-start | bytes 393224 | tf_op jit(solution)/shard_map/ppermute | solution.py:58
  12.0 2.1 %collective-permute-start.1 = (bf16[2,64,512]{2,1,0:T(8,128)(2,1)S(1)}, bf16[2,64,512]{2,1,0:T(8,128)(2,1)S(1)}, u32[]{:S(2)}, u32[]{:S(2)}) collective-permute-start(bf16[2,64,512]{2,1,0:T(8,128)(2,1)S(1)} %bitcast.32), channel_id=1, source_target_pairs={{0,1},{1,0},{2,3},{3,2},{4,5},{5,4},{6,7},{7,6},{8,9},{9,8},{10,11... | collective-permute-start | bytes 393224 | tf_op jit(solution)/shard_map/ppermute | solution.py:58
  12.8 0.6 copy-start.14
  13.4 0.7 copy-start.8
  14.1 0.7 copy-start.10
  14.7 0.9 copy-start.7
  15.6 0.9 copy-start.9
  16.5 0.9 copy-start.11
  17.4 0.7 copy-start.13
  18.1 0.7 copy-start.15
  30.3 2.8 %collective-permute-start.4 = (f32[528,128]{1,0:T(8,128)S(1)}, f32[528,128]{1,0:T(8,128)S(1)}, u32[]{:S(2)}, u32[]{:S(2)}) collective-permute-start(f32[528,128]{1,0:T(8,128)S(1)} %get-tuple-element.69.own), channel_id=1, source_target_pairs={{0,1},{1,0},{2,3},{3,2},{4,5},{5,4},{6,7},{7,6},{8,9},{9,8},{10,11... | collective-permute-start | bytes 811016 | tf_op jit(solution)/shard_map/ppermute | solution.py:58
  32.8 2.2 %collective-permute-start.3 = (f32[528,128]{1,0:T(8,128)S(1)}, f32[528,128]{1,0:T(8,128)S(1)}, u32[]{:S(2)}, u32[]{:S(2)}) collective-permute-start(f32[528,128]{1,0:T(8,128)S(1)} %get-tuple-element.64.own), channel_id=1, source_target_pairs={{0,1},{1,0},{2,3},{3,2},{4,5},{5,4},{6,7},{7,6},{8,9},{9,8},{10,11... | collective-permute-start | bytes 811016 | tf_op jit(solution)/shard_map/ppermute | solution.py:58
  37.1 20.5 %copy-start.1 = (f32[24,3072]{1,0:T(8,128)S(1)}, f32[24,3072]{1,0:T(8,128)}, u32[]{:S(2)}) copy-start(f32[24,3072]{1,0:T(8,128)} %params.5) | copy-start | bytes 884740
  37.1 20.5 %copy-start.2 = (f32[1,24,3072]{2,1,0:T(8,128)S(1)}, f32[1,24,3072]{2,1,0:T(8,128)}, u32[]{:S(2)}) copy-start(f32[1,24,3072]{2,1,0:T(8,128)} %param.11) | copy-start | bytes 884740
  37.1 20.5 %copy-start.3 = (f32[1,24,3072]{2,1,0:T(8,128)S(1)}, f32[1,24,3072]{2,1,0:T(8,128)}, u32[]{:S(2)}) copy-start(f32[1,24,3072]{2,1,0:T(8,128)} %param.12) | copy-start | bytes 884740
  80.2 2.5 %collective-permute-start.6 = (f32[528,128]{1,0:T(8,128)S(1)}, f32[528,128]{1,0:T(8,128)S(1)}, u32[]{:S(2)}, u32[]{:S(2)}) collective-permute-start(f32[528,128]{1,0:T(8,128)S(1)} %get-tuple-element.79.own), channel_id=1, source_target_pairs={{0,1},{1,0},{2,3},{3,2},{4,5},{5,4},{6,7},{7,6},{8,9},{9,8},{10,11... | collective-permute-start | bytes 811016 | tf_op jit(solution)/shard_map/ppermute | solution.py:58
  82.6 2.0 %collective-permute-start.5 = (f32[528,128]{1,0:T(8,128)S(1)}, f32[528,128]{1,0:T(8,128)S(1)}, u32[]{:S(2)}, u32[]{:S(2)}) collective-permute-start(f32[528,128]{1,0:T(8,128)S(1)} %get-tuple-element.74.own), channel_id=1, source_target_pairs={{0,1},{1,0},{2,3},{3,2},{4,5},{5,4},{6,7},{7,6},{8,9},{9,8},{10,11... | collective-permute-start | bytes 811016 | tf_op jit(solution)/shard_map/ppermute | solution.py:58
  107.0 28.7 %copy-start.4 = (f32[24,3072]{1,0:T(8,128)S(1)}, f32[24,3072]{1,0:T(8,128)}, u32[]{:S(2)}) copy-start(f32[24,3072]{1,0:T(8,128)} %momentum.1) | copy-start | bytes 884740
  107.4 4.3 %collective-permute-start.7 = (bf16[24,1536]{1,0:T(8,128)(2,1)S(1)}, bf16[24,1536]{1,0:T(8,128)(2,1)S(1)}, u32[]{:S(2)}, u32[]{:S(2)}) collective-permute-start(bf16[24,1536]{1,0:T(8,128)(2,1)S(1)} %get-tuple-element.86.mine), channel_id=1, source_target_pairs={{0,16},{16,0},{32,48},{48,32},{64,80},{80,64},{96,112},{112,96},{1... | collective-permute-start | bytes 221192 | tf_op jit(solution)/shard_map/ppermute | solution.py:351
  108.7 6.9 %collective-permute-start.11 = (bf16[24,1536]{1,0:T(8,128)(2,1)S(1)}, bf16[24,1536]{1,0:T(8,128)(2,1)S(1)}, u32[]{:S(2)}, u32[]{:S(2)}) collective-permute-start(bf16[24,1536]{1,0:T(8,128)(2,1)S(1)} %get-tuple-element.87.mine), channel_id=1, source_target_pairs={{0,64},{16,80},{32,96},{48,112},{64,0},{80,16},{96,32},{112,48},{1... | collective-permute-start | bytes 221192 | tf_op jit(solution)/shard_map/ppermute | solution.py:351
  111.7 9.2 %collective-permute-start.8 = (bf16[24,1536]{1,0:T(8,128)(2,1)S(1)}, bf16[24,1536]{1,0:T(8,128)(2,1)S(1)}, u32[]{:S(2)}, u32[]{:S(2)}) collective-permute-start(bf16[24,1536]{1,0:T(8,128)(2,1)S(1)} %pair_add.8.mine), channel_id=1, source_target_pairs={{0,32},{16,48},{32,0},{48,16},{64,96},{80,112},{96,64},{112,80},{1... | collective-permute-start | bytes 221192 | tf_op jit(solution)/shard_map/ppermute | solution.py:351
  115.5 7.2 %collective-permute-start.12 = (bf16[24,1536]{1,0:T(8,128)(2,1)S(1)}, bf16[24,1536]{1,0:T(8,128)(2,1)S(1)}, u32[]{:S(2)}, u32[]{:S(2)}) collective-permute-start(bf16[24,1536]{1,0:T(8,128)(2,1)S(1)} %pair_add.12.mine), channel_id=1, source_target_pairs={{0,128},{16,144},{32,160},{48,176},{64,192},{80,208},{96,224},{112... | collective-permute-start | bytes 221192 | tf_op jit(solution)/shard_map/ppermute | solution.py:351
  120.9 7.5 %collective-permute-start.9 = (bf16[24,1536]{1,0:T(8,128)(2,1)S(1)}, bf16[24,1536]{1,0:T(8,128)(2,1)S(1)}, u32[]{:S(2)}, u32[]{:S(2)}) collective-permute-start(bf16[24,1536]{1,0:T(8,128)(2,1)S(1)} %pair_add.9.mine), channel_id=1, source_target_pairs={{0,64},{16,80},{32,96},{48,112},{64,0},{80,16},{96,32},{112,48},{1... | collective-permute-start | bytes 221192 | tf_op jit(solution)/shard_map/ppermute | solution.py:351
  122.8 5.8 %collective-permute-start.13 = (bf16[24,1536]{1,0:T(8,128)(2,1)S(1)}, bf16[24,1536]{1,0:T(8,128)(2,1)S(1)}, u32[]{:S(2)}, u32[]{:S(2)}) collective-permute-start(bf16[24,1536]{1,0:T(8,128)(2,1)S(1)} %pair_add.13.mine), channel_id=1, source_target_pairs={{0,16},{16,0},{32,48},{48,32},{64,80},{80,64},{96,112},{112,96},{1... | collective-permute-start | bytes 221192 | tf_op jit(solution)/shard_map/ppermute | solution.py:351
  128.4 7.2 %collective-permute-start.10 = (bf16[24,1536]{1,0:T(8,128)(2,1)S(1)}, bf16[24,1536]{1,0:T(8,128)(2,1)S(1)}, u32[]{:S(2)}, u32[]{:S(2)}) collective-permute-start(bf16[24,1536]{1,0:T(8,128)(2,1)S(1)} %pair_add.10.mine), channel_id=1, source_target_pairs={{0,128},{16,144},{32,160},{48,176},{64,192},{80,208},{96,224},{112... | collective-permute-start | bytes 221192 | tf_op jit(solution)/shard_map/ppermute | solution.py:351
  128.6 7.1 %collective-permute-start.14 = (bf16[24,1536]{1,0:T(8,128)(2,1)S(1)}, bf16[24,1536]{1,0:T(8,128)(2,1)S(1)}, u32[]{:S(2)}, u32[]{:S(2)}) collective-permute-start(bf16[24,1536]{1,0:T(8,128)(2,1)S(1)} %pair_add.14.mine), channel_id=1, source_target_pairs={{0,32},{16,48},{32,0},{48,16},{64,96},{80,112},{96,64},{112,80},{1... | collective-permute-start | bytes 221192 | tf_op jit(solution)/shard_map/ppermute | solution.py:351
